TPU v7x, 32 devices: a whole 2x2x4 slice. The times are simulated.
32 devices in a mesh: seq: 2 (over core), kax: 4 (over y, x), vax: 4 (over z).
Axes of the slice: x: 2, y: 2, z: 4, core: 2. Of those that a mesh axis runs over, the one named last changes fastest.
Arguments:
- tokens: bfloat16 [2048, 1024], P('seq'), may hold values from -6 to 6
- norm_gain: bfloat16 [1024], replicated, may hold values from 0.5 to 1.5
- query_weight: bfloat16 [1024, 4, 128], P(None, None, 'kax'), may hold values from -0.1875 to 0.1875
- key_weight: bfloat16 [1024, 4, 128], P(None, None, 'kax'), may hold values from -0.1875 to 0.1875
- value_weight: bfloat16 [1024, 4, 256], P(None, None, 'vax'), may hold values from -0.1875 to 0.1875
- gate_weight: bfloat16 [1024, 4, 256], P(None, None, 'vax'), may hold values from -0.1875 to 0.1875
- decay_down: bfloat16 [1024, 16], replicated, may hold values from -0.1875 to 0.1875
- decay_up: bfloat16 [16, 4, 128], P(None, None, 'kax'), may hold values from -1.5 to 1.5
- decay_bias: bfloat16 [4, 128], P(None, 'kax'), may hold values from 0 to 12
- group_gain: bfloat16 [256], P('vax'), may hold values from 0.5 to 1.5
- out_weight: bfloat16 [4, 256, 1024], P('kax', 'vax'), may hold values from -0.25 to 0.25
- ffn_gain: bfloat16 [1024], replicated, may hold values from 0.5 to 1.5
- ffn_gate: bfloat16 [1024, 2816], P(None, ('kax', 'vax')), may hold values from -0.1875 to 0.1875
- ffn_up: bfloat16 [1024, 2816], P(None, ('kax', 'vax')), may hold values from -0.1875 to 0.1875
- ffn_down: bfloat16 [2816, 1024], P(('kax', 'vax')), may hold values from -0.109375 to 0.109375
- cotangent: bfloat16 [2048, 1024], P('seq'), may hold values from -6 to 6
Outputs:
- output: bfloat16 [2048, 1024], P('seq', ('kax', 'vax'))
- input_grad: bfloat16 [2048, 1024], P('seq', ('kax', 'vax'))
- norm_gain_grad: float32 [1024], P(('kax', 'vax'))
- query_weight_grad: float32 [1024, 4, 128], P(None, 'vax', 'kax')
- key_weight_grad: float32 [1024, 4, 128], P(None, 'vax', 'kax')
- value_weight_grad: float32 [1024, 4, 256], P(None, 'kax', 'vax')
- gate_weight_grad: float32 [1024, 4, 256], P(None, 'kax', 'vax')
- decay_down_grad: float32 [1024, 16], P(None, ('kax', 'vax'))
- decay_up_grad: float32 [16, 4, 128], P(None, 'vax', 'kax')
- decay_bias_grad: float32 [4, 128], P('vax', 'kax')
- group_gain_grad: float32 [256], P('vax')
- out_weight_grad: float32 [4, 256, 1024], P('kax', 'vax')
- ffn_gain_grad: float32 [1024], P(('kax', 'vax'))
- ffn_gate_grad: float32 [1024, 2816], P(None, ('kax', 'vax'))
- ffn_up_grad: float32 [1024, 2816], P(None, ('kax', 'vax'))
- ffn_down_grad: float32 [2816, 1024], P(('kax', 'vax'))
All inputs are finite; a program needn't handle non-finite values.
Results may differ from a plain program's by a relative error of at most 0.03.
Values may be sent and summed in bfloat16 or wider, within the bound.
A program may use at most 128 MiB of HBM per device.

v0:
```python
import jax
import jax.numpy as jnp
from jax import lax
from jax.sharding import PartitionSpec as P

DKH = 128
DVH = 256
CH = 64


epsilon = 1e-06


def entering(value, axis, join, neutral):
    place = lax.axis_index(axis)
    gathered = jax.tree.map(
        lambda a, kind: lax.all_gather(a.astype(kind), axis), value, (jnp.bfloat16, jnp.bfloat16)
    )
    state = jax.tree.map(lambda a, e: jnp.zeros_like(a) + jnp.asarray(e, a.dtype), value, neutral)

    def entering_one(lap, state):
        return join(
            state,
            jax.tree.map(
                lambda a, own: lax.dynamic_index_in_dim(a, lap, 0, False).astype(own.dtype),
                gathered,
                value,
            ),
        )

    return lax.fori_loop(0, place, entering_one, state)


def shortened(value):

    def short(part):
        return part.astype(jnp.bfloat16) if part.dtype == jnp.float32 else part

    return jax.tree.map(short, value)


def prefix(value, axis, join, neutral):
    count = lax.axis_size(axis)
    place = lax.axis_index(axis)
    ahead = count - 1 - place
    gathered = jax.tree.map(
        lambda a, kind: lax.all_gather(a.astype(kind), axis),
        value,
        jax.tree.map(lambda a: jnp.bfloat16 if a.dtype == jnp.float32 else a.dtype, value),
    )
    state = jax.tree.map(lambda a, e: jnp.zeros_like(a) + jnp.asarray(e, a.dtype), value, neutral)

    def prefix_one(lap, state):
        source = count - 1 - lap
        return join(
            state,
            jax.tree.map(
                lambda a, own: lax.dynamic_index_in_dim(a, source, 0, False).astype(own.dtype),
                gathered,
                value,
            ),
        )

    return lax.fori_loop(0, ahead, prefix_one, state)


def product(left, right):
    return jnp.dot(left, right, preferred_element_type=jnp.float32)


def inner(left, right):
    return lax.dot_general(
        left, right, (((0,), (0,)), ((), ())), preferred_element_type=jnp.float32
    )


def highest(form, left, right):
    return jnp.einsum(form, left, right, precision=lax.Precision.HIGHEST)


def compose(earlier, later):
    return (earlier[0] * later[0], later[0][..., None] * earlier[1] + later[1])


def silu_grad(values):
    sigma = jax.nn.sigmoid(values)
    return sigma * (1.0 + values * (1.0 - sigma))


def shards(
    tokens,
    norm_gain,
    query_weight,
    key_weight,
    value_weight,
    gate_weight,
    decay_down,
    decay_up,
    decay_bias,
    group_gain,
    out_weight,
    ffn_gain,
    ffn_gate,
    ffn_up,
    ffn_down,
    cotangent,
):
    rows, width = tokens.shape
    heads = query_weight.shape[1]
    key_local = query_weight.shape[2]
    value_local = value_weight.shape[2]
    rank = decay_down.shape[1]
    spans = rows // CH
    kax_count = lax.axis_size("kax")
    vax_count = lax.axis_size("vax")
    group_count = kax_count * vax_count
    kax_index = lax.axis_index("kax")
    vax_index = lax.axis_index("vax")
    pair_index = lax.axis_index(("kax", "vax"))
    heads_kax = heads // kax_count
    heads_vax = heads // vax_count
    slab = width // group_count
    query_scale = DKH ** (-0.5)
    highest_mode = lax.Precision.HIGHEST
    token_float = tokens.astype(jnp.float32)
    gain_one = norm_gain.astype(jnp.float32)
    inv_one = lax.rsqrt(jnp.mean(token_float * token_float, axis=-1, keepdims=True) + epsilon)
    normed = (token_float * inv_one * gain_one).astype(jnp.bfloat16)
    query_all = (
        product(normed, query_weight.reshape(width, -1)).reshape(rows, heads, key_local)
        * query_scale
    )
    key_all = product(normed, key_weight.reshape(width, -1)).reshape(rows, heads, key_local)
    value_all = product(normed, value_weight.reshape(width, -1)).reshape(rows, heads, value_local)
    gate_local = lax.dynamic_slice_in_dim(gate_weight, kax_index * heads_kax, heads_kax, 1)
    gate_pre = product(normed, gate_local.reshape(width, -1)).reshape(rows, heads_kax, value_local)
    low_rank = product(normed, decay_down)
    up_float = decay_up.astype(jnp.float32)
    decay_arg = jnp.dot(low_rank, up_float.reshape(rank, -1), precision=highest_mode).reshape(
        rows, heads, key_local
    )
    decay_arg = decay_arg + decay_bias.astype(jnp.float32)
    decay_log = jax.nn.log_sigmoid(decay_arg) / 16.0
    query_blocks = query_all.reshape(spans, CH, heads, key_local)
    key_blocks = key_all.reshape(spans, CH, heads, key_local)
    value_blocks = value_all.reshape(spans, CH, heads, value_local)
    cum_decay = jnp.cumsum(decay_log.reshape(spans, CH, heads, key_local), axis=1)
    last_decay = cum_decay[:, -1]
    query_decayed = query_blocks * jnp.exp(cum_decay)
    key_decayed = key_blocks * jnp.exp(-cum_decay)
    key_to_end = key_blocks * jnp.exp(last_decay[:, None] - cum_decay)
    causal = (jnp.arange(CH)[:, None] >= jnp.arange(CH)[None, :]).astype(jnp.float32)
    scores = highest("cthk,cshk->chts", query_decayed, key_decayed) * causal
    span_decay = jnp.exp(last_decay)
    span_update = highest("cshk,cshv->chkv", key_to_end, value_blocks)
    run_decay, run_state = lax.associative_scan(compose, (span_decay, span_update), axis=0)
    identity = (jnp.ones_like(run_decay[-1]), jnp.zeros_like(run_state[-1]))
    state_in = entering((run_decay[-1], run_state[-1]), "seq", compose, identity)[1]
    state_end = run_decay[..., None] * state_in[None] + run_state
    state_start = jnp.concatenate([state_in[None], state_end[:-1]], axis=0)
    mixed_part = highest("chts,cshv->cthv", scores, value_blocks)
    mixed_part = mixed_part + highest("cthk,chkv->cthv", query_decayed, state_start)
    head_out = lax.psum_scatter(
        mixed_part.reshape(rows, heads, value_local), "kax", scatter_dimension=1, tiled=True
    )
    square_sum = lax.psum(jnp.sum(head_out * head_out, axis=-1), "vax")
    inv_two = lax.rsqrt(square_sum / DVH + epsilon)[..., None]
    normal_out = head_out * inv_two
    group_float = group_gain.astype(jnp.float32)
    gate_act = jax.nn.silu(gate_pre)
    gated = (normal_out * group_float * gate_act).astype(jnp.bfloat16)
    gated_flat = gated.reshape(rows, -1)
    out_flat = out_weight.reshape(-1, width)
    attn_slab = lax.psum_scatter(
        product(gated_flat, out_flat).astype(jnp.bfloat16),
        ("kax", "vax"),
        scatter_dimension=1,
        tiled=True,
    ).astype(jnp.float32)
    token_slab = lax.dynamic_slice_in_dim(token_float, pair_index * slab, slab, 1)
    resid_slab = token_slab + attn_slab
    resid = lax.all_gather(
        resid_slab.astype(jnp.bfloat16), ("kax", "vax"), axis=1, tiled=True
    ).astype(resid_slab.dtype)
    gain_two = ffn_gain.astype(jnp.float32)
    inv_three = lax.rsqrt(jnp.mean(resid * resid, axis=-1, keepdims=True) + epsilon)
    ffn_in = (resid * inv_three * gain_two).astype(jnp.bfloat16)
    gate_val = product(ffn_in, ffn_gate)
    up_val = product(ffn_in, ffn_up)
    gate_silu = jax.nn.silu(gate_val)
    hidden = (gate_silu * up_val).astype(jnp.bfloat16)
    ffn_slab = lax.psum_scatter(
        product(hidden, ffn_down).astype(jnp.bfloat16),
        ("kax", "vax"),
        scatter_dimension=1,
        tiled=True,
    ).astype(jnp.float32)
    output = (resid_slab + ffn_slab).astype(jnp.bfloat16)
    grad_down = inner(hidden, cotangent)
    grad_hidden = jnp.dot(cotangent, ffn_down.T, preferred_element_type=jnp.float32)
    grad_up = (grad_hidden * gate_silu).astype(jnp.bfloat16)
    grad_gate = (grad_hidden * up_val * silu_grad(gate_val)).astype(jnp.bfloat16)
    grad_ffn_gate = inner(ffn_in, grad_gate)
    grad_ffn_up = inner(ffn_in, grad_up)
    ffn_in_part = jnp.dot(grad_gate, ffn_gate.T, preferred_element_type=jnp.float32)
    ffn_in_part = ffn_in_part + jnp.dot(grad_up, ffn_up.T, preferred_element_type=jnp.float32)
    ffn_in_grad = lax.psum(ffn_in_part.astype(jnp.bfloat16), ("kax", "vax")).astype(jnp.float32)
    scaled_grad = ffn_in_grad * gain_two
    grad_resid = cotangent.astype(jnp.float32) + inv_three * scaled_grad
    grad_resid = grad_resid - resid * inv_three**3 * jnp.mean(
        resid * scaled_grad, axis=-1, keepdims=True
    )
    full_gain_grad = jnp.sum(ffn_in_grad * resid * inv_three, axis=0)
    grad_ffn_gain = lax.dynamic_slice_in_dim(full_gain_grad, pair_index * slab, slab, 0)
    grad_resid_slab = lax.dynamic_slice_in_dim(grad_resid, pair_index * slab, slab, 1)
    resid_low = grad_resid.astype(jnp.bfloat16)
    grad_gated_flat = jnp.dot(resid_low, out_flat.T, preferred_element_type=jnp.float32)
    grad_out_flat = inner(gated_flat, resid_low)
    grad_gated = grad_gated_flat.reshape(rows, heads_kax, value_local)
    grad_scaled = grad_gated * gate_act
    grad_group_part = jnp.sum(grad_scaled * normal_out, axis=(0, 1))
    grad_normal = grad_scaled * group_float
    grad_gate_low = (grad_gated * normal_out * group_float * silu_grad(gate_pre)).astype(
        jnp.bfloat16
    )
    dot_sum = lax.psum(jnp.sum(normal_out * grad_normal, axis=-1), "vax")
    grad_head = inv_two * (grad_normal - normal_out * dot_sum[..., None] / DVH)
    grad_mixed = lax.all_gather(shortened(grad_head), "kax", axis=1, tiled=True).astype(
        grad_head.dtype
    )
    grad_blocks = grad_mixed.reshape(spans, CH, heads, value_local)
    state_weight = highest("cthk,cthv->chkv", query_decayed, grad_blocks)
    back_decay, back_state = lax.associative_scan(
        compose, (span_decay[::-1], state_weight[::-1]), axis=0
    )
    back_decay = back_decay[::-1]
    back_state = back_state[::-1]
    state_after_end = prefix((back_decay[0], back_state[0]), "seq", compose, identity)[1]
    grad_state_start = back_decay[..., None] * state_after_end[None] + back_state
    grad_state_after = jnp.concatenate([grad_state_start[1:], state_after_end[None]], axis=0)
    grad_scores = highest("cthv,cshv->chts", grad_blocks, value_blocks) * causal
    grad_query_dec = highest("chts,cshk->cthk", grad_scores, key_decayed)
    grad_query_dec = grad_query_dec + highest("cthv,chkv->cthk", grad_blocks, state_start)
    grad_key_dec = highest("chts,cthk->cshk", grad_scores, query_decayed)
    grad_key_end = highest("cshv,chkv->cshk", value_blocks, grad_state_after)
    grad_value_part = highest("chts,cthv->cshv", scores, grad_blocks)
    grad_value_part = grad_value_part + highest("cshk,chkv->cshv", key_to_end, grad_state_after)
    grad_query_part = grad_query_dec * jnp.exp(cum_decay)
    grad_key_part = grad_key_dec * jnp.exp(-cum_decay) + grad_key_end * jnp.exp(
        last_decay[:, None] - cum_decay
    )
    extra_part = jnp.sum(grad_state_after * state_end, axis=-1)
    grad_query_h, grad_key_h, extra_h = (
        lax.psum_scatter(
            grad_query_part.reshape(rows, heads, key_local), "vax", scatter_dimension=1, tiled=True
        ),
        lax.psum_scatter(
            grad_key_part.reshape(rows, heads, key_local), "vax", scatter_dimension=1, tiled=True
        ),
        lax.psum_scatter(extra_part, "vax", scatter_dimension=1, tiled=True),
    )
    group_rep = jnp.broadcast_to(grad_group_part[None, None], (1, kax_count, value_local))
    grad_value_h, group_total = (
        lax.psum_scatter(
            grad_value_part.reshape(rows, heads, value_local).astype(jnp.bfloat16),
            "kax",
            scatter_dimension=1,
            tiled=True,
        ).astype(jnp.float32),
        lax.psum_scatter(
            group_rep.astype(jnp.bfloat16), "kax", scatter_dimension=1, tiled=True
        ).astype(jnp.float32),
    )
    grad_group_gain = group_total[0, 0]
    query_here = lax.dynamic_slice_in_dim(query_all, vax_index * heads_vax, heads_vax, 1)
    key_here = lax.dynamic_slice_in_dim(key_all, vax_index * heads_vax, heads_vax, 1)
    arg_here = lax.dynamic_slice_in_dim(decay_arg, vax_index * heads_vax, heads_vax, 1)
    rate_grad = (query_here * grad_query_h - key_here * grad_key_h).reshape(
        spans, CH, heads_vax, key_local
    )
    last_mark = (jnp.arange(CH) == CH - 1).astype(jnp.float32)[None, :, None, None]
    rate_grad = rate_grad + last_mark * extra_h[:, None]
    decay_grad = highest("ts,cthk->cshk", causal, rate_grad)
    arg_grad = decay_grad.reshape(rows, heads_vax, key_local) * jax.nn.sigmoid(-arg_here) / 16.0
    grad_decay_bias = jnp.sum(arg_grad, axis=0)
    arg_flat = arg_grad.reshape(rows, -1)
    up_here = lax.dynamic_slice_in_dim(up_float, vax_index * heads_vax, heads_vax, 1).reshape(
        rank, -1
    )
    grad_decay_up = jnp.dot(low_rank.T, arg_flat, precision=highest_mode).reshape(
        rank, heads_vax, key_local
    )
    rank_part = jnp.dot(arg_flat, up_here.T, precision=highest_mode)
    query_low = (grad_query_h * query_scale).astype(jnp.bfloat16).reshape(rows, -1)
    key_low = grad_key_h.astype(jnp.bfloat16).reshape(rows, -1)
    value_low = grad_value_h.astype(jnp.bfloat16).reshape(rows, -1)
    gate_low = grad_gate_low.reshape(rows, -1)
    query_sub = lax.dynamic_slice_in_dim(query_weight, vax_index * heads_vax, heads_vax, 1).reshape(
        width, -1
    )
    key_sub = lax.dynamic_slice_in_dim(key_weight, vax_index * heads_vax, heads_vax, 1).reshape(
        width, -1
    )
    value_sub = lax.dynamic_slice_in_dim(value_weight, kax_index * heads_kax, heads_kax, 1).reshape(
        width, -1
    )
    gate_sub = gate_local.reshape(width, -1)
    grad_query_weight = inner(normed, query_low).reshape(width, heads_vax, key_local)
    grad_key_weight = inner(normed, key_low).reshape(width, heads_vax, key_local)
    grad_value_weight = inner(normed, value_low).reshape(width, heads_kax, value_local)
    grad_gate_weight = inner(normed, gate_low).reshape(width, heads_kax, value_local)
    normed_part = jnp.dot(query_low, query_sub.T, preferred_element_type=jnp.float32)
    normed_part = normed_part + jnp.dot(key_low, key_sub.T, preferred_element_type=jnp.float32)
    normed_part = normed_part + jnp.dot(value_low, value_sub.T, preferred_element_type=jnp.float32)
    normed_part = normed_part + jnp.dot(gate_low, gate_sub.T, preferred_element_type=jnp.float32)
    normed_part = normed_part + jnp.dot(
        rank_part, decay_down.astype(jnp.float32).T, precision=highest_mode
    )
    stat_one_part = jnp.sum(token_float * gain_one * normed_part, axis=-1, keepdims=True)
    normed_slab, rank_column, stat_one = (
        lax.psum_scatter(
            normed_part.astype(jnp.bfloat16), ("kax", "vax"), scatter_dimension=1, tiled=True
        ).astype(jnp.float32),
        lax.psum_scatter(
            rank_part.astype(jnp.bfloat16), ("kax", "vax"), scatter_dimension=1, tiled=True
        ).astype(jnp.float32),
        lax.psum_scatter(
            jnp.broadcast_to(stat_one_part, (rows, group_count)).astype(jnp.bfloat16),
            ("kax", "vax"),
            scatter_dimension=1,
            tiled=True,
        ).astype(jnp.float32),
    )
    gain_slab = lax.dynamic_slice_in_dim(gain_one, pair_index * slab, slab, 0)
    input_slab = (
        grad_resid_slab
        + inv_one * gain_slab * normed_slab
        - token_slab * inv_one**3 * stat_one / width
    )
    grad_norm_gain = jnp.sum(normed_slab * token_slab * inv_one, axis=0)
    grad_decay_down = jnp.dot(normed.astype(jnp.float32).T, rank_column, precision=highest_mode)
    grad_out = grad_out_flat.reshape(heads_kax, value_local, width)
    summed = (
        lax.psum(grad_norm_gain.astype(jnp.bfloat16), "seq").astype(jnp.float32),
        lax.psum(grad_query_weight.astype(jnp.bfloat16), "seq").astype(jnp.float32),
        lax.psum(grad_key_weight.astype(jnp.bfloat16), "seq").astype(jnp.float32),
        lax.psum(grad_value_weight.astype(jnp.bfloat16), "seq").astype(jnp.float32),
        lax.psum(grad_gate_weight.astype(jnp.bfloat16), "seq").astype(jnp.float32),
        lax.psum(grad_decay_down.astype(jnp.bfloat16), "seq").astype(jnp.float32),
        lax.psum(grad_decay_up.astype(jnp.bfloat16), "seq").astype(jnp.float32),
        lax.psum(grad_decay_bias.astype(jnp.bfloat16), "seq").astype(jnp.float32),
        lax.psum(grad_group_gain.astype(jnp.bfloat16), "seq").astype(jnp.float32),
        lax.psum(grad_out.astype(jnp.bfloat16), "seq").astype(jnp.float32),
        lax.psum(grad_ffn_gain.astype(jnp.bfloat16), "seq").astype(jnp.float32),
        lax.psum(grad_ffn_gate.astype(jnp.bfloat16), "seq").astype(jnp.float32),
        lax.psum(grad_ffn_up.astype(jnp.bfloat16), "seq").astype(jnp.float32),
        lax.psum(grad_down.astype(jnp.bfloat16), "seq").astype(jnp.float32),
    )
    return (
        output,
        input_slab.astype(jnp.bfloat16),
        summed[0],
        summed[1],
        summed[2],
        summed[3],
        summed[4],
        summed[5],
        summed[6],
        summed[7],
        summed[8],
        summed[9],
        summed[10],
        summed[11],
        summed[12],
        summed[13],
    )


def solution(mesh):
    in_specs = (
        P("seq", None),
        P(),
        P(None, None, "kax"),
        P(None, None, "kax"),
        P(None, None, "vax"),
        P(None, None, "vax"),
        P(),
        P(None, None, "kax"),
        P(None, "kax"),
        P("vax"),
        P("kax", "vax", None),
        P(),
        P(None, ("kax", "vax")),
        P(None, ("kax", "vax")),
        P(("kax", "vax"), None),
        P("seq", None),
    )
    out_specs = (
        P("seq", ("kax", "vax")),
        P("seq", ("kax", "vax")),
        P(("kax", "vax")),
        P(None, "vax", "kax"),
        P(None, "vax", "kax"),
        P(None, "kax", "vax"),
        P(None, "kax", "vax"),
        P(None, ("kax", "vax")),
        P(None, "vax", "kax"),
        P("vax", "kax"),
        P("vax"),
        P("kax", "vax", None),
        P(("kax", "vax")),
        P(None, ("kax", "vax")),
        P(None, ("kax", "vax")),
        P(("kax", "vax"), None),
    )
    return jax.shard_map(shards, mesh=mesh, in_specs=in_specs, out_specs=out_specs, check_vma=False)
```

profile of v0, /device:TPU:0, one launch (start us, length us, event | category | flops | bytes accessed | tf_op | source)
XLA Modules:
  0.0 984.4 jit_solution(2593803545641135105)
XLA Ops:
  75.5 8.7 pad.113
  88.4 15.6 %pad.114 = f32[16,4,32,64]{3,2,1,0:T(8,128)} pad(f32[8,4,32,64]{3,2,1,0:T(8,128)} %pad_maximum_fusion.6, f32[]{:T(128)} %constant.95.clone.1), padding=0_1_1x0_0_0x0_0_0x0_0_0 | pad | bytes 786436 | tf_op jit(solution)/shard_map/pad | solution.py:156
  104.0 10.6 %pad.115 = f32[16,4,32,64]{3,2,1,0:T(8,128)} pad(f32[8,4,32,64]{3,2,1,0:T(8,128)S(1)} %copy-done.39, f32[]{:T(128)} %constant.95.clone.1), padding=1_0_1x0_0_0x0_0_0x0_0_0 | pad | bytes 786436 | tf_op jit(solution)/shard_map/pad | solution.py:156
  135.9 29.0 %reduce-scatter.26.cloned.1.call-done = f32[1024,1,64]{0,2,1:T(8,128)} async-done(((f32[1024,4,64]{0,2,1:T(8,128)}), f32[1024,1,64]{0,2,1:T(8,128)}) %reduce-scatter.26.cloned.1.call-update) | async-done | bytes 262160
  165.9 11.7 %psum.119 = f32[1024,1]{0,1:T(1,128)S(1)} all-reduce(f32[1024,1]{0,1:T(1,128)S(1)} %bitcast.287), channel_id=1, replica_groups=mesh['seq'=2,'kax'=4,'vax'=4] {'vax'}, use_global_device_ids=true, to_apply=%region_6.7 | all-reduce | flops 1024 | bytes 8192 | tf_op jit(solution)/shard_map/psum | solution.py:166
  185.0 77.5 %reduce-scatter.14.cloned.1.call-done = bf16[1024,64]{0,1:T(8,128)(2,1)} async-done(((bf16[1024,1024]{0,1:T(8,128)(2,1)}), bf16[1024,64]{0,1:T(8,128)(2,1)}) %reduce-scatter.14.cloned.1.call-update) | async-done | bytes 131088 | tf_op jit(solution)/shard_map/reduce_scatter | solution.py:174
  264.7 58.9 %all-gather.2.cloned.1.call-done = bf16[1024,1024]{0,1:T(8,128)(2,1)} async-done(((bf16[1024,64]{0,1:T(8,128)(2,1)}), bf16[1024,1024]{0,1:T(8,128)(2,1)}) %all-gather.2.cloned.1.call-update) | async-done | bytes 2097168 | tf_op jit(solution)/shard_map/all_gather | solution.py:182
  352.5 106.8 %all-reduce.44.cloned.1.call-done = bf16[1024,1024]{0,1:T(8,128)(2,1)} async-done(((bf16[1024,1024]{0,1:T(8,128)(2,1)}), bf16[1024,1024]{0,1:T(8,128)(2,1)}) %all-reduce.44.cloned.1.call-update) | async-done | bytes 2097168 | tf_op jit(solution)/shard_map/psum | solution.py:207
  469.0 10.1 %psum.121 = f32[1024]{0:T(1024)S(1)} all-reduce(f32[1024]{0:T(1024)S(1)} %get-tuple-element.249), channel_id=1, replica_groups=mesh['seq'=2,'kax'=4,'vax'=4] {'vax'}, use_global_device_ids=true, to_apply=%region_13.14 | all-reduce | flops 1024 | bytes 8192 | tf_op jit(solution)/shard_map/psum | solution.py:226
  480.0 10.8 %all_gather.25 = bf16[1024,4,64]{0,2,1:T(8,128)(2,1)S(1)} all-gather(bf16[1024,1,64]{0,2,1:T(8,128)(2,1)S(1)} %get-tuple-element.298), channel_id=1, replica_groups=mesh['seq'=2,'kax'=4,'vax'=4] {'kax'}, dimensions={1}, use_global_device_ids=true | all-gather | bytes 655360 | tf_op jit(solution)/shard_map/all_gather | solution.py:228
  509.8 8.7 pad.129
  522.7 15.6 %pad.130 = f32[16,4,32,64]{3,2,1,0:T(8,128)} pad(f32[8,4,32,64]{3,2,1,0:T(8,128)} %pad_maximum_fusion.7, f32[]{:T(128)} %constant.95.clone.1), padding=0_1_1x0_0_0x0_0_0x0_0_0 | pad | bytes 786436 | tf_op jit(solution)/shard_map/pad | solution.py:233
  538.3 10.6 %pad.131 = f32[16,4,32,64]{3,2,1,0:T(8,128)} pad(f32[8,4,32,64]{3,2,1,0:T(8,128)S(1)} %copy-done.40, f32[]{:T(128)} %constant.95.clone.1), padding=1_0_1x0_0_0x0_0_0x0_0_0 | pad | bytes 786436 | tf_op jit(solution)/shard_map/pad | solution.py:233
  562.5 5.4 fusion.41
  577.2 5.3 fusion.28
  610.0 5.1 reduce-scatter.18.cloned.1.call-done
  616.4 18.6 %reduce-scatter.22.cloned.1.call-done = f32[16,1,32]{2,0,1:T(8,128)} async-done(((f32[16,4,32]{2,0,1:T(8,128)}), f32[16,1,32]{2,0,1:T(8,128)}) %reduce-scatter.22.cloned.1.call-update) | async-done | bytes 2064 | tf_op jit(solution)/shard_map/reduce_scatter | solution.py:260
  645.4 15.6 %reduce-scatter.28.cloned.1.call-done = bf16[1024,1,64]{0,2,1:T(8,128)(2,1)} async-done(((bf16[1024,4,64]{0,2,1:T(8,128)(2,1)}), bf16[1024,1,64]{0,2,1:T(8,128)(2,1)}) %reduce-scatter.28.cloned.1.call-update) | async-done | bytes 131088
  662.8 7.3 multiply_reduce_fusion
  681.4 8.9 all-reduce.36
  691.2 82.2 %all-reduce.46.cloned.1.call-done = (bf16[1024,16]{0,1:T(8,128)(2,1)}, bf16[1024,16]{0,1:T(8,128)(2,1)}) async-done(((bf16[1024,16]{0,1:T(8,128)(2,1)}, bf16[1024,16]{0,1:T(8,128)(2,1)}), (bf16[1024,16]{0,1:T(8,128)(2,1)}, bf16[1024,16]{0,1:T(8,128)(2,1)})) %all-reduce.46.cloned.1.call-update) | async-done | bytes 65552
  776.8 20.6 %all-reduce.48.cloned.1.call-done = (bf16[1024,1,32]{0,2,1:T(8,128)(2,1)}, bf16[1024,1,32]{0,2,1:T(8,128)(2,1)}, bf16[1024,1,64]{0,2,1:T(8,128)(2,1)}, bf16[1024...) async-done(((bf16[1024,1,32]{0,2,1:T(8,128)(2,1)}, ...) | async-done | bytes 1605648 | tf_op jit(solution)/shard_map/psum | solution.py:345
  809.1 76.1 %reduce-scatter.16.cloned.1.call-done = bf16[1024,64]{0,1:T(8,128)(2,1)} async-done(((bf16[1024,1024]{0,1:T(8,128)(2,1)}), bf16[1024,64]{0,1:T(8,128)(2,1)}) %reduce-scatter.16.cloned.1.call-update) | async-done | bytes 131088 | tf_op jit(solution)/shard_map/reduce_scatter | solution.py:192
  885.3 83.1 %reduce-scatter.24.cloned.1.call-done = bf16[1024,64]{0,1:T(8,128)(2,1)} async-done(((bf16[1024,1024]{0,1:T(8,128)(2,1)}), bf16[1024,64]{0,1:T(8,128)(2,1)}) %reduce-scatter.24.cloned.1.call-update) | async-done | bytes 131088 | tf_op jit(solution)/shard_map/reduce_scatter | solution.py:321
  (504 shorter events, 265.3 us)
Async XLA Ops:
  7.2 49.4 %copy-start = (bf16[1024,4,64]{0,2,1:T(8,128)(2,1)S(1)}, bf16[1024,4,64]{0,2,1:T(8,128)(2,1)}, u32[]{:S(2)}) copy-start(bf16[1024,4,64]{0,2,1:T(8,128)(2,1)} %param.24) | copy-start | bytes 1572868
  7.2 157.7 %reduce-scatter.26.cloned.1.call-start = ((), (), s32[]{:S(2)}) async-start(), calls=%async_computation.16 | async-start | bytes 1310720
  7.3 118.0 %copy-start.53 = (f32[64,64]{1,0:T(8,128)}, f32[64,64]{1,0:T(8,128)S(1)}, u32[]{:S(2)}) copy-start(f32[64,64]{1,0:T(8,128)S(1)} %fusion.134) | copy-start | bytes 49156
  87.5 29.8 %copy-start.94 = (bf16[2,4,32]{2,1,0:T(4,128)(2,1)S(1)}, bf16[2,4,32]{2,1,0:T(4,128)(2,1)}, u32[]{:S(2)}) copy-start(bf16[2,4,32]{2,1,0:T(4,128)(2,1)} %all_gather.22) | copy-start | bytes 1540
  88.4 29.2 %copy-start.72 = (f32[16,4,32]{2,1,0:T(4,128)S(1)}, f32[16,4,32]{2,1,0:T(4,128)}, u32[]{:S(2)}) copy-start(f32[16,4,32]{2,1,0:T(4,128)} %copy.212) | copy-start | bytes 24580
  134.4 44.3 %copy-start.57 = (bf16[1,64,1024]{2,1,0:T(8,128)(2,1)S(1)}, bf16[1,64,1024]{2,1,0:T(8,128)(2,1)}, u32[]{:S(2)}) copy-start(bf16[1,64,1024]{2,1,0:T(8,128)(2,1)} %param.30) | copy-start | bytes 393220
  134.4 128.1 %reduce-scatter.14.cloned.1.call-start = ((), (), s32[]{:S(2)}) async-start(), calls=%async_computation.8 | async-start | bytes 2228224 | tf_op jit(solution)/shard_map/reduce_scatter | solution.py:174
  134.5 46.3 %copy-start.105 = (f32[64]{0:T(128)}, f32[64]{0:T(128)S(1)}, u32[]{:S(2)}) copy-start(f32[64]{0:T(128)S(1)} %convert_element_type.309) | copy-start | bytes 772
  180.9 142.7 %all-gather.2.cloned.1.call-start = ((), (), s32[]{:S(2)}) async-start(), calls=%async_computation.9 | async-start | bytes 2228224 | tf_op jit(solution)/shard_map/all_gather | solution.py:182
  180.9 83.8 %copy-start.107 = (bf16[1024]{0:T(1024)(128)(2,1)S(1)}, bf16[1024]{0:T(1024)(128)(2,1)}, u32[]{:S(2)}) copy-start(bf16[1024]{0:T(1024)(128)(2,1)} %param.31) | copy-start | bytes 6148
  264.3 195.0 %all-reduce.44.cloned.1.call-start = ((), (), s32[]{:S(2)}) async-start(), calls=%async_computation.11 | async-start | bytes 4194304 | tf_op jit(solution)/shard_map/psum | solution.py:207
  334.5 275.5 %reduce-scatter.20.cloned.1.call-start = ((), (), s32[]{:S(2)}) async-start(), calls=%async_computation.13 | async-start | bytes 655360 | tf_op jit(solution)/shard_map/reduce_scatter | solution.py:257
  574.0 41.1 %reduce-scatter.18.cloned.1.call-start = ((), (), s32[]{:S(2)}) async-start(), calls=%async_computation.12 | async-start | bytes 655360 | tf_op jit(solution)/shard_map/reduce_scatter | solution.py:254
  592.7 42.2 %reduce-scatter.22.cloned.1.call-start = ((), (), s32[]{:S(2)}) async-start(), calls=%async_computation.14 | async-start | bytes 40960 | tf_op jit(solution)/shard_map/reduce_scatter | solution.py:260
  603.8 57.2 %reduce-scatter.28.cloned.1.call-start = ((), (), s32[]{:S(2)}) async-start(), calls=%async_computation.17 | async-start | bytes 655360
  606.9 28.0 %copy-start.109 = (f32[64]{0:T(128)S(1)}, f32[64]{0:T(128)}, u32[]{:S(2)}) copy-start(f32[64]{0:T(128)} %compare_convert_fusion) | copy-start | bytes 772
  609.6 163.8 %all-reduce.46.cloned.1.call-start = ((), (), s32[]{:S(2)}) async-start(), calls=%async_computation.18 | async-start | bytes 131072
  610.0 28.2 %copy-start.49 = (f32[1024,1,32]{0,2,1:T(8,128)S(1)}, f32[1024,1,32]{0,2,1:T(8,128)}, u32[]{:S(2)}) copy-start(f32[1024,1,32]{0,2,1:T(8,128)} %reduce-scatter.20.cloned.1.call-done) | copy-start | bytes 393220
  670.8 126.6 %all-reduce.48.cloned.1.call-start = ((), (), s32[]{:S(2)}) async-start(), calls=%async_computation.19 | async-start | bytes 3211264 | tf_op jit(solution)/shard_map/psum | solution.py:345
  675.0 210.3 %reduce-scatter.16.cloned.1.call-start = ((), (), s32[]{:S(2)}) async-start(), calls=%async_computation.10 | async-start | bytes 2228224 | tf_op jit(solution)/shard_map/reduce_scatter | solution.py:192
  678.2 290.2 %reduce-scatter.24.cloned.1.call-start = ((), (), s32[]{:S(2)}) async-start(), calls=%async_computation.15 | async-start | bytes 2228224 | tf_op jit(solution)/shard_map/reduce_scatter | solution.py:321
  802.1 166.3 %copy-start.59 = (bf16[1024,64]{0,1:T(8,128)(2,1)S(1)}, bf16[1024,64]{0,1:T(8,128)(2,1)}, u32[]{:S(2)}) copy-start(bf16[1024,64]{0,1:T(8,128)(2,1)} %reduce-scatter.14.cloned.1.call-done) | copy-start | bytes 393220
  802.1 166.3 %copy-start.88 = (f32[1024]{0:T(1024)S(1)}, f32[1024]{0:T(1024)}, u32[]{:S(2)}) copy-start(f32[1024]{0:T(1024)} %copy-done.87) | copy-start | bytes 12292
  802.1 166.3 %copy-start.97 = (f32[1024]{0:T(1024)S(1)}, f32[1024]{0:T(1024)}, u32[]{:S(2)}) copy-start(f32[1024]{0:T(1024)} %get-tuple-element.316) | copy-start | bytes 12292
  (103 other events, 441.4 us)
Sparse Core Ops, SparseCore 0:
  134.5 30.2 reduce-scatter.25
  181.0 81.5 reduce-scatter.13
  266.3 57.2 all-gather.1
  334.6 124.6 all-reduce.43
  574.1 18.8 reduce-scatter.19
  595.2 19.8 reduce-scatter.17
  617.9 16.9 reduce-scatter.21
  638.0 22.9 reduce-scatter.27
  670.9 102.4 all-reduce.45
  777.5 19.8 all-reduce.47
  799.7 85.5 reduce-scatter.15
  887.5 80.8 reduce-scatter.23
where the time goes:
time: 998 us; the launch traced here: 984 us
  waiting for transfers between devices  574 us (58%)
  local copies, waits for them, and re-layouts  155 us (16%)
  matrix products  103 us (10%)
  other arithmetic  81.2 us (8%)
  blocking collectives  52.8 us (5%)
  between operations  16.3 us (2%)
    unnamed x15, waiting for transfers between devices  127 us
    psum x1, waiting for transfers between devices, shards(): lax.psum(ffn_in_part.astype(jnp.bfloat16), ('kax', 'vax'))  107 us
    reduce_scatter x1, waiting for transfers between devices, shards(): lax.psum_scatter(normed_part.astype(jnp.bfloat16), ('kax', 'vax'), scatte...  83.1 us
    reduce_scatter x1, waiting for transfers between devices, shards(): lax.psum_scatter(product(gated_flat, out_flat).astype(jnp.bfloat16), ('ka...  77.5 us
    reduce_scatter x1, waiting for transfers between devices, shards(): lax.psum_scatter(product(hidden, ffn_down).astype(jnp.bfloat16), ('kax',...  76.1 us
    all_gather x1, waiting for transfers between devices, shards(): lax.all_gather(resid_slab.astype(jnp.bfloat16), ('kax', 'vax'), axis=1, t...  58.9 us
    dot_general x13, matrix products, highest(): return jnp.einsum(form, left, right, precision=lax.Precision.HIGHEST)  44.5 us
    pad x12, local copies, waits for them, and re-layouts, shards(): lax.associative_scan(compose, (span_decay[::-1], state_weight[::-1]), axi...  43.1 us
  transfers between devices with their start and end apart: 12, of which 11 were waited for; matrix products, arithmetic and copies ran while one was open for 9% of the time, Pallas kernels for 0%

commit v1 on v0

v1 whole, which is shorter than its diff:
```python
import functools

import jax
import jax.numpy as jnp
from jax import lax
from jax.experimental import pallas as pl
from jax.experimental.pallas import tpu as pltpu
from jax.sharding import PartitionSpec as P

MESH = pl.DeviceIdType.MESH
BF = jnp.bfloat16
F32 = jnp.float32
CB = 128
WAYS = 4
EPS = 1e-06
HIGH = lax.Precision.HIGHEST


def nn(a, b, precision=None):
    return lax.dot_general(
        a, b, (((1,), (0,)), ((), ())), precision=precision, preferred_element_type=F32
    )


def nt(a, b, precision=None):
    return lax.dot_general(
        a, b, (((1,), (1,)), ((), ())), precision=precision, preferred_element_type=F32
    )


def tn(a, b, precision=None):
    return lax.dot_general(
        a, b, (((0,), (0,)), ((), ())), precision=precision, preferred_element_type=F32
    )


def xor(index, d):
    if d == 1:
        return index + 1 - 2 * lax.rem(index, 2)
    if d == 2:
        return lax.rem(index + 2, 4)
    return 3 - index


def as_row(column):
    return jnp.broadcast_to(column, (column.shape[0], 128)).T[:8]


def as_column(row):
    return jnp.broadcast_to(row[:1], (128, row.shape[1])).T[:, :1]


def layer_kernel(
    n_seq,
    tok,
    cot,
    gains,
    wq,
    wk,
    ext,
    wv,
    wg,
    gge,
    dd,
    wo,
    fg,
    fu,
    fd,
    o_out,
    o_in,
    o_f,
    o_vg,
    o_qk,
    o_ext,
    o_ow,
    o_small,
    x_v,
    c_v,
    n_v,
    xr_v,
    dd_v,
    gain_v,
    qk_v,
    ext_v,
    v_v,
    g_v,
    gge_v,
    o_v,
    f_v,
    st_v,
    tt_v,
    bst_v,
    btt_v,
    ga_v,
    sgg,
    rgg,
    sst,
    rst,
    so,
    ro,
    sgf,
    rgf,
    sgn,
    rgn,
    snt,
    rnt,
    ao,
    oseg,
    ai,
    iseg,
    gw,
    pre,
    pres,
    rfw,
    fin_f,
    gv,
    prev,
    presv,
    rvg,
    mid_vg,
    perm_vg,
    fin_vg,
    gq,
    preq,
    presq,
    rqk,
    fin_qk,
    ge,
    preg,
    rge,
    fin_e,
    gow,
    preo,
    preso,
    row_,
    mid_ow,
    fin_ow,
    sm0,
    sm1,
    sm2,
    sm3,
    pick,
    gh_v,
    act_v,
    p_v,
    ss,
    rs,
    ls,
):
    s = lax.axis_index("seq")
    i = lax.axis_index("kax")
    j = lax.axis_index("vax")
    par = lax.rem(s, 2)
    oth = 1 - par
    T = x_v.shape[0]
    D = x_v.shape[1]
    half = D // 2
    W = WAYS
    mine = pl.ds(pl.multiple_of(par * half, half), half)
    other = pl.ds(pl.multiple_of(oth * half, half), half)
    partner = {"seq": s + 1 - 2 * par}
    kdev = [None] + [{"kax": xor(i, d)} for d in (1, 2, 3)]
    vdev = [None] + [{"vax": xor(j, d)} for d in (1, 2, 3)]
    ki = [None] + [xor(i, d) for d in (1, 2, 3)]
    vj = [None] + [xor(j, d) for d in (1, 2, 3)]
    seqdev = [{"seq": lax.rem(s + e, n_seq)} for e in range(1, n_seq)]
    flip = {"kax": j, "vax": i}

    count = [0, 0]
    sent = []

    def remote(src, dst, dev):
        n = count[0]
        count[0] += 1
        return pltpu.make_async_remote_copy(
            src_ref=src,
            dst_ref=dst,
            send_sem=ss.at[n],
            recv_sem=rs.at[n],
            device_id=dev,
            device_id_type=MESH,
        )

    def send(src, dst, dev):
        cp = remote(src, dst, dev)
        cp.start()
        sent.append(cp)
        return cp

    def load(src, dst):
        n = count[1]
        count[1] += 1
        cp = pltpu.make_async_copy(src, dst, ls.at[n])
        cp.start()
        return cp

    l_qk = [load(wq.at[j], qk_v.at[i, 0]), load(wk.at[j], qk_v.at[i, 1]), load(ext, ext_v.at[i])]
    l_x = [load(tok.at[pl.ds(pl.multiple_of(i * T, T), T)], x_v), load(gains, gain_v)]
    dd_v[16:, :] = jnp.zeros((dd_v.shape[0] - 16, D), BF)
    l_dd = load(dd, dd_v.at[pl.ds(0, 16)])
    l_v = load(wv.at[j], v_v.at[j])
    l_g = [load(wg.at[j], g_v.at[j]), load(gge, gge_v.at[j])]
    l_c = load(cot.at[pl.ds(pl.multiple_of(i * T, T), T)], c_v)
    l_f = [load(fg, f_v.at[0, i]), load(fu, f_v.at[1, i]), load(fd, f_v.at[2, i])]
    l_o = load(wo, o_v.at[i, j])

    barrier = pltpu.get_barrier_semaphore()
    for dev in kdev[1:] + vdev[1:] + seqdev:
        pl.semaphore_signal(barrier, inc=1, device_id=dev, device_id_type=MESH)

    others = 6 + len(seqdev)

    @pl.when(i != j)
    def _():
        pl.semaphore_signal(barrier, inc=1, device_id=flip, device_id_type=MESH)
        pl.semaphore_wait(barrier, others + 1)

    @pl.when(i == j)
    def _():
        pl.semaphore_wait(barrier, others)

    for cp in l_qk:
        cp.wait()
    t_qk = [None] + [send(qk_v.at[i, par], qk_v.at[i, par], kdev[d]) for d in (1, 2, 3)]
    t_ext = [None] + [send(ext_v.at[i], ext_v.at[i], kdev[d]) for d in (1, 2, 3)]
    t_v = [None] + [
        send(wv.at[vj[d], :, mine], v_v.at[j, :, mine], vdev[d]) for d in (1, 2, 3)
    ]

    for cp in l_x:
        cp.wait()
    x = x_v[...].astype(F32)
    g1 = gain_v[0:1, :]
    g3 = gain_v[1:2, :]
    r1 = lax.rsqrt(jnp.sum(x * x, axis=1, keepdims=True) / D + EPS)
    n_v[...] = (x * r1 * g1).astype(BF)
    l_dd.wait()
    lane = lax.broadcasted_iota(jnp.int32, (T, 128), 1)
    lrp = jnp.where(lane == 16, 1.0, nt(n_v[...], dd_v[...]))
    xr_v[...] = (x * (r1 * r1 * r1)).astype(BF).T

    f_qk = []
    for d in (1, 2, 3):
        t_qk[d].wait_recv()
        f_qk.append(send(qk_v.at[ki[d], par], qk_v.at[ki[d], par], partner))
    t_f = []
    for d in (1, 2, 3):
        t_f.append(
            [
                send(w.at[:, mine], f_v.at[n, i, :, mine], kdev[d])
                for n, w in enumerate((fg, fu, fd))
            ]
        )
    for d in (1, 2, 3):
        t_ext[d].wait_recv()
    for cp in f_qk:
        cp.wait_recv()
    normed = n_v[...]
    wq_all = qk_v[:, 0].reshape(W * 32, D)
    wk_all = qk_v[:, 1].reshape(W * 32, D)
    ext_all = ext_v[...].reshape(W * 32, 128)
    scale = 128.0 ** (-0.5)
    q = nt(normed, wq_all) * scale
    k = nt(normed, wk_all)
    arg = nt(lrp, ext_all.astype(F32), HIGH)
    rates = (jnp.minimum(arg, 0.0) - jnp.log1p(jnp.exp(-jnp.abs(arg)))) / 16.0
    row_id = lax.broadcasted_iota(jnp.int32, (CB, CB), 0)
    col_id = lax.broadcasted_iota(jnp.int32, (CB, CB), 1)
    causal = row_id >= col_id
    tri = jnp.where(causal, 1.0, 0.0)
    nblk = T // CB
    blk = [slice(c * CB, (c + 1) * CB) for c in range(nblk)]
    e1, e2, em, el, dec, qd, kd, qi, ke, score = [], [], [], [], [], [], [], [], [], []
    for c in range(nblk):
        cum = nn(tri, rates[blk[c]], HIGH)
        mid = cum[CB // 2 - 1 : CB // 2]
        last = cum[CB - 1 : CB]
        e1.append(jnp.exp(cum - mid))
        e2.append(jnp.exp(mid - cum))
        em.append(jnp.exp(mid))
        el.append(jnp.exp(last - mid))
        dec.append(jnp.exp(last))
        a = q[blk[c]] * e1[c]
        b = k[blk[c]] * e2[c]
        qd.append(a.astype(BF))
        kd.append(b.astype(BF))
        qi.append((a * em[c]).astype(BF))
        ke.append((b * el[c]).astype(BF))
        score.append(jnp.where(causal, nt(qd[c], kd[c]), 0.0).astype(BF))

    l_v.wait()
    f_vv = []
    for d in (1, 2, 3):
        t_v[d].wait_recv()
        f_vv.append(send(v_v.at[vj[d], :, mine], v_v.at[vj[d], :, mine], partner))
    t_g = [None] + [
        send(wg.at[vj[d], :, mine], g_v.at[j, :, mine], vdev[d]) for d in (1, 2, 3)
    ]
    t_gge = [None] + [send(gge, gge_v.at[j], vdev[d]) for d in (1, 2, 3)]
    t_o = [None] + [
        send(wo.at[:, mine], o_v.at[i, j, :, mine], vdev[d]) for d in (1, 2, 3)
    ]
    for cp in f_vv:
        cp.wait_recv()
    wv_all = v_v[...].reshape(W * 64, D)
    v = nt(normed, wv_all).astype(BF)
    up = [tn(v[blk[c]], ke[c]) for c in range(nblk)]
    loc = up[0]
    locd = dec[0]
    for c in range(1, nblk):
        loc = loc * dec[c] + up[c]
        locd = locd * dec[c]
    VC = loc.shape[0]
    st_v[i, :VC] = loc.astype(BF)
    st_v[i, VC:] = jnp.broadcast_to(locd, (16, 128)).astype(BF)
    t_st = [send(st_v.at[i], st_v.at[i], kdev[d]) for d in (1, 2, 3)]
    mixed = [nn(score[c], v[blk[c]]) for c in range(nblk)]

    f_g = []
    for cp in l_g:
        cp.wait()
    for d in (1, 2, 3):
        t_g[d].wait_recv()
        f_g.append(send(g_v.at[vj[d], :, mine], g_v.at[vj[d], :, mine], partner))

    def entering(slots, totals, back):
        order = range(W - 1, -1, -1) if back else range(W)
        pre_s = jnp.zeros((VC, 128), F32)
        pre_d = jnp.ones((1, 128), F32)
        tot_s = jnp.zeros((VC, 128), F32)
        tot_d = jnp.ones((1, 128), F32)
        for other_i in order:
            one_s = slots[other_i, :VC].astype(F32)
            one_d = slots[other_i, VC : VC + 1].astype(F32)
            use = (other_i > i) if back else (other_i < i)
            pre_s = jnp.where(use, pre_s * one_d + one_s, pre_s)
            pre_d = jnp.where(use, pre_d * one_d, pre_d)
            tot_s = tot_s * one_d + one_s
            tot_d = tot_d * one_d
        totals[s, :VC] = tot_s.astype(BF)
        totals[s, VC:] = jnp.broadcast_to(tot_d, (16, 128)).astype(BF)
        moves = [send(totals.at[s], totals.at[s], dev) for dev in seqdev]
        for cp in moves:
            cp.wait_recv()
        order = range(n_seq - 1, -1, -1) if back else range(n_seq)
        far = jnp.zeros((VC, 128), F32)
        for other_s in order:
            one_s = totals[other_s, :VC].astype(F32)
            one_d = totals[other_s, VC : VC + 1].astype(F32)
            use = (other_s > s) if back else (other_s < s)
            far = jnp.where(use, far * one_d + one_s, far)
        return pre_s + pre_d * far

    for cp in t_st:
        cp.wait_recv()
    start = [entering(st_v, tt_v, False)]
    for c in range(nblk):
        start.append(start[c] * dec[c] + up[c])
    start_low = [a.astype(BF) for a in start]
    for c in range(nblk):
        mixed[c] = mixed[c] + nt(qi[c], start_low[c])
    mix = jnp.concatenate(mixed, axis=0)
    r2 = lax.rsqrt(jnp.sum(mix * mix, axis=1, keepdims=True) / VC + EPS)
    normal = mix * r2
    for cp in f_g:
        cp.wait_recv()
    for d in (1, 2, 3):
        t_gge[d].wait_recv()
    wg_all = g_v[...].reshape(W * 64, D)
    gate = nt(normed, wg_all)
    gg = gge_v[...].astype(F32).reshape(W * 64, 128).T[:1]
    sig = 1.0 / (1.0 + jnp.exp(-gate))
    act = gate * sig
    dact = sig + act * (1.0 - sig)
    ga_v[j] = (normal * gg * act).astype(BF)
    t_ga = [send(ga_v.at[j], ga_v.at[j], vdev[d]) for d in (1, 2, 3)]
    act_v[0] = act
    act_v[1] = dact
    act_v[2] = normal

    l_o.wait()
    for d in (1, 2, 3):
        t_o[d].wait_recv()
    t_o2 = [None] + [
        send(o_v.at[i, :, :, mine], o_v.at[i, :, :, mine], kdev[d]) for d in (1, 2, 3)
    ]
    f_o = [
        send(o_v.at[i, vj[d], :, mine], o_v.at[i, vj[d], :, mine], partner) for d in (1, 2, 3)
    ]
    for cp in l_f:
        cp.wait()
    f_f = []
    for d in (1, 2, 3):
        for cp in t_f[d - 1]:
            cp.wait_recv()
        f_f.append(send(f_v.at[:, ki[d], :, mine], f_v.at[:, ki[d], :, mine], partner))
    l_c.wait()
    for cp in f_f:
        cp.wait_recv()
    FB = f_v.shape[2]
    gT = f_v[0].reshape(W * FB, D)
    uT = f_v[1].reshape(W * FB, D)
    dn = f_v[2].reshape(W * FB, D)
    gh_v[...] = nt(c_v[...], dn)
    for d in (1, 2, 3):
        t_o2[d].wait_recv()
        f_o.append(
            send(o_v.at[ki[d], :, :, mine], o_v.at[ki[d], :, :, mine], partner)
        )
    for cp in t_ga:
        cp.wait_recv()
    for cp in f_o:
        cp.wait_recv()
    att = nn(ga_v[0], o_v[0].reshape(W * 64, D))
    for h in range(1, W):
        att = att + nn(ga_v[h], o_v[h].reshape(W * 64, D))
    resid = x_v[...].astype(F32) + att
    r3 = lax.rsqrt(jnp.sum(resid * resid, axis=1, keepdims=True) / D + EPS)
    fin = (resid * r3 * g3).astype(BF)

    gval = nt(fin, gT)
    uval = nt(fin, uT)
    fsig = 1.0 / (1.0 + jnp.exp(-gval))
    fact = gval * fsig
    hid = (fact * uval).astype(BF)
    gh = gh_v[...]
    gup = (gh * fact).astype(BF)
    ggate = (gh * uval * (fsig + fact * (1.0 - fsig))).astype(BF)
    part = nn(ggate, gT) + nn(gup, uT)
    p_v[...] = part
    ow_flat = o_v[...].reshape(W * W * 64, D)
    ggp = nt((part * g3).astype(BF), ow_flat)
    for h in range(W):
        sgg[h] = ggp[:, h * VC : (h + 1) * VC].astype(BF)
    t_gg = [send(sgg.at[vj[d]], rgg.at[d], vdev[d]) for d in (1, 2, 3)]
    m3p = jnp.sum(resid * g3 * part, axis=1, keepdims=True)
    sst[...] = as_row(m3p)
    t_m3 = [send(sst, rst.at[d], vdev[d]) for d in (1, 2, 3)]

    feature = lax.broadcasted_iota(jnp.int32, (1, D), 1)
    own_slab = jnp.where(lax.rem(feature // 64, W) == j, 1.0, 0.0)
    own_run = jnp.where(feature // (D // W) == j, 1.0, 0.0)
    outp = nn(hid, dn) + own_slab * resid
    so[...] = outp.astype(BF).T.reshape(W, W, 64, T)
    t_out = [send(so.at[:, vj[d]], ro.at[d], vdev[d]) for d in (1, 2, 3)]
    ffn_gain = jnp.sum(part * resid * r3, axis=0, keepdims=True)

    gw[0] = tn(ggate, fin).astype(BF).reshape(W, FB, D)
    gw[1] = tn(gup, fin).astype(BF).reshape(W, FB, D)
    gw[2] = tn(hid, c_v[...]).astype(BF).reshape(W, FB, D)
    t_pre = send(gw.at[:, :, :, other], pre, partner)

    for cp in t_m3:
        cp.wait_recv()
    m3 = as_column(sst[...] + rst[1] + rst[2] + rst[3]) / D
    base = c_v[...].astype(F32) - resid * (r3 * r3 * r3 * m3)
    direct = nt(base.astype(BF), o_v[j].reshape(W * 64, D))
    for cp in t_gg:
        cp.wait_recv()
    ggs = sgg[j].astype(F32) + rgg[1].astype(F32) + rgg[2].astype(F32) + rgg[3].astype(F32)
    ggrad = direct + r3 * ggs
    act = act_v[0]
    normal = act_v[2]
    dgate = (ggrad * normal * gg * act_v[1]).astype(BF)
    gs = ggrad * act
    group = jnp.sum(gs * normal, axis=0, keepdims=True)
    gnm = gs * gg
    gmix = (r2 * (gnm - normal * (jnp.sum(normal * gnm, axis=1, keepdims=True) / VC))).astype(BF)

    qst = [tn(gmix[blk[c]], qi[c]) for c in range(nblk)]
    bloc = qst[nblk - 1]
    for c in range(nblk - 2, -1, -1):
        bloc = bloc * dec[c] + qst[c]
    bst_v[i, :VC] = bloc.astype(BF)
    bst_v[i, VC:] = jnp.broadcast_to(locd, (16, 128)).astype(BF)
    t_bst = [send(bst_v.at[i], bst_v.at[i], kdev[d]) for d in (1, 2, 3)]

    full = p_v[...] * (g3 * r3)
    mixed_in = full + own_run * base
    for h in range(W):
        sgf[h] = mixed_in[:, h * (D // W) : (h + 1) * (D // W)].astype(BF)
    t_gf = [send(sgf.at[vj[d]], rgf.at[d], vdev[d]) for d in (1, 2, 3)]
    gv[1] = tn(dgate, normed).astype(BF).reshape(W, 64, D)
    dscore, dq_in, dk_in, dv_in = [], [], [], []
    for c in range(nblk):
        ds = jnp.where(causal, nt(gmix[blk[c]], v[blk[c]]), 0.0).astype(BF)
        dq_in.append(nn(ds, kd[c]) + em[c] * nn(gmix[blk[c]], start_low[c]))
        dk_in.append(tn(ds, qd[c]))
        dv_in.append(tn(score[c], gmix[blk[c]]))
    t_pre.wait_recv()
    for n in range(3):
        pres[n] = (gw[n, :, :, mine].astype(F32) + pre[n].astype(F32)).astype(BF)
    for cp in t_bst:
        cp.wait_recv()
    after = [None] * nblk
    after[nblk - 1] = entering(bst_v, btt_v, True)
    for c in range(nblk - 2, -1, -1):
        after[c] = after[c + 1] * dec[c + 1] + qst[c + 1]
    t_fw = [send(pres.at[:, ki[d]], rfw.at[d], kdev[d]) for d in (1, 2, 3)]

    ql, kl, vl, ga = [], [], [], []
    for c in range(nblk):
        low_after = after[c].astype(BF)
        dq = e1[c] * dq_in[c]
        dk = e2[c] * (dk_in[c] + el[c] * nn(v[blk[c]], low_after))
        dv = dv_in[c] + nt(ke[c], low_after)
        gc = q[blk[c]] * dq - k[blk[c]] * dk
        extra = jnp.sum(after[c] * start[c + 1], axis=0, keepdims=True)
        gc = jnp.where(row_id == CB - 1, gc + extra, gc)
        gr = tn(tri, gc, HIGH)
        a = arg[blk[c]]
        ga.append(gr / (1.0 + jnp.exp(a)) / 16.0)
        ql.append((dq * scale).astype(BF))
        kl.append(dk.astype(BF))
        vl.append(dv.astype(BF))
    ql = jnp.concatenate(ql, axis=0)
    kl = jnp.concatenate(kl, axis=0)
    vl = jnp.concatenate(vl, axis=0)
    ga = jnp.concatenate(ga, axis=0).astype(BF)
    glr = nn(ga, ext_all).astype(BF)
    gn = nn(ql, wq_all) + nn(kl, wk_all) + nn(vl, wv_all) + nn(dgate, wg_all) + nn(glr, dd_v[...])
    x = x_v[...].astype(F32)
    gnx = gn * x
    snt[...] = as_row(jnp.sum(gnx * g1, axis=1, keepdims=True))
    t_m1 = [send(snt, rnt.at[d], vdev[d]) for d in (1, 2, 3)]
    whole = gn * (r1 * g1) + full + own_slab * base
    sgn[...] = whole.astype(BF).T.reshape(W, W, 64, T)
    t_gn = [send(sgn.at[:, vj[d]], rgn.at[d], vdev[d]) for d in (1, 2, 3)]

    norm_gain = jnp.sum(gnx * r1, axis=0, keepdims=True)
    small = tn(glr, normed)[:16]
    rid = lax.broadcasted_iota(jnp.int32, (16, D), 0)
    wide = jnp.concatenate([group, jnp.zeros((1, D - VC), F32)], axis=1)
    rest = jnp.where(rid == 0, norm_gain, jnp.where(rid == 1, ffn_gain, jnp.where(rid == 2, wide, 0.0)))
    sm0[:16] = small.astype(BF)
    sm0[16:] = rest.astype(BF)
    t_s0 = [send(sm0, sm1.at[d], vdev[d]) for d in (1, 2, 3)]

    gv[0] = tn(vl, normed).astype(BF).reshape(W, 64, D)
    gq[:, 0] = tn(ql, normed).astype(BF).reshape(W, 32, D)
    gq[:, 1] = tn(kl, normed).astype(BF).reshape(W, 32, D)
    ge[...] = tn(ga, lrp.astype(BF)).reshape(W, 32, 128)
    t_pv = send(gv.at[:, :, :, other], prev, partner)
    t_pq = send(gq.at[:, oth], preq, partner)
    t_ge = send(ge, preg, partner)
    t_pv.wait_recv()
    for n in range(2):
        presv[n] = (gv[n, :, :, mine].astype(F32) + prev[n].astype(F32)).astype(BF)
    t_vg = [send(presv.at[:, ki[d]], rvg.at[d], kdev[d]) for d in (1, 2, 3)]
    t_pq.wait_recv()
    presq[...] = (gq[:, par].astype(F32) + preq[...].astype(F32)).astype(BF)
    t_qk2 = [send(presq.at[ki[d]], rqk.at[d], kdev[d]) for d in (1, 2, 3)]
    t_ge.wait_recv()
    preg[...] = ge[...] + preg[...]
    t_ge2 = [send(preg.at[ki[d]], rge.at[d], kdev[d]) for d in (1, 2, 3)]

    for cp in t_gf:
        cp.wait_recv()
    gatt = (
        sgf[j].astype(F32) + rgf[1].astype(F32) + rgf[2].astype(F32) + rgf[3].astype(F32)
    ).astype(BF)
    for h in range(W):
        gow[h] = tn(ga_v[h], gatt).astype(BF).reshape(W, 64, D // W)
    qtr = D // W // 2
    t_po = send(
        gow.at[:, :, :, pl.ds(pl.multiple_of(oth * qtr, qtr), qtr)], preo, partner
    )

    for cp in t_out:
        cp.wait_recv()
    ao[...] = (
        so[:, j].astype(F32) + ro[1].astype(F32) + ro[2].astype(F32) + ro[3].astype(F32)
    ).astype(BF)
    oseg[i] = ao[i]
    t_ao = [send(ao.at[ki[d]], oseg.at[i], kdev[d]) for d in (1, 2, 3)]
    t_po.wait_recv()
    preso[...] = (
        gow[:, :, :, pl.ds(pl.multiple_of(par * qtr, qtr), qtr)].astype(F32)
        + preo[...].astype(F32)
    ).astype(BF)
    t_ow = [send(preso.at[ki[d]], row_.at[d], kdev[d]) for d in (1, 2, 3)]

    for cp in t_m1:
        cp.wait_recv()
    m1 = (snt[:1] + rnt[1, :1] + rnt[2, :1] + rnt[3, :1]) / D
    for cp in t_gn:
        cp.wait_recv()
    xr = xr_v[...].reshape(W, W, 64, T)
    for h in range(W):
        here = (
            sgn[h, j].astype(F32)
            + rgn[1, h].astype(F32)
            + rgn[2, h].astype(F32)
            + rgn[3, h].astype(F32)
        )
        at = pl.ds(pl.multiple_of((h * W + j) * 64, 64), 64)
        ai[h] = (here - xr_v[at, :].astype(F32) * m1).astype(BF)
    iseg[i] = ai[i]
    t_ai = [send(ai.at[ki[d]], iseg.at[i], kdev[d]) for d in (1, 2, 3)]

    for cp in t_vg:
        cp.wait_recv()
    mid_vg[...] = (
        presv[:, i].astype(F32)
        + rvg[1].astype(F32)
        + rvg[2].astype(F32)
        + rvg[3].astype(F32)
    ).astype(BF)
    t_flip = remote(mid_vg, perm_vg, flip)

    @pl.when(i != j)
    def _():
        t_flip.start()

    for cp in t_qk2 + t_ge2:
        cp.wait_recv()
    fin_qk[par] = (
        presq[i].astype(F32)
        + rqk[1].astype(F32)
        + rqk[2].astype(F32)
        + rqk[3].astype(F32)
    ).astype(BF)
    t_fq = send(fin_qk.at[par], fin_qk.at[par], partner)
    fin_e[...] = preg[i] + rge[1] + rge[2] + rge[3]

    for cp in t_ow:
        cp.wait_recv()
    mid_ow[...] = (
        preso[i].astype(F32)
        + row_[1].astype(F32)
        + row_[2].astype(F32)
        + row_[3].astype(F32)
    ).astype(BF)
    fin_ow[par, j] = mid_ow[j]
    t_mo = [send(mid_ow.at[vj[d]], fin_ow.at[par, j], vdev[d]) for d in (1, 2, 3)]

    for cp in t_s0:
        cp.wait_recv()
    sm2[0] = (
        sm0[...].astype(F32)
        + sm1[1].astype(F32)
        + sm1[2].astype(F32)
        + sm1[3].astype(F32)
    ).astype(BF)
    t_s1 = [send(sm2.at[0], sm2.at[d], kdev[d]) for d in (1, 2, 3)]

    for cp in t_fw:
        cp.wait_recv()
    for n in range(3):
        fin_f[par, n] = (
            pres[n, i].astype(F32)
            + rfw[1, n].astype(F32)
            + rfw[2, n].astype(F32)
            + rfw[3, n].astype(F32)
        ).astype(BF)
    t_ff = send(fin_f.at[par], fin_f.at[par], partner)

    for cp in t_s1:
        cp.wait_recv()
    sm3[0] = (
        sm2[0].astype(F32)
        + sm2[1].astype(F32)
        + sm2[2].astype(F32)
        + sm2[3].astype(F32)
    ).astype(BF)
    t_s2 = send(sm3.at[0], sm3.at[1], partner)

    @pl.when(i != j)
    def _():
        t_flip.wait_recv()
        fin_vg[par] = perm_vg[...]

    @pl.when(i == j)
    def _():
        fin_vg[par] = mid_vg[...]

    t_fv = send(fin_vg.at[par], fin_vg.at[par], partner)
    for cp in t_mo:
        cp.wait_recv()
    t_fo = send(fin_ow.at[par], fin_ow.at[par], partner)

    outs = []
    for cp in t_ao:
        cp.wait_recv()
    outs.append(load(oseg, o_out))
    t_fq.wait_recv()
    outs.append(load(fin_qk, o_qk))
    outs.append(load(fin_e, o_ext))
    t_ff.wait_recv()
    outs.append(load(fin_f, o_f))
    t_s2.wait_recv()
    tot = sm3[0].astype(F32) + sm3[1].astype(F32)
    pick[...] = tot
    outs.append(load(pick, o_small))
    for cp in t_ai:
        cp.wait_recv()
    outs.append(load(iseg, o_in))
    t_fv.wait_recv()
    outs.append(load(fin_vg, o_vg))
    t_fo.wait_recv()
    outs.append(load(fin_ow, o_ow))
    for cp in outs:
        cp.wait()
    for cp in sent:
        cp.wait_send()

    @pl.when(i != j)
    def _():
        t_flip.wait_send()


N_REMOTE = 200
N_LOCAL = 40


def layer(n_seq, args):
    tok = args[0]
    rows, D = tok.shape
    T = rows // WAYS
    FB = args[11].shape[0]
    W = WAYS
    VC = W * 64
    half = D // 2
    qtr = D // W // 2

    def sds(shape, dtype=BF):
        return jax.ShapeDtypeStruct(shape, dtype)

    def vm(shape, dtype=BF):
        return pltpu.VMEM(shape, dtype)

    outs = [
        sds((W, 64, T)),
        sds((W, 64, T)),
        sds((2, 3, FB, half)),
        sds((2, 2, 64, half)),
        sds((2, 32, D)),
        sds((32, 128), F32),
        sds((2, W, 64, qtr)),
        sds((32, D), F32),
    ]
    scratch = [
        vm((T, D)),
        vm((T, D)),
        vm((T, D)),
        vm((D, T)),
        vm((128, D)),
        vm((8, D), F32),
        vm((W, 2, 32, D)),
        vm((W, 32, 128)),
        vm((W, 64, D)),
        vm((W, 64, D)),
        vm((W, 64, 128)),
        vm((W, W, 64, D)),
        vm((3, W, FB, D)),
        vm((W, VC + 16, 128)),
        vm((n_seq, VC + 16, 128)),
        vm((W, VC + 16, 128)),
        vm((n_seq, VC + 16, 128)),
        vm((W, T, VC)),
        vm((W, T, VC)),
        vm((W, T, VC)),
        vm((8, T), F32),
        vm((W, 8, T), F32),
        vm((W, W, 64, T)),
        vm((W, W, 64, T)),
        vm((W, T, D // W)),
        vm((W, T, D // W)),
        vm((W, W, 64, T)),
        vm((W, W, 64, T)),
        vm((8, T), F32),
        vm((W, 8, T), F32),
        vm((W, 64, T)),
        vm((W, 64, T)),
        vm((W, 64, T)),
        vm((W, 64, T)),
        vm((3, W, FB, D)),
        vm((3, W, FB, half)),
        vm((3, W, FB, half)),
        vm((W, 3, FB, half)),
        vm((2, 3, FB, half)),
        vm((2, W, 64, D)),
        vm((2, W, 64, half)),
        vm((2, W, 64, half)),
        vm((W, 2, 64, half)),
        vm((2, 64, half)),
        vm((2, 64, half)),
        vm((2, 2, 64, half)),
        vm((W, 2, 32, D)),
        vm((W, 32, D)),
        vm((W, 32, D)),
        vm((W, 32, D)),
        vm((2, 32, D)),
        vm((W, 32, 128), F32),
        vm((W, 32, 128), F32),
        vm((W, 32, 128), F32),
        vm((32, 128), F32),
        vm((W, W, 64, D // W)),
        vm((W, W, 64, qtr)),
        vm((W, W, 64, qtr)),
        vm((W, W, 64, qtr)),
        vm((W, 64, qtr)),
        vm((2, W, 64, qtr)),
        vm((32, D)),
        vm((W, 32, D)),
        vm((W, 32, D)),
        vm((2, 32, D)),
        vm((32, D), F32),
        vm((T, W * FB), F32),
        vm((3, T, VC), F32),
        vm((T, D), F32),
        pltpu.SemaphoreType.DMA((N_REMOTE,)),
        pltpu.SemaphoreType.DMA((N_REMOTE,)),
        pltpu.SemaphoreType.DMA((N_LOCAL,)),
    ]
    return pl.pallas_call(
        functools.partial(layer_kernel, n_seq),
        out_shape=outs,
        in_specs=[pl.BlockSpec(memory_space=pl.ANY)] * len(args),
        out_specs=[pl.BlockSpec(memory_space=pl.ANY)] * len(outs),
        scratch_shapes=scratch,
        compiler_params=pltpu.CompilerParams(
            collective_id=0, has_side_effects=True, vmem_limit_bytes=60 * 2**20
        ),
        name="layer",
    )(*args)


def finish_kernel(
    o_out, o_in, o_f, o_vg, o_qk, o_ow, r_out, r_in, r_fg, r_fu, r_fd, r_v, r_g, r_q, r_k, r_o
):
    T = o_out.shape[2]
    for h in range(WAYS):
        r_out[:, h * T : (h + 1) * T] = o_out[h]
        r_in[:, h * T : (h + 1) * T] = o_in[h]
    half = o_f.shape[3]
    for h in range(2):
        at = slice(h * half, (h + 1) * half)
        for n, r in enumerate((r_fg, r_fu, r_fd)):
            r[:, at] = o_f[h, n].astype(F32)
        for n, r in enumerate((r_v, r_g)):
            r[:, at] = o_vg[h, n].astype(F32)
    r_q[...] = o_qk[0].astype(F32)
    r_k[...] = o_qk[1].astype(F32)
    qtr = o_ow.shape[3]
    for z in range(WAYS):
        for h in range(2):
            at = (2 * z + h) * qtr
            r_o[:, at : at + qtr] = o_ow[h, z].astype(F32)


def finish(parts):
    rows = parts[0].shape[0] * parts[0].shape[2]
    D = 2 * parts[2].shape[3]
    FB = parts[2].shape[2]

    def sds(shape, dtype=F32):
        return jax.ShapeDtypeStruct(shape, dtype)

    outs = [
        sds((64, rows), BF),
        sds((64, rows), BF),
        sds((FB, D)),
        sds((FB, D)),
        sds((FB, D)),
        sds((64, D)),
        sds((64, D)),
        sds((32, D)),
        sds((32, D)),
        sds((64, D)),
    ]
    return pl.pallas_call(
        finish_kernel,
        out_shape=outs,
        in_specs=[pl.BlockSpec(memory_space=pltpu.VMEM)] * len(parts),
        out_specs=[pl.BlockSpec(memory_space=pltpu.VMEM)] * len(outs),
        compiler_params=pltpu.CompilerParams(vmem_limit_bytes=32 * 2**20),
        name="finish",
    )(*parts)


def shards(
    n_seq,
    tokens,
    norm_gain,
    query_weight,
    key_weight,
    value_weight,
    gate_weight,
    decay_down,
    decay_up,
    decay_bias,
    group_gain,
    out_weight,
    ffn_gain,
    ffn_gate,
    ffn_up,
    ffn_down,
    cotangent,
):
    D = tokens.shape[1]
    i = lax.axis_index("kax")
    j = lax.axis_index("vax")
    pair = i * WAYS + j
    gains = jnp.concatenate(
        [norm_gain[None], ffn_gain[None], jnp.zeros((6, D), BF)], axis=0
    ).astype(F32)
    up_here = lax.dynamic_index_in_dim(decay_up, j, 1, False).T
    bias_here = lax.dynamic_index_in_dim(decay_bias, j, 0, False)[:, None]
    ext = jnp.concatenate(
        [up_here, bias_here, jnp.zeros((32, 128 - up_here.shape[1] - 1), BF)], axis=1
    )
    gge = jnp.broadcast_to(group_gain[:, None], (64, 128))
    parts = layer(
        n_seq,
        (
            tokens,
            cotangent,
            gains,
            query_weight.transpose(1, 2, 0),
            key_weight.transpose(1, 2, 0),
            ext,
            value_weight.transpose(1, 2, 0),
            gate_weight.transpose(1, 2, 0),
            gge,
            decay_down.T,
            out_weight[0],
            ffn_gate.T,
            ffn_up.T,
            ffn_down,
        ),
    )
    o_out, o_in, o_f, o_vg, o_qk, o_ext, o_ow, o_small = parts
    if n_seq > 2:

        def over_pairs(a):
            return jnp.sum(lax.all_gather(a, "seq")[::2].astype(F32), axis=0).astype(a.dtype)

        o_f, o_vg, o_qk, o_ext, o_ow, o_small = (
            over_pairs(a) for a in (o_f, o_vg, o_qk, o_ext, o_ow, o_small)
        )
    r_out, r_in, r_fg, r_fu, r_fd, r_v, r_g, r_q, r_k, r_o = finish(
        (o_out, o_in, o_f, o_vg, o_qk, o_ow)
    )
    slab = D // (WAYS * WAYS)
    norm_gain_grad = lax.dynamic_slice(o_small, (16, pair * slab), (1, slab))[0]
    ffn_gain_grad = lax.dynamic_slice(o_small, (17, pair * slab), (1, slab))[0]
    group_gain_grad = lax.dynamic_slice(o_small, (18, j * 64), (1, 64))[0]
    decay_down_grad = lax.dynamic_slice(o_small, (pair, 0), (1, D)).T
    decay_up_grad = o_ext[:, :16].T[:, None, :]
    decay_bias_grad = o_ext[:, 16][None, :]
    return (
        r_out.T,
        r_in.T,
        norm_gain_grad,
        r_q.T[:, None, :],
        r_k.T[:, None, :],
        r_v.T[:, None, :],
        r_g.T[:, None, :],
        decay_down_grad,
        decay_up_grad,
        decay_bias_grad,
        group_gain_grad,
        r_o[None],
        ffn_gain_grad,
        r_fg.T,
        r_fu.T,
        r_fd,
    )


def solution(mesh):
    in_specs = (
        P("seq", None),
        P(),
        P(None, None, "kax"),
        P(None, None, "kax"),
        P(None, None, "vax"),
        P(None, None, "vax"),
        P(),
        P(None, None, "kax"),
        P(None, "kax"),
        P("vax"),
        P("kax", "vax", None),
        P(),
        P(None, ("kax", "vax")),
        P(None, ("kax", "vax")),
        P(("kax", "vax"), None),
        P("seq", None),
    )
    out_specs = (
        P("seq", ("kax", "vax")),
        P("seq", ("kax", "vax")),
        P(("kax", "vax")),
        P(None, "vax", "kax"),
        P(None, "vax", "kax"),
        P(None, "kax", "vax"),
        P(None, "kax", "vax"),
        P(None, ("kax", "vax")),
        P(None, "vax", "kax"),
        P("vax", "kax"),
        P("vax"),
        P("kax", "vax", None),
        P(("kax", "vax")),
        P(None, ("kax", "vax")),
        P(None, ("kax", "vax")),
        P(("kax", "vax"), None),
    )
    return jax.shard_map(
        functools.partial(shards, mesh.shape["seq"]),
        mesh=mesh,
        in_specs=in_specs,
        out_specs=out_specs,
        check_vma=False,
    )
```

time: 998 us -> 154 us (0.15); the launches traced: 984 us -> 154 us
  waiting for transfers between devices: 574 us -> 0 us
  local copies, waits for them, and re-layouts: 155 us -> 15.1 us
  Pallas kernels: 0 us -> 136 us
  matrix products: 103 us -> 0 us
  other arithmetic: 81.2 us -> 1.37 us
  blocking collectives: 52.8 us -> 0 us
  between operations: 16.3 us -> 0.69 us
    reduce_scatter x6 -> x0, waiting for transfers between devices: 260 us -> none  [the longest x1 83.1 us: shards(): lax.psum_scatter(normed_part.astype(jnp.bfloat16), ('kax', 'vax'), scatte...]
    pallas_call x0 -> x2, Pallas kernels: none -> 136 us  [the longest x1 135 us: layer(): pl.pallas_call(functools.partial(layer_kernel, n_seq), out_shape=outs, in...]
    unnamed x15 -> x0, waiting for transfers between devices: 127 us -> none
    psum x2 -> x0, waiting for transfers between devices: 127 us -> none  [the longest x1 107 us: shards(): lax.psum(ffn_in_part.astype(jnp.bfloat16), ('kax', 'vax'))]
    dot_general x43 -> x0, matrix products: 103 us -> none  [the longest x13 44.5 us: highest(): return jnp.einsum(form, left, right, precision=lax.Precision.HIGHEST)]
    pad x24 -> x0, local copies, waits for them, and re-layouts: 86.2 us -> none  [the longest x12 43.1 us: shards(): lax.associative_scan(compose, (span_decay[::-1], state_weight[::-1]), axi...]
    all_gather x1 -> x0, waiting for transfers between devices: 58.9 us -> none  [shards(): lax.all_gather(resid_slab.astype(jnp.bfloat16), ('kax', 'vax'), axis=1, t...]
    convert_element_type x27 -> x1, other arithmetic: 26.2 us -> 0.69 us  [shards(): gains = jnp.concatenate([norm_gain[None], ffn_gain[None], jnp.zeros((6, D...]
  transfers between devices with their start and end apart: 12 -> 0, of which waited for: 11 -> 0; matrix products, arithmetic and copies ran while one was open for 9% -> 0% of each run, Pallas kernels for 0% -> 0%
where the time goes in v1:
time: 154 us
  Pallas kernels  136 us (88%)
  local copies, waits for them, and re-layouts  15.1 us (10%)
    pallas_call x1, Pallas kernels, layer(): pl.pallas_call(functools.partial(layer_kernel, n_seq), out_shape=outs, in...  135 us
    unnamed x15, local copies, waits for them, and re-layouts  6.48 us

profile of v1, /device:TPU:0, one launch (start us, length us, event | category | flops | bytes accessed | tf_op | source)
XLA Modules:
  0.0 153.7 jit_solution(2419963554219859184)
XLA Ops:
  0.6 0.0 copy-start
  0.7 0.7 fusion
  1.4 0.1 pad.2.clone
  1.4 0.1 pad.5.clone
  1.5 0.7 broadcast_in_dim.39
  2.2 0.7 broadcast_in_dim.40
  2.9 0.1 copy.35
  3.0 0.1 copy.36
  3.1 0.7 maximum_maximum_fusion.ext
  3.8 1.3 broadcast_in_dim.44.gge
  5.1 0.7 maximum_convert_fusion.gains
  5.8 134.7 %layer.1 = (bf16[4,64,256]{2,1,0:T(8,128)(2,1)}, bf16[4,64,256]{2,1,0:T(8,128)(2,1)}, bf16[2,3,176,512]{3,2,1,0:T(8,128)(2,1)}, bf16[2,2,64,512]{3,2,1,0:T(8,128...) custom-call(bf16[1024,1024]{1,0:T(8,128)(2,1)} %tok.1, ...), custom_call_target="tpu_custom_call" | custom-call | tf_op jit(solution)/shard_map/layer/pallas_call | solution.py:816
  140.5 1.4 slice_reduce_fusion
  141.9 0.7 slice_bitcast_fusion
  142.7 0.7 copy.37
  143.3 1.4 dynamic-slice_bitcast_fusion.1
  144.7 1.4 dynamic-slice_bitcast_fusion
  146.1 1.2 copy-done.1
  147.3 0.9 copy-done.2
  148.3 0.9 copy-done.3
  149.2 0.9 copy-done.4
  150.1 0.9 copy-done.5
  151.0 0.9 copy-done.6
  151.9 1.8 %finish.1 = (bf16[64,1024]{1,0:T(8,128)(2,1)}, bf16[64,1024]{1,0:T(8,128)(2,1)}, f32[176,1024]{1,0:T(8,128)}, f32[176,1024]{1,0:T(8,128)}, f32[176,1024]{1,0:T(8...) custom-call(bf16[4,64,256]{2,1,0:T(8,128)(2,1)S(1)} %copy-done.3, ...), custom_call_target="tpu_custom_call" | custom-call | tf_op jit(solution)/shard_map/finish/pallas_call | solution.py:872
  (10 shorter events, 0.0 us)
Async XLA Ops:
  0.6 2.3 %copy-start = (bf16[16,4,32]{2,1,0:T(4,128)(2,1)S(1)}, bf16[16,4,32]{2,1,0:T(4,128)(2,1)}, u32[]{:S(2)}) copy-start(bf16[16,4,32]{2,1,0:T(4,128)(2,1)} %param.23) | copy-start | bytes 12292
  146.1 1.2 copy-start.1
  147.3 0.9 copy-start.2
  148.3 0.9 copy-start.3
  149.2 0.9 copy-start.4
  150.1 0.9 copy-start.5
  151.0 0.9 copy-start.6

commit v2 on v1

v2 whole, which is shorter than its diff:
```python
import functools

import jax
import jax.numpy as jnp
from jax import lax
from jax.experimental import pallas as pl
from jax.experimental.pallas import tpu as pltpu
from jax.sharding import PartitionSpec as P

MESH = pl.DeviceIdType.MESH
BF = jnp.bfloat16
F32 = jnp.float32
CB = 128
WAYS = 4
EPS = 1e-06
HIGH = lax.Precision.HIGHEST


def nn(a, b, precision=None):
    return lax.dot_general(
        a, b, (((1,), (0,)), ((), ())), precision=precision, preferred_element_type=F32
    )


def nt(a, b, precision=None):
    return lax.dot_general(
        a, b, (((1,), (1,)), ((), ())), precision=precision, preferred_element_type=F32
    )


def tn(a, b, precision=None):
    return lax.dot_general(
        a, b, (((0,), (0,)), ((), ())), precision=precision, preferred_element_type=F32
    )


def xor(index, d):
    if d == 1:
        return index + 1 - 2 * lax.rem(index, 2)
    if d == 2:
        return lax.rem(index + 2, 4)
    return 3 - index


def as_row(column):
    return jnp.broadcast_to(column, (column.shape[0], 128)).T[:8]


def as_column(row):
    return jnp.broadcast_to(row[:1], (128, row.shape[1])).T[:, :1]


def flat_row(block):
    return jnp.concatenate([block[r : r + 1] for r in range(block.shape[0])], axis=1)


def lanes(block):
    return jnp.concatenate([block[n] for n in range(block.shape[0])], axis=1)


def total(own, got):
    out = own.astype(F32)
    for d in (1, 2, 3):
        out = out + got[d].astype(F32)
    return out


def layer_kernel(
    n_seq,
    tok,
    cot,
    ng,
    ffg,
    dup,
    dbi,
    ggn,
    wq,
    wk,
    wv,
    wg,
    dd,
    wo,
    fg,
    fu,
    fd,
    o_out,
    o_in,
    o_f,
    o_d,
    o_vg,
    o_qk,
    o_ext,
    o_ow,
    o_small,
    x_v,
    c_v,
    x_all,
    c_all,
    n_all,
    n_v,
    xr_v,
    dd_v,
    ng_v,
    ffg_v,
    dup_v,
    dbi_v,
    ggn_v,
    sq_v,
    gain_v,
    qk_v,
    ext_v,
    v_v,
    g_v,
    gge_v,
    o_v,
    f_v,
    st_v,
    tt_v,
    bst_v,
    btt_v,
    ga_v,
    sgg,
    rgg,
    sst,
    rst,
    so,
    ro,
    sgn,
    rgn,
    ao,
    oseg,
    ai,
    iseg,
    hd,
    hseg,
    gw,
    pre,
    pres,
    rfw,
    fin_f,
    dsum,
    gow,
    preo,
    preso,
    rowk,
    mid_o,
    rowz,
    fin_ow,
    vz,
    zvg,
    kvg,
    vgsum,
    qka,
    kqa,
    qksum,
    esum,
    sm0,
    sm1,
    sm2,
    sm3,
    sm4,
    pick,
    small_v,
    gh_v,
    act_v,
    p_v,
    ss,
    rs,
    ls,
):
    s = lax.axis_index("seq")
    i = lax.axis_index("kax")
    j = lax.axis_index("vax")
    par = lax.rem(s, 2)
    oth = 1 - par
    T, D = x_v.shape
    rows = x_all.shape[0]
    FB = f_v.shape[2]
    half = D // 2
    W = WAYS
    DIRS = (1, 2, 3)
    mine = pl.ds(pl.multiple_of(par * half, half), half)
    other = pl.ds(pl.multiple_of(oth * half, half), half)
    partner = {"seq": s + 1 - 2 * par}
    kdev = [None] + [{"kax": xor(i, d)} for d in DIRS]
    vdev = [None] + [{"vax": xor(j, d)} for d in DIRS]
    ki = [None] + [xor(i, d) for d in DIRS]
    vj = [None] + [xor(j, d) for d in DIRS]
    seqdev = [{"seq": lax.rem(s + e, n_seq)} for e in range(1, n_seq)]

    count = [0, 0]
    sent = []

    def remote(src, dst, dev):
        n = count[0]
        count[0] += 1
        return pltpu.make_async_remote_copy(
            src_ref=src,
            dst_ref=dst,
            send_sem=ss.at[n],
            recv_sem=rs.at[n],
            device_id=dev,
            device_id_type=MESH,
        )

    def send(src, dst, dev):
        cp = remote(src, dst, dev)
        cp.start()
        sent.append(cp)
        return cp

    def load(src, dst):
        n = count[1]
        count[1] += 1
        cp = pltpu.make_async_copy(src, dst, ls.at[n])
        cp.start()
        return cp

    def left(cp):
        cp.wait_send()
        sent[:] = [one for one in sent if one is not cp]

    def arrived(copies):
        for cp in copies:
            cp.wait_recv()

    def here(copies):
        for cp in copies:
            cp.wait()

    l_small = [load(dup, dup_v), load(dbi, dbi_v), load(ggn, ggn_v)]
    l_qk = [load(wq.at[j], qk_v.at[i, 0]), load(wk.at[j], qk_v.at[i, 1])]
    segment = pl.ds(pl.multiple_of(i * T, T), T)
    l_x = [load(tok.at[segment], x_v), load(ng, ng_v), load(ffg, ffg_v)]
    l_dd = load(dd, dd_v.at[pl.ds(0, 16)])
    l_v = load(wv.at[j], v_v.at[j])
    l_g = load(wg.at[j], g_v.at[j])
    l_c = load(cot.at[segment], c_v)
    l_f = [load(fg, f_v.at[0, i]), load(fu, f_v.at[1, i]), load(fd, f_v.at[2, i])]
    l_o = load(wo, o_v.at[i, j])
    l_xa = load(tok, x_all)
    l_ca = load(cot, c_all)

    barrier = pltpu.get_barrier_semaphore()
    for dev in kdev[1:] + vdev[1:] + seqdev:
        pl.semaphore_signal(barrier, inc=1, device_id=dev, device_id_type=MESH)

    dd_v[16:, :] = jnp.zeros((dd_v.shape[0] - 16, D), BF)
    here(l_small)
    head3 = lax.broadcasted_iota(jnp.int32, (16, W, 32), 1)
    head2 = lax.broadcasted_iota(jnp.int32, (W, 32), 0)
    sq_v[...] = jnp.zeros_like(sq_v)
    sq_v[0:16, 0:32] = jnp.sum(jnp.where(head3 == j, dup_v[...].astype(F32), 0.0), axis=1)
    sq_v[16:17, 0:32] = jnp.sum(
        jnp.where(head2 == j, dbi_v[...].astype(F32), 0.0), axis=0, keepdims=True
    )
    ext_v[i] = sq_v[...].T[:32].astype(BF)
    sq_v[...] = jnp.zeros_like(sq_v)
    sq_v[0:8, 0:64] = jnp.broadcast_to(ggn_v[...].astype(F32), (8, 64))
    gge_v[j] = sq_v[...].T[:64].astype(BF)

    pl.semaphore_wait(barrier, 6 + len(seqdev))

    here(l_qk)
    t_qk = [None] + [send(qk_v.at[i, par], qk_v.at[i, par], kdev[d]) for d in DIRS]
    t_v = [None] + [send(wv.at[vj[d], :, mine], v_v.at[j, :, mine], vdev[d]) for d in DIRS]
    t_ext = [send(ext_v.at[i], ext_v.at[i], kdev[d]) for d in DIRS]
    low = pl.ds(0, 32)
    high = pl.ds(32, 32)
    t_oa = [None] + [
        send(wo.at[low, mine], o_v.at[i, j, low, mine], vdev[d]) for d in DIRS
    ]
    t_ob = [None] + [
        send(wo.at[high, mine], o_v.at[i, j, high, mine], kdev[d]) for d in DIRS
    ]
    cut = FB // 32 * 16
    weights = (fg, fu, fd)
    pieces = [(2, 0, cut), (2, cut, FB - cut), (0, 0, FB), (1, 0, FB)]

    def send_piece(piece):
        n, first, size = piece
        at = pl.ds(first, size)
        return [None] + [
            send(weights[n].at[at, mine], f_v.at[n, i, at, mine], kdev[d]) for d in DIRS
        ]

    def pass_piece(piece, copies):
        n, first, size = piece
        at = pl.ds(first, size)
        moves = []
        for d in DIRS:
            copies[d].wait_recv()
            view = f_v.at[n, ki[d], at, mine]
            moves.append(send(view, view, partner))
        return moves

    t_f = [send_piece(pieces[0])]
    t_g = [None] + [send(wg.at[vj[d], :, mine], g_v.at[j, :, mine], vdev[d]) for d in DIRS]
    t_gge = [send(gge_v.at[j], gge_v.at[j], vdev[d]) for d in DIRS]

    here(l_x)
    x = x_v[...].astype(F32)
    g1 = flat_row(ng_v[...].astype(F32))
    g3 = flat_row(ffg_v[...].astype(F32))
    r1 = lax.rsqrt(jnp.sum(x * x, axis=1, keepdims=True) / D + EPS)
    n_v[...] = (x * r1 * g1).astype(BF)
    l_dd.wait()
    lane = lax.broadcasted_iota(jnp.int32, (T, 128), 1)
    lrp = jnp.where(lane == 16, 1.0, nt(n_v[...], dd_v[...]))

    f_qk = []
    for d in DIRS:
        t_qk[d].wait_recv()
        f_qk.append(send(qk_v.at[ki[d], par], qk_v.at[ki[d], par], partner))
    arrived(t_ext)
    arrived(f_qk)
    normed = n_v[...]
    wq_all = qk_v[:, 0].reshape(W * 32, D)
    wk_all = qk_v[:, 1].reshape(W * 32, D)
    ext_all = ext_v[...].reshape(W * 32, 128)
    scale = 128.0 ** (-0.5)
    q = nt(normed, wq_all) * scale
    k = nt(normed, wk_all)
    arg = nt(lrp, ext_all.astype(F32), HIGH)
    rates = (jnp.minimum(arg, 0.0) - jnp.log1p(jnp.exp(-jnp.abs(arg)))) / 16.0
    row_id = lax.broadcasted_iota(jnp.int32, (CB, CB), 0)
    col_id = lax.broadcasted_iota(jnp.int32, (CB, CB), 1)
    causal = row_id >= col_id
    tri = jnp.where(causal, 1.0, 0.0)
    nblk = T // CB
    blk = [slice(c * CB, (c + 1) * CB) for c in range(nblk)]
    e1, e2, em, el, dec, qd, kd, qi, ke, score = [], [], [], [], [], [], [], [], [], []
    for c in range(nblk):
        cum = nn(tri, rates[blk[c]], HIGH)
        mid = cum[CB // 2 - 1 : CB // 2]
        last = cum[CB - 1 : CB]
        e1.append(jnp.exp(cum - mid))
        e2.append(jnp.exp(mid - cum))
        em.append(jnp.exp(mid))
        el.append(jnp.exp(last - mid))
        dec.append(jnp.exp(last))
        a = q[blk[c]] * e1[c]
        b = k[blk[c]] * e2[c]
        qd.append(a.astype(BF))
        kd.append(b.astype(BF))
        qi.append((a * em[c]).astype(BF))
        ke.append((b * el[c]).astype(BF))
        score.append(jnp.where(causal, nt(qd[c], kd[c]), 0.0).astype(BF))

    l_v.wait()
    f_vv = []
    for d in DIRS:
        t_v[d].wait_recv()
        f_vv.append(send(v_v.at[vj[d], :, mine], v_v.at[vj[d], :, mine], partner))
    arrived(f_vv)
    wv_all = v_v[...].reshape(W * 64, D)
    v = nt(normed, wv_all).astype(BF)
    up = [tn(v[blk[c]], ke[c]) for c in range(nblk)]
    loc = up[0]
    locd = dec[0]
    for c in range(1, nblk):
        loc = loc * dec[c] + up[c]
        locd = locd * dec[c]
    VC = loc.shape[0]
    st_v[i, :VC] = loc.astype(BF)
    st_v[i, VC:] = jnp.broadcast_to(locd, (16, 128)).astype(BF)
    t_st = [send(st_v.at[i], st_v.at[i], kdev[d]) for d in DIRS]
    for piece in pieces[1:]:
        t_f.append(send_piece(piece))
    mixed = [nn(score[c], v[blk[c]]) for c in range(nblk)]

    f_o = []
    l_o.wait()
    for d in DIRS:
        t_oa[d].wait_recv()
        view = o_v.at[i, vj[d], low, mine]
        f_o.append(send(view, view, partner))
    t_oa2 = [None] + [
        send(o_v.at[i, :, low, mine], o_v.at[i, :, low, mine], kdev[d]) for d in DIRS
    ]
    for d in DIRS:
        t_ob[d].wait_recv()
        view = o_v.at[ki[d], j, high, mine]
        f_o.append(send(view, view, partner))
    f_g = []
    l_g.wait()
    for d in DIRS:
        t_g[d].wait_recv()
        f_g.append(send(g_v.at[vj[d], :, mine], g_v.at[vj[d], :, mine], partner))
    arrived(f_g)
    arrived(t_gge)
    wg_all = g_v[...].reshape(W * 64, D)
    gate = nt(normed, wg_all)
    gg = gge_v[...].astype(F32).reshape(W * 64, 128).T[:1]
    sig = 1.0 / (1.0 + jnp.exp(-gate))
    act = gate * sig
    act_v[0] = act
    act_v[1] = sig + act * (1.0 - sig)

    def entering(slots, totals, back):
        order = range(W - 1, -1, -1) if back else range(W)
        pre_s = jnp.zeros((VC, 128), F32)
        pre_d = jnp.ones((1, 128), F32)
        tot_s = jnp.zeros((VC, 128), F32)
        tot_d = jnp.ones((1, 128), F32)
        for other_i in order:
            one_s = slots[other_i, :VC].astype(F32)
            one_d = slots[other_i, VC : VC + 1].astype(F32)
            use = (other_i > i) if back else (other_i < i)
            pre_s = jnp.where(use, pre_s * one_d + one_s, pre_s)
            pre_d = jnp.where(use, pre_d * one_d, pre_d)
            tot_s = tot_s * one_d + one_s
            tot_d = tot_d * one_d
        totals[s, :VC] = tot_s.astype(BF)
        totals[s, VC:] = jnp.broadcast_to(tot_d, (16, 128)).astype(BF)
        arrived([send(totals.at[s], totals.at[s], dev) for dev in seqdev])
        order = range(n_seq - 1, -1, -1) if back else range(n_seq)
        far = jnp.zeros((VC, 128), F32)
        for other_s in order:
            one_s = totals[other_s, :VC].astype(F32)
            one_d = totals[other_s, VC : VC + 1].astype(F32)
            use = (other_s > s) if back else (other_s < s)
            far = jnp.where(use, far * one_d + one_s, far)
        return pre_s + pre_d * far

    arrived(t_st)
    start = [entering(st_v, tt_v, False)]
    for c in range(nblk):
        start.append(start[c] * dec[c] + up[c])
    start_low = [a.astype(BF) for a in start]
    for c in range(nblk):
        mixed[c] = mixed[c] + nt(qi[c], start_low[c])
    mix = jnp.concatenate(mixed, axis=0)
    r2 = lax.rsqrt(jnp.sum(mix * mix, axis=1, keepdims=True) / VC + EPS)
    normal = mix * r2
    ga_v[j] = (normal * gg * act_v[0]).astype(BF)
    act_v[2] = normal
    t_ga = [send(ga_v.at[j], ga_v.at[j], vdev[d]) for d in DIRS]
    t_ob2 = [None] + [
        send(o_v.at[:, j, high, mine], o_v.at[:, j, high, mine], vdev[d]) for d in DIRS
    ]

    here([l_xa, l_ca])
    for part in range(rows // T):
        at = pl.ds(part * T, T)
        xa = x_all[at, :].astype(F32)
        ra = lax.rsqrt(jnp.sum(xa * xa, axis=1, keepdims=True) / D + EPS)
        n_all[at, :] = (xa * ra * g1).astype(BF)
    xr_v[...] = (x * (r1 * r1 * r1)).astype(BF).T
    here(l_f + [l_c])
    f_f = []
    for piece, copies in zip(pieces[:2], t_f[:2]):
        f_f += pass_piece(piece, copies)
    arrived(f_f)
    dn = f_v[2].reshape(W * FB, D)
    gh_v[...] = nt(c_v[...], dn)
    f_f = []
    for piece, copies in zip(pieces[2:], t_f[2:]):
        f_f += pass_piece(piece, copies)
    for d in DIRS:
        t_oa2[d].wait_recv()
        view = o_v.at[ki[d], :, low, mine]
        f_o.append(send(view, view, partner))
    arrived(t_ga)
    for d in DIRS:
        t_ob2[d].wait_recv()
        view = o_v.at[:, vj[d], high, mine]
        f_o.append(send(view, view, partner))
    arrived(f_o)
    att = nn(ga_v[0], o_v[0].reshape(W * 64, D))
    for h in range(1, W):
        att = att + nn(ga_v[h], o_v[h].reshape(W * 64, D))
    resid = x_v[...].astype(F32) + att
    r3 = lax.rsqrt(jnp.sum(resid * resid, axis=1, keepdims=True) / D + EPS)
    fin = (resid * r3 * g3).astype(BF)
    arrived(f_f)

    gT = f_v[0].reshape(W * FB, D)
    uT = f_v[1].reshape(W * FB, D)
    gval = nt(fin, gT)
    uval = nt(fin, uT)
    fsig = 1.0 / (1.0 + jnp.exp(-gval))
    fact = gval * fsig
    hid = (fact * uval).astype(BF)
    gh = gh_v[...]
    gup = (gh * fact).astype(BF)
    ggate = (gh * uval * (fsig + fact * (1.0 - fsig))).astype(BF)
    part = nn(ggate, gT) + nn(gup, uT)
    p_v[...] = part
    sst[...] = as_row(jnp.sum(resid * g3 * part, axis=1, keepdims=True))
    t_m3 = [send(sst, rst.at[d], vdev[d]) for d in DIRS]
    ggp = nt((part * g3).astype(BF), o_v[...].reshape(W * W * 64, D))
    for h in range(W):
        sgg[h] = ggp[:, h * VC : (h + 1) * VC].astype(BF)
    t_gg = [send(sgg.at[vj[d]], rgg.at[d], vdev[d]) for d in DIRS]
    hd[...] = hid.T.reshape(W, FB, T)
    t_hd = [send(hd.at[ki[d]], hseg.at[i], kdev[d]) for d in DIRS]
    hseg[i] = hd[i]

    t_pre = []
    for n, grad in enumerate((ggate, gup)):
        gw[n] = tn(grad, fin).astype(BF).reshape(W, FB, D)
        t_pre.append(send(gw.at[n, :, :, other], pre.at[n], partner))

    feature = lax.broadcasted_iota(jnp.int32, (1, D), 1)
    own_slab = jnp.where(lax.rem(feature // 64, W) == j, 1.0, 0.0)
    own_run = jnp.where(feature // (D // W) == j, 1.0, 0.0)
    so[...] = (nn(hid, dn) + own_slab * resid).astype(BF).T.reshape(W, W, 64, T)
    pair01 = pl.ds(0, W // 2)
    pair23 = pl.ds(W // 2, W // 2)
    t_out = [send(so.at[pair01, vj[d]], ro.at[d, pair01], vdev[d]) for d in DIRS]
    ffn_gain = jnp.sum(part * resid * r3, axis=0, keepdims=True)

    def settle(n):
        t_pre[n].wait_recv()
        pres[n] = (gw[n, :, :, mine].astype(F32) + pre[n].astype(F32)).astype(BF)
        return [send(pres.at[n, ki[d]], rfw.at[n, d], kdev[d]) for d in DIRS]

    t_fw = settle(0)

    arrived(t_m3)
    m3 = as_column(sst[...] + rst[1] + rst[2] + rst[3]) / D
    base = c_v[...].astype(F32) - resid * (r3 * r3 * r3 * m3)
    direct = nt(base.astype(BF), o_v[j].reshape(W * 64, D))
    full = p_v[...] * (g3 * r3)
    mixed_in = (full + own_run * base).astype(BF)
    for h in range(W):
        gow[h] = tn(ga_v[h], mixed_in).astype(BF)
    t_po = send(gow.at[:, :, other], preo, partner)
    arrived(t_gg)

    ggs = total(sgg[j], rgg)
    ggrad = direct + r3 * ggs
    act = act_v[0]
    normal = act_v[2]
    dgate = (ggrad * normal * gg * act_v[1]).astype(BF)
    gs = ggrad * act
    group = jnp.sum(gs * normal, axis=0, keepdims=True)
    gnm = gs * gg
    gmix = (r2 * (gnm - normal * (jnp.sum(normal * gnm, axis=1, keepdims=True) / VC))).astype(BF)

    qst = [tn(gmix[blk[c]], qi[c]) for c in range(nblk)]
    bloc = qst[nblk - 1]
    for c in range(nblk - 2, -1, -1):
        bloc = bloc * dec[c] + qst[c]
    bst_v[i, :VC] = bloc.astype(BF)
    bst_v[i, VC:] = jnp.broadcast_to(locd, (16, 128)).astype(BF)
    t_bst = [send(bst_v.at[i], bst_v.at[i], kdev[d]) for d in DIRS]
    vz[1] = dgate.T.reshape(W, 64, T)
    t_gz = [send(vz.at[1, vj[d]], zvg.at[1, j], vdev[d]) for d in DIRS]
    t_fw += settle(1)
    dscore, dq_in, dk_in, dv_in = [], [], [], []
    for c in range(nblk):
        ds = jnp.where(causal, nt(gmix[blk[c]], v[blk[c]]), 0.0).astype(BF)
        dq_in.append(nn(ds, kd[c]) + em[c] * nn(gmix[blk[c]], start_low[c]))
        dk_in.append(tn(ds, qd[c]))
        dv_in.append(tn(score[c], gmix[blk[c]]))
    t_po.wait_recv()
    preso[...] = (gow[:, :, mine].astype(F32) + preo[...].astype(F32)).astype(BF)
    arrived(t_bst)
    after = [None] * nblk
    after[nblk - 1] = entering(bst_v, btt_v, True)
    for c in range(nblk - 2, -1, -1):
        after[c] = after[c + 1] * dec[c + 1] + qst[c + 1]

    ql, kl, vl, ga = [], [], [], []
    for c in range(nblk):
        low_after = after[c].astype(BF)
        dq = e1[c] * dq_in[c]
        dk = e2[c] * (dk_in[c] + el[c] * nn(v[blk[c]], low_after))
        dv = dv_in[c] + nt(ke[c], low_after)
        gc = q[blk[c]] * dq - k[blk[c]] * dk
        extra = jnp.sum(after[c] * start[c + 1], axis=0, keepdims=True)
        gc = jnp.where(row_id == CB - 1, gc + extra, gc)
        gr = tn(tri, gc, HIGH)
        ga.append(gr / (1.0 + jnp.exp(arg[blk[c]])) / 16.0)
        ql.append((dq * scale).astype(BF))
        kl.append(dk.astype(BF))
        vl.append(dv.astype(BF))
    ql = jnp.concatenate(ql, axis=0)
    kl = jnp.concatenate(kl, axis=0)
    vl = jnp.concatenate(vl, axis=0)
    ga = jnp.concatenate(ga, axis=0).astype(BF)
    vz[0] = vl.T.reshape(W, 64, T)
    t_vz = [send(vz.at[0, vj[d]], zvg.at[0, j], vdev[d]) for d in DIRS]
    qka[:, 0] = ql.T.reshape(W, 32, T)
    qka[:, 1] = kl.T.reshape(W, 32, T)
    qka[:, 2] = ga.T.reshape(W, 32, T)
    t_qa = [send(qka.at[ki[d]], kqa.at[i], kdev[d]) for d in DIRS]
    glr = nn(ga, ext_all).astype(BF)
    gn = nn(ql, wq_all) + nn(kl, wk_all) + nn(vl, wv_all) + nn(dgate, wg_all) + nn(glr, dd_v[...])
    x = x_v[...].astype(F32)
    gnx = gn * x
    norm_gain = jnp.sum(gnx * r1, axis=0, keepdims=True)
    m1p = as_row(jnp.sum(gnx * g1, axis=1, keepdims=True))[:1]
    small = tn(glr, normed)[:16]
    rid = lax.broadcasted_iota(jnp.int32, (16, T), 0)
    for h in range(W):
        at = slice(h * T, (h + 1) * T)
        sm0[h, 0:16] = small[:, at].astype(BF)
        rest = jnp.where(rid == 0, norm_gain[:, at], 0.0)
        rest = jnp.where(rid == 1, ffn_gain[:, at], rest)
        rest = jnp.where(rid == 3, m1p, rest)
        if h == 0:
            rest = jnp.where(rid == 2, group, rest)
        sm0[h, 16:32] = rest.astype(BF)
    t_s0 = [send(sm0.at[vj[d]], sm1.at[d], vdev[d]) for d in DIRS]
    whole = gn * (r1 * g1) + full + own_slab * base
    sgn[...] = whole.astype(BF).T.reshape(W, W, 64, T)
    t_gn = [send(sgn.at[:, vj[d]], rgn.at[d], vdev[d]) for d in DIRS]
    t_out2 = [send(so.at[pair23, vj[d]], ro.at[d, pair23], vdev[d]) for d in DIRS]
    t_ow = [send(preso.at[ki[d]], rowk.at[d], kdev[d]) for d in DIRS]

    arrived(t_hd)
    dsum[0] = nn(lanes(hseg[...]), c_all[...]).astype(BF)
    t_ds = send(dsum.at[0], dsum.at[1], partner)

    arrived(t_gz)
    zvg[1, j] = vz[1, j]
    t_gk = [send(zvg.at[1, ki[d]], kvg.at[1, i], kdev[d]) for d in DIRS]
    kvg[1, i] = zvg[1, i]

    arrived(t_s0)
    sm2[0] = total(sm0[j], sm1).astype(BF)
    m1 = (
        sm0[0, 19:20].astype(F32)
        + sm1[1, 19:20].astype(F32)
        + sm1[2, 19:20].astype(F32)
        + sm1[3, 19:20].astype(F32)
    ) / D
    t_s1 = [send(sm2.at[0], sm2.at[d], kdev[d]) for d in DIRS]
    arrived(t_vz)
    zvg[0, j] = vz[0, j]
    t_vk = [send(zvg.at[0, ki[d]], kvg.at[0, i], kdev[d]) for d in DIRS]
    kvg[0, i] = zvg[0, i]

    arrived(t_qa)
    kqa[i] = qka[i]
    nall = n_all[...]
    for n in range(2):
        qksum[0, n] = nn(lanes(kqa[:, n]), nall).astype(BF)
    low_all = jnp.where(
        lax.broadcasted_iota(jnp.int32, (rows, 128), 1) == 16, 1.0, nt(nall, dd_v[...])
    )
    esum[0] = nn(lanes(kqa[:, 2]), low_all.astype(BF))
    t_qs = send(qksum.at[0], qksum.at[1], partner)
    t_es = send(esum.at[0], esum.at[1], partner)

    arrived(t_fw)
    for n in range(2):
        fin_f[par, n] = total(pres[n, i], rfw.at[n]).astype(BF)
    t_ff = send(fin_f.at[par], fin_f.at[par], partner)
    arrived(t_s1)
    sm3[0] = total(sm2[0], sm2).astype(BF)
    t_s2 = send(sm3.at[0], sm3.at[1], partner)

    arrived(t_gk + t_vk)
    for n in range(2):
        vgsum[0, n] = nn(lanes(kvg[n]), nall).astype(BF)
    t_vs = send(vgsum.at[0], vgsum.at[1], partner)
    t_s2.wait_recv()
    sm4[j] = (sm3[0].astype(F32) + sm3[1].astype(F32)).astype(BF)
    t_s3 = [send(sm4.at[j], sm4.at[j], vdev[d]) for d in DIRS]

    arrived(t_ow)
    mid_o[...] = total(preso[i], rowk).astype(BF).reshape(W, 64, half)
    t_oz = [send(mid_o.at[vj[d]], rowz.at[d], vdev[d]) for d in DIRS]

    arrived(t_gn)
    for h in range(W):
        got = sgn[h, j].astype(F32)
        for d in DIRS:
            got = got + rgn[d, h].astype(F32)
        at = pl.ds(pl.multiple_of((h * W + j) * 64, 64), 64)
        ai[h] = (got - xr_v[at, :].astype(F32) * m1).astype(BF)
    t_ai = [send(ai.at[ki[d]], iseg.at[i], kdev[d]) for d in DIRS]
    iseg[i] = ai[i]

    arrived(t_out + t_out2)
    for h in range(W):
        got = so[h, j].astype(F32)
        for d in DIRS:
            got = got + ro[d, h].astype(F32)
        ao[h] = got.astype(BF)
    t_ao = [send(ao.at[ki[d]], oseg.at[i], kdev[d]) for d in DIRS]
    oseg[i] = ao[i]

    outs = []
    t_ds.wait_recv()
    left(t_ds)
    dsum[0] = (dsum[0].astype(F32) + dsum[1].astype(F32)).astype(BF)
    outs.append(load(dsum.at[0], o_d))
    t_qs.wait_recv()
    t_es.wait_recv()
    left(t_qs)
    left(t_es)
    qksum[0] = (qksum[0].astype(F32) + qksum[1].astype(F32)).astype(BF)
    esum[0] = esum[0] + esum[1]
    outs.append(load(qksum.at[0], o_qk))
    outs.append(load(esum.at[0], o_ext))
    t_ff.wait_recv()
    outs.append(load(fin_f, o_f))
    t_vs.wait_recv()
    left(t_vs)
    vgsum[0] = (vgsum[0].astype(F32) + vgsum[1].astype(F32)).astype(BF)
    outs.append(load(vgsum.at[0], o_vg))
    arrived(t_s3)
    for h in range(W):
        pick[:, h * T : (h + 1) * T] = sm4[h].astype(F32)
    pair = i * W + j
    small_v[...] = jnp.zeros_like(small_v)
    small_v[0:1, :] = pick[pl.ds(pair, 1), :]
    wide = pick[16:24, :]
    slab = D // (W * W)
    chosen = jnp.zeros((8, slab), F32)
    for n in range(W * W):
        chosen = jnp.where(pair == n, wide[:, n * slab : (n + 1) * slab], chosen)
    for n in range(W):
        group_slab = jnp.where(j == n, wide[2:3, n * 64 : (n + 1) * 64], 0.0)
        small_v[3:4, 0:64] = small_v[3:4, 0:64] + group_slab
    small_v[1:3, 0:slab] = chosen[0:2]
    outs.append(load(small_v, o_small))
    arrived(t_oz)
    fin_ow[par] = total(mid_o[j], rowz).astype(BF)
    t_fo = send(fin_ow.at[par], fin_ow.at[par], partner)
    arrived(t_ai)
    outs.append(load(iseg, o_in))
    arrived(t_ao)
    outs.append(load(oseg, o_out))
    t_fo.wait_recv()
    outs.append(load(fin_ow, o_ow))
    here(outs)
    for cp in sent:
        cp.wait_send()


N_REMOTE = 260
N_LOCAL = 40


def layer(n_seq, args):
    rows, D = args[0].shape
    W = WAYS
    T = rows // W
    FB = args[-1].shape[0]
    VC = W * 64
    half = D // 2

    def sds(shape, dtype=BF):
        return jax.ShapeDtypeStruct(shape, dtype)

    def vm(shape, dtype=BF):
        return pltpu.VMEM(shape, dtype)

    outs = [
        sds((W, 64, T)),
        sds((W, 64, T)),
        sds((2, 2, FB, half)),
        sds((FB, D)),
        sds((2, 64, D)),
        sds((2, 32, D)),
        sds((32, 128), F32),
        sds((2, 64, half)),
        sds((8, D), F32),
    ]
    scratch = [
        vm((T, D)),
        vm((T, D)),
        vm((rows, D)),
        vm((rows, D)),
        vm((rows, D)),
        vm((T, D)),
        vm((D, T)),
        vm((128, D)),
        vm((8, 128)),
        vm((8, 128)),
        vm((16, W, 32)),
        vm((W, 32)),
        vm((1, 64)),
        vm((128, 128), F32),
        vm((8, D), F32),
        vm((W, 2, 32, D)),
        vm((W, 32, 128)),
        vm((W, 64, D)),
        vm((W, 64, D)),
        vm((W, 64, 128)),
        vm((W, W, 64, D)),
        vm((3, W, FB, D)),
        vm((W, VC + 16, 128)),
        vm((n_seq, VC + 16, 128)),
        vm((W, VC + 16, 128)),
        vm((n_seq, VC + 16, 128)),
        vm((W, T, VC)),
        vm((W, T, VC)),
        vm((W, T, VC)),
        vm((8, T), F32),
        vm((W, 8, T), F32),
        vm((W, W, 64, T)),
        vm((W, W, 64, T)),
        vm((W, W, 64, T)),
        vm((W, W, 64, T)),
        vm((W, 64, T)),
        vm((W, 64, T)),
        vm((W, 64, T)),
        vm((W, 64, T)),
        vm((W, FB, T)),
        vm((W, FB, T)),
        vm((2, W, FB, D)),
        vm((2, W, FB, half)),
        vm((2, W, FB, half)),
        vm((2, W, FB, half)),
        vm((2, 2, FB, half)),
        vm((2, FB, D)),
        vm((W, VC, D)),
        vm((W, VC, half)),
        vm((W, VC, half)),
        vm((W, VC, half)),
        vm((W, 64, half)),
        vm((W, 64, half)),
        vm((2, 64, half)),
        vm((2, W, 64, T)),
        vm((2, W, 64, T)),
        vm((2, W, 64, T)),
        vm((2, 2, 64, D)),
        vm((W, 3, 32, T)),
        vm((W, 3, 32, T)),
        vm((2, 2, 32, D)),
        vm((2, 32, 128), F32),
        vm((W, 32, T)),
        vm((W, 32, T)),
        vm((W, 32, T)),
        vm((2, 32, T)),
        vm((W, 32, T)),
        vm((32, D), F32),
        vm((8, D), F32),
        vm((T, W * FB), F32),
        vm((3, T, VC), F32),
        vm((T, D), F32),
        pltpu.SemaphoreType.DMA((N_REMOTE,)),
        pltpu.SemaphoreType.DMA((N_REMOTE,)),
        pltpu.SemaphoreType.DMA((N_LOCAL,)),
    ]
    return pl.pallas_call(
        functools.partial(layer_kernel, n_seq),
        out_shape=outs,
        in_specs=[pl.BlockSpec(memory_space=pl.ANY)] * len(args),
        out_specs=[pl.BlockSpec(memory_space=pl.ANY)] * len(outs),
        scratch_shapes=scratch,
        compiler_params=pltpu.CompilerParams(
            collective_id=0, has_side_effects=True, vmem_limit_bytes=60 * 2**20
        ),
        name="layer",
    )(*args)


def finish_kernel(*refs):
    n_in = 9
    parts, rest = refs[:n_in], refs[n_in:]
    results, held, sem = rest[:16], rest[16:-1], rest[-1]
    copies = [pltpu.make_async_copy(a, b, sem.at[n]) for n, (a, b) in enumerate(zip(parts, held))]
    for cp in copies:
        cp.start()
    o_out, o_in, o_f, o_d, o_vg, o_qk, o_ext, o_ow, o_small = held
    (r_out, r_in, r_ng, r_q, r_k, r_v, r_g, r_dd, r_du, r_db, r_gg, r_o, r_fn, r_fg, r_fu, r_fd) = results
    T = o_out.shape[2]
    half = o_f.shape[3]
    copies[3].wait()
    r_fd[...] = o_d[...].astype(F32)
    copies[2].wait()
    for h in range(2):
        at = slice(h * half, (h + 1) * half)
        r_fg[:, at] = o_f[h, 0].astype(F32)
        r_fu[:, at] = o_f[h, 1].astype(F32)
    copies[4].wait()
    r_v[...] = o_vg[0].astype(F32)
    r_g[...] = o_vg[1].astype(F32)
    copies[5].wait()
    r_q[...] = o_qk[0].astype(F32)
    r_k[...] = o_qk[1].astype(F32)
    copies[7].wait()
    for h in range(2):
        r_o[:, h * half : (h + 1) * half] = o_ow[h].astype(F32)
    copies[0].wait()
    copies[1].wait()
    for n in range(WAYS):
        r_out[:, n * T : (n + 1) * T] = o_out[n]
        r_in[:, n * T : (n + 1) * T] = o_in[n]
    copies[8].wait()
    r_dd[...] = o_small[0:1, :]
    r_ng[...] = o_small[1:2, 0 : r_ng.shape[1]]
    r_fn[...] = o_small[2:3, 0 : r_fn.shape[1]]
    r_gg[...] = o_small[3:4, 0:64]
    copies[6].wait()
    decay = o_ext[...].T
    r_du[...] = decay[0:16, :].reshape(16, 1, 32)
    r_db[...] = decay[16:17, :]


def finish(parts):
    rows = parts[0].shape[0] * parts[0].shape[2]
    D = parts[3].shape[1]
    FB = parts[3].shape[0]
    slab = D // (WAYS * WAYS)

    def sds(shape, dtype=F32):
        return jax.ShapeDtypeStruct(shape, dtype)

    outs = [
        sds((64, rows), BF),
        sds((64, rows), BF),
        sds((1, slab)),
        sds((32, D)),
        sds((32, D)),
        sds((64, D)),
        sds((64, D)),
        sds((1, D)),
        sds((16, 1, 32)),
        sds((1, 32)),
        sds((1, 64)),
        sds((64, D)),
        sds((1, slab)),
        sds((FB, D)),
        sds((FB, D)),
        sds((FB, D)),
    ]
    return pl.pallas_call(
        finish_kernel,
        out_shape=outs,
        in_specs=[pl.BlockSpec(memory_space=pl.ANY)] * len(parts),
        out_specs=[pl.BlockSpec(memory_space=pltpu.VMEM)] * len(outs),
        scratch_shapes=[pltpu.VMEM(p.shape, p.dtype) for p in parts]
        + [pltpu.SemaphoreType.DMA((len(parts),))],
        compiler_params=pltpu.CompilerParams(vmem_limit_bytes=60 * 2**20),
        name="finish",
    )(*parts)


def shards(
    n_seq,
    tokens,
    norm_gain,
    query_weight,
    key_weight,
    value_weight,
    gate_weight,
    decay_down,
    decay_up,
    decay_bias,
    group_gain,
    out_weight,
    ffn_gain,
    ffn_gate,
    ffn_up,
    ffn_down,
    cotangent,
):
    parts = layer(
        n_seq,
        (
            tokens,
            cotangent,
            norm_gain.reshape(8, -1),
            ffn_gain.reshape(8, -1),
            decay_up,
            decay_bias,
            group_gain[None],
            query_weight.transpose(1, 2, 0),
            key_weight.transpose(1, 2, 0),
            value_weight.transpose(1, 2, 0),
            gate_weight.transpose(1, 2, 0),
            decay_down.T,
            out_weight[0],
            ffn_gate.T,
            ffn_up.T,
            ffn_down,
        ),
    )
    if n_seq > 2:

        def over_pairs(a):
            return jnp.sum(lax.all_gather(a, "seq")[::2].astype(F32), axis=0).astype(a.dtype)

        parts = list(parts[:2]) + [over_pairs(a) for a in parts[2:]]
    (r_out, r_in, r_ng, r_q, r_k, r_v, r_g, r_dd, r_du, r_db, r_gg, r_o, r_fn, r_fg, r_fu, r_fd) = finish(parts)
    return (
        r_out.T,
        r_in.T,
        r_ng[0],
        r_q.T[:, None, :],
        r_k.T[:, None, :],
        r_v.T[:, None, :],
        r_g.T[:, None, :],
        r_dd.T,
        r_du,
        r_db,
        r_gg[0],
        r_o[None],
        r_fn[0],
        r_fg.T,
        r_fu.T,
        r_fd,
    )


def solution(mesh):
    in_specs = (
        P("seq", None),
        P(),
        P(None, None, "kax"),
        P(None, None, "kax"),
        P(None, None, "vax"),
        P(None, None, "vax"),
        P(),
        P(None, None, "kax"),
        P(None, "kax"),
        P("vax"),
        P("kax", "vax", None),
        P(),
        P(None, ("kax", "vax")),
        P(None, ("kax", "vax")),
        P(("kax", "vax"), None),
        P("seq", None),
    )
    out_specs = (
        P("seq", ("kax", "vax")),
        P("seq", ("kax", "vax")),
        P(("kax", "vax")),
        P(None, "vax", "kax"),
        P(None, "vax", "kax"),
        P(None, "kax", "vax"),
        P(None, "kax", "vax"),
        P(None, ("kax", "vax")),
        P(None, "vax", "kax"),
        P("vax", "kax"),
        P("vax"),
        P("kax", "vax", None),
        P(("kax", "vax")),
        P(None, ("kax", "vax")),
        P(None, ("kax", "vax")),
        P(("kax", "vax"), None),
    )
    return jax.shard_map(
        functools.partial(shards, mesh.shape["seq"]),
        mesh=mesh,
        in_specs=in_specs,
        out_specs=out_specs,
        check_vma=False,
    )
```

time: 154 us -> 120 us (0.78)
  Pallas kernels: 136 us -> 119 us
  local copies, waits for them, and re-layouts: 15.1 us -> 0 us
    pallas_call x1, Pallas kernels: 135 us -> 115 us  [layer(): pl.pallas_call(functools.partial(layer_kernel, n_seq), out_shape=outs, in...]
    unnamed x15 -> x0, local copies, waits for them, and re-layouts: 6.48 us -> none
    broadcast_in_dim x8 -> x0, local copies, waits for them, and re-layouts: 4.22 us -> none  [the longest x1 1.34 us: shards(): gge = jnp.broadcast_to(group_gain[:, None], (64, 128))]
    pallas_call x1, Pallas kernels: 1.79 us -> 3.46 us  [finish(): pl.pallas_call(finish_kernel, out_shape=outs, in_specs=[pl.BlockSpec(memo...]
where the time goes in v2:
time: 120 us
  Pallas kernels  119 us (99%)
    pallas_call x1, Pallas kernels, layer(): pl.pallas_call(functools.partial(layer_kernel, n_seq), out_shape=outs, in...  115 us
    pallas_call x1, Pallas kernels, finish(): pl.pallas_call(finish_kernel, out_shape=outs, in_specs=[pl.BlockSpec(memo...  3.46 us

profile of v2, /device:TPU:0, one launch (start us, length us, event | category | flops | bytes accessed | tf_op | source)
XLA Modules:
  0.0 119.7 jit_solution(16106500764516968007)
XLA Ops:
  0.7 115.4 %layer.1 = (bf16[4,64,256]{2,1,0:T(8,128)(2,1)}, bf16[4,64,256]{2,1,0:T(8,128)(2,1)}, bf16[2,2,176,512]{3,2,1,0:T(8,128)(2,1)}, bf16[176,1024]{1,0:T(8,128)(2,1)...) custom-call(bf16[1024,1024]{1,0:T(8,128)(2,1)} %tok.1, ...), custom_call_target="tpu_custom_call" | custom-call | tf_op jit(solution)/shard_map/layer/pallas_call | solution.py:843
  116.0 3.5 %finish.1 = (bf16[64,1024]{1,0:T(8,128)(2,1)}, bf16[64,1024]{1,0:T(8,128)(2,1)}, f32[1,64]{1,0:T(1,128)}, f32[32,1024]{1,0:T(8,128)}, f32[32,1024]{1,0:T(8,128)}...) custom-call(bf16[4,64,256]{2,1,0:T(8,128)(2,1)} %get-tuple-element.4, ...), custom_call_target="tpu_custom_call" | custom-call | tf_op jit(solution)/shard_map/finish/pallas_call | solution.py:926

commit v3 on v2

--- a/solution.py
+++ b/solution.py
@@ -121,12 +121,15 @@
     ga_v,
     sgg,
     rgg,
+    cgg,
     sst,
     rst,
     so,
     ro,
+    co,
     sgn,
     rgn,
+    cgn,
     ao,
     oseg,
     ai,
@@ -137,12 +140,16 @@
     pre,
     pres,
     rfw,
+    qfw,
+    cfw,
     fin_f,
     dsum,
     gow,
     preo,
     preso,
     rowk,
+    qow,
+    cow,
     mid_o,
     rowz,
     fin_ow,
@@ -191,14 +198,17 @@
     count = [0, 0]
     sent = []
 
-    def remote(src, dst, dev):
-        n = count[0]
+    def slot():
         count[0] += 1
+        return count[0] - 1
+
+    def remote(src, dst, dev, to=None):
+        n = slot()
         return pltpu.make_async_remote_copy(
             src_ref=src,
             dst_ref=dst,
             send_sem=ss.at[n],
-            recv_sem=rs.at[n],
+            recv_sem=rs.at[n if to is None else to],
             device_id=dev,
             device_id_type=MESH,
         )
@@ -227,6 +237,131 @@
     def here(copies):
         for cp in copies:
             cp.wait()
+
+    inner = lax.rem(j + 1, W) >= 2
+    inner_sent = []
+    outer_sent = []
+
+    class LineGather:
+        def __init__(self, view):
+            a, b, c = slot(), slot(), slot()
+            self.near = remote(view(j), view(j), vdev[1], a)
+            self.near.start()
+            sent.append(self.near)
+            across = remote(view(j), view(j), vdev[3], c)
+            self.got = [
+                pltpu.make_async_remote_copy(
+                    src_ref=view(vj[d]),
+                    dst_ref=view(vj[d]),
+                    send_sem=ss.at[n],
+                    recv_sem=rs.at[n],
+                    device_id=vdev[1],
+                    device_id_type=MESH,
+                )
+                for d, n in zip(DIRS, (a, b, c))
+            ]
+            self.on = [
+                remote(view(vj[1]), view(vj[1]), vdev[3], b),
+                remote(view(vj[3]), view(vj[3]), vdev[1], b),
+                remote(view(vj[2]), view(vj[2]), vdev[1], c),
+            ]
+            inner_sent.extend([across] + self.on)
+
+            @pl.when(inner)
+            def _():
+                across.start()
+
+        def step(self, n):
+            @pl.when(inner)
+            def _():
+                self.got[(0, 2, 1)[n]].wait_recv()
+                self.on[n].start()
+
+        def collect(self):
+            @pl.when(jnp.logical_not(inner))
+            def _():
+                arrived(self.got)
+
+    class LineSum:
+        def __init__(self, part, near, far, relay, summed):
+            self.part, self.near, self.far, self.relay, self.summed = part, near, far, relay, summed
+            b = slot()
+            self.first = [
+                remote(part(vj[3]), relay.at[0], vdev[1]),
+                remote(part(vj[2]), relay.at[1], vdev[1]),
+            ]
+            outer_sent.extend(self.first)
+
+            @pl.when(jnp.logical_not(inner))
+            def _():
+                for cp in self.first:
+                    cp.start()
+
+            self.direct = send(part(vj[1]), near, vdev[1])
+            self.second = [
+                remote(summed.at[0], far, vdev[2], b),
+                remote(summed.at[1], far, vdev[3], b),
+            ]
+            inner_sent.extend(self.second)
+            self.last = pltpu.make_async_remote_copy(
+                src_ref=far,
+                dst_ref=far,
+                send_sem=ss.at[b],
+                recv_sem=rs.at[b],
+                device_id=vdev[1],
+                device_id_type=MESH,
+            )
+
+        def step(self, n):
+            @pl.when(inner)
+            def _():
+                self.first[n].wait_recv()
+                mine_too = self.part(vj[2 + n])[...].astype(F32)
+                self.summed[n] = (mine_too + self.relay[n].astype(F32)).astype(BF)
+                self.second[n].start()
+
+        def collect(self):
+            self.direct.wait_recv()
+            self.last.wait_recv()
+
+        def total(self):
+            out = self.part(j)[...].astype(F32)
+            return out + self.near[...].astype(F32) + self.far[...].astype(F32)
+
+    class SquareSum:
+        def __init__(self, part, got, relay, summed):
+            self.part, self.got, self.relay, self.summed = part, got, relay, summed
+            q = got.shape[-1] // 2
+            self.at = [pl.ds(0, q), pl.ds(q, q)]
+            self.first = [
+                send(self.half(ki[3], n), relay.at[n], kdev[1 + n]) for n in range(2)
+            ]
+            self.direct = [
+                send(self.half(ki[1 + n], n), self.into(n, n), kdev[1 + n]) for n in range(2)
+            ]
+
+        def half(self, target, n):
+            return self.part(target, self.at[n])
+
+        def into(self, n, h):
+            return self.got.at[n, :, self.at[h]]
+
+        def step(self):
+            self.second = []
+            for n in range(2):
+                self.first[n].wait_recv()
+                own = self.half(ki[2 - n], n)[...].astype(F32)
+                self.summed[n] = (own + self.relay[n].astype(F32)).astype(BF)
+                self.second.append(
+                    send(self.summed.at[n], self.into(1 - n, n), kdev[2 - n])
+                )
+
+        def collect(self):
+            arrived(self.direct + self.second)
+
+        def total(self):
+            out = self.part(i, pl.ds(0, self.got.shape[-1]))[...].astype(F32)
+            return out + self.got[0].astype(F32) + self.got[1].astype(F32)
 
     l_small = [load(dup, dup_v), load(dbi, dbi_v), load(ggn, ggn_v)]
     l_qk = [load(wq.at[j], qk_v.at[i, 0]), load(wk.at[j], qk_v.at[i, 1])]
@@ -273,28 +408,38 @@
     t_ob = [None] + [
         send(wo.at[high, mine], o_v.at[i, j, high, mine], kdev[d]) for d in DIRS
     ]
-    cut = FB // 32 * 16
+    quarter = half // 2
+    two = [
+        pl.ds(pl.multiple_of(par * half + n * quarter, quarter), quarter) for n in range(2)
+    ]
+
+    class SquareGather:
+        def __init__(self, view, own=None):
+            self.view = view
+            own = view(i, mine) if own is None else own
+            self.near = [send(own, view(i, mine), kdev[d]) for d in (1, 2)]
+
+        def step(self):
+            self.far, moves = [], []
+            for n in range(2):
+                self.near[n].wait_recv()
+                view = self.view(ki[1 + n], two[n])
+                self.far.append(send(view, view, kdev[2 - n]))
+                view = self.view(ki[1 + n], mine)
+                moves.append(send(view, view, partner))
+            return moves
+
+        def collect(self):
+            arrived(self.far)
+            view = self.view(ki[3], mine)
+            return [send(view, view, partner)]
+
     weights = (fg, fu, fd)
-    pieces = [(2, 0, cut), (2, cut, FB - cut), (0, 0, FB), (1, 0, FB)]
-
-    def send_piece(piece):
-        n, first, size = piece
-        at = pl.ds(first, size)
-        return [None] + [
-            send(weights[n].at[at, mine], f_v.at[n, i, at, mine], kdev[d]) for d in DIRS
-        ]
-
-    def pass_piece(piece, copies):
-        n, first, size = piece
-        at = pl.ds(first, size)
-        moves = []
-        for d in DIRS:
-            copies[d].wait_recv()
-            view = f_v.at[n, ki[d], at, mine]
-            moves.append(send(view, view, partner))
-        return moves
-
-    t_f = [send_piece(pieces[0])]
+
+    def gather_weight(n):
+        return SquareGather(lambda src, at: f_v.at[n, src, :, at], weights[n].at[:, mine])
+
+    t_fd = gather_weight(2)
     t_g = [None] + [send(wg.at[vj[d], :, mine], g_v.at[j, :, mine], vdev[d]) for d in DIRS]
     t_gge = [send(gge_v.at[j], gge_v.at[j], vdev[d]) for d in DIRS]
 
@@ -365,8 +510,8 @@
     st_v[i, :VC] = loc.astype(BF)
     st_v[i, VC:] = jnp.broadcast_to(locd, (16, 128)).astype(BF)
     t_st = [send(st_v.at[i], st_v.at[i], kdev[d]) for d in DIRS]
-    for piece in pieces[1:]:
-        t_f.append(send_piece(piece))
+    t_fg = gather_weight(0)
+    t_fu = gather_weight(1)
     mixed = [nn(score[c], v[blk[c]]) for c in range(nblk)]
 
     f_o = []
@@ -375,29 +520,16 @@
         t_oa[d].wait_recv()
         view = o_v.at[i, vj[d], low, mine]
         f_o.append(send(view, view, partner))
-    t_oa2 = [None] + [
-        send(o_v.at[i, :, low, mine], o_v.at[i, :, low, mine], kdev[d]) for d in DIRS
-    ]
+    t_oa2 = SquareGather(lambda src, at: o_v.at[src, :, low, at])
     for d in DIRS:
         t_ob[d].wait_recv()
         view = o_v.at[ki[d], j, high, mine]
         f_o.append(send(view, view, partner))
-    f_g = []
-    l_g.wait()
-    for d in DIRS:
-        t_g[d].wait_recv()
-        f_g.append(send(g_v.at[vj[d], :, mine], g_v.at[vj[d], :, mine], partner))
-    arrived(f_g)
-    arrived(t_gge)
-    wg_all = g_v[...].reshape(W * 64, D)
-    gate = nt(normed, wg_all)
-    gg = gge_v[...].astype(F32).reshape(W * 64, 128).T[:1]
-    sig = 1.0 / (1.0 + jnp.exp(-gate))
-    act = gate * sig
-    act_v[0] = act
-    act_v[1] = sig + act * (1.0 - sig)
-
-    def entering(slots, totals, back):
+    t_ob2 = LineGather(lambda src: o_v.at[:, src, high, mine])
+    here(l_f)
+    f_f = t_fd.step()
+
+    def gather_states(slots, totals, back):
         order = range(W - 1, -1, -1) if back else range(W)
         pre_s = jnp.zeros((VC, 128), F32)
         pre_d = jnp.ones((1, 128), F32)
@@ -413,7 +545,10 @@
             tot_d = tot_d * one_d
         totals[s, :VC] = tot_s.astype(BF)
         totals[s, VC:] = jnp.broadcast_to(tot_d, (16, 128)).astype(BF)
-        arrived([send(totals.at[s], totals.at[s], dev) for dev in seqdev])
+        return pre_s, pre_d, [send(totals.at[s], totals.at[s], dev) for dev in seqdev]
+
+    def entering(totals, back, pre_s, pre_d, moves):
+        arrived(moves)
         order = range(n_seq - 1, -1, -1) if back else range(n_seq)
         far = jnp.zeros((VC, 128), F32)
         for other_s in order:
@@ -424,7 +559,14 @@
         return pre_s + pre_d * far
 
     arrived(t_st)
-    start = [entering(st_v, tt_v, False)]
+    states = gather_states(st_v, tt_v, False)
+
+    f_g = []
+    l_g.wait()
+    for d in DIRS:
+        t_g[d].wait_recv()
+        f_g.append(send(g_v.at[vj[d], :, mine], g_v.at[vj[d], :, mine], partner))
+    start = [entering(tt_v, False, *states)]
     for c in range(nblk):
         start.append(start[c] * dec[c] + up[c])
     start_low = [a.astype(BF) for a in start]
@@ -433,12 +575,18 @@
     mix = jnp.concatenate(mixed, axis=0)
     r2 = lax.rsqrt(jnp.sum(mix * mix, axis=1, keepdims=True) / VC + EPS)
     normal = mix * r2
-    ga_v[j] = (normal * gg * act_v[0]).astype(BF)
+    arrived(f_g)
+    arrived(t_gge)
+    wg_all = g_v[...].reshape(W * 64, D)
+    gate = nt(normed, wg_all)
+    gg = gge_v[...].astype(F32).reshape(W * 64, 128).T[:1]
+    sig = 1.0 / (1.0 + jnp.exp(-gate))
+    act = gate * sig
+    act_v[0] = act
+    act_v[1] = sig + act * (1.0 - sig)
+    ga_v[j] = (normal * gg * act).astype(BF)
     act_v[2] = normal
-    t_ga = [send(ga_v.at[j], ga_v.at[j], vdev[d]) for d in DIRS]
-    t_ob2 = [None] + [
-        send(o_v.at[:, j, high, mine], o_v.at[:, j, high, mine], vdev[d]) for d in DIRS
-    ]
+    t_ga = LineGather(lambda src: ga_v.at[src])
 
     here([l_xa, l_ca])
     for part in range(rows // T):
@@ -447,25 +595,28 @@
         ra = lax.rsqrt(jnp.sum(xa * xa, axis=1, keepdims=True) / D + EPS)
         n_all[at, :] = (xa * ra * g1).astype(BF)
     xr_v[...] = (x * (r1 * r1 * r1)).astype(BF).T
-    here(l_f + [l_c])
-    f_f = []
-    for piece, copies in zip(pieces[:2], t_f[:2]):
-        f_f += pass_piece(piece, copies)
+    t_ob2.step(0)
+    t_ob2.step(1)
+    f_f += t_fg.step()
+    t_ob2.step(2)
+    t_ga.step(0)
+    t_ga.step(1)
+    f_f += t_fd.collect()
+    f_f += t_fu.step()
+    f_o += t_oa2.step()
+    t_ga.step(2)
+    l_c.wait()
     arrived(f_f)
     dn = f_v[2].reshape(W * FB, D)
     gh_v[...] = nt(c_v[...], dn)
-    f_f = []
-    for piece, copies in zip(pieces[2:], t_f[2:]):
-        f_f += pass_piece(piece, copies)
+    f_f = t_fg.collect()
+    f_f += t_fu.collect()
+    f_o += t_oa2.collect()
+    t_ob2.collect()
     for d in DIRS:
-        t_oa2[d].wait_recv()
-        view = o_v.at[ki[d], :, low, mine]
-        f_o.append(send(view, view, partner))
-    arrived(t_ga)
-    for d in DIRS:
-        t_ob2[d].wait_recv()
         view = o_v.at[:, vj[d], high, mine]
         f_o.append(send(view, view, partner))
+    t_ga.collect()
     arrived(f_o)
     att = nn(ga_v[0], o_v[0].reshape(W * 64, D))
     for h in range(1, W):
@@ -492,10 +643,12 @@
     ggp = nt((part * g3).astype(BF), o_v[...].reshape(W * W * 64, D))
     for h in range(W):
         sgg[h] = ggp[:, h * VC : (h + 1) * VC].astype(BF)
-    t_gg = [send(sgg.at[vj[d]], rgg.at[d], vdev[d]) for d in DIRS]
+    t_gg = LineSum(lambda to: sgg.at[to], rgg.at[0], rgg.at[1], rgg.at[pl.ds(2, 2)], cgg)
     hd[...] = hid.T.reshape(W, FB, T)
     t_hd = [send(hd.at[ki[d]], hseg.at[i], kdev[d]) for d in DIRS]
     hseg[i] = hd[i]
+
+    t_gg.step(0)
 
     t_pre = []
     for n, grad in enumerate((ggate, gup)):
@@ -506,17 +659,18 @@
     own_slab = jnp.where(lax.rem(feature // 64, W) == j, 1.0, 0.0)
     own_run = jnp.where(feature // (D // W) == j, 1.0, 0.0)
     so[...] = (nn(hid, dn) + own_slab * resid).astype(BF).T.reshape(W, W, 64, T)
-    pair01 = pl.ds(0, W // 2)
-    pair23 = pl.ds(W // 2, W // 2)
-    t_out = [send(so.at[pair01, vj[d]], ro.at[d, pair01], vdev[d]) for d in DIRS]
+    t_gg.step(1)
+    t_out = LineSum(lambda to: so.at[:, to], ro.at[0], ro.at[1], ro.at[pl.ds(2, 2)], co)
     ffn_gain = jnp.sum(part * resid * r3, axis=0, keepdims=True)
 
     def settle(n):
         t_pre[n].wait_recv()
         pres[n] = (gw[n, :, :, mine].astype(F32) + pre[n].astype(F32)).astype(BF)
-        return [send(pres.at[n, ki[d]], rfw.at[n, d], kdev[d]) for d in DIRS]
-
-    t_fw = settle(0)
+        return SquareSum(
+            lambda to, at: pres.at[n, to, :, at], rfw.at[n], qfw.at[n], cfw.at[n]
+        )
+
+    t_fw = [settle(0)]
 
     arrived(t_m3)
     m3 = as_column(sst[...] + rst[1] + rst[2] + rst[3]) / D
@@ -527,9 +681,10 @@
     for h in range(W):
         gow[h] = tn(ga_v[h], mixed_in).astype(BF)
     t_po = send(gow.at[:, :, other], preo, partner)
-    arrived(t_gg)
-
-    ggs = total(sgg[j], rgg)
+    t_out.step(0)
+    t_gg.collect()
+
+    ggs = t_gg.total()
     ggrad = direct + r3 * ggs
     act = act_v[0]
     normal = act_v[2]
@@ -548,7 +703,9 @@
     t_bst = [send(bst_v.at[i], bst_v.at[i], kdev[d]) for d in DIRS]
     vz[1] = dgate.T.reshape(W, 64, T)
     t_gz = [send(vz.at[1, vj[d]], zvg.at[1, j], vdev[d]) for d in DIRS]
-    t_fw += settle(1)
+    t_fw.append(settle(1))
+    t_out.step(1)
+    t_fw[0].step()
     dscore, dq_in, dk_in, dv_in = [], [], [], []
     for c in range(nblk):
         ds = jnp.where(causal, nt(gmix[blk[c]], v[blk[c]]), 0.0).astype(BF)
@@ -559,7 +716,9 @@
     preso[...] = (gow[:, :, mine].astype(F32) + preo[...].astype(F32)).astype(BF)
     arrived(t_bst)
     after = [None] * nblk
-    after[nblk - 1] = entering(bst_v, btt_v, True)
+    states = gather_states(bst_v, btt_v, True)
+    t_fw[1].step()
+    after[nblk - 1] = entering(btt_v, True, *states)
     for c in range(nblk - 2, -1, -1):
         after[c] = after[c + 1] * dec[c + 1] + qst[c + 1]
 
@@ -607,9 +766,13 @@
     t_s0 = [send(sm0.at[vj[d]], sm1.at[d], vdev[d]) for d in DIRS]
     whole = gn * (r1 * g1) + full + own_slab * base
     sgn[...] = whole.astype(BF).T.reshape(W, W, 64, T)
-    t_gn = [send(sgn.at[:, vj[d]], rgn.at[d], vdev[d]) for d in DIRS]
-    t_out2 = [send(so.at[pair23, vj[d]], ro.at[d, pair23], vdev[d]) for d in DIRS]
-    t_ow = [send(preso.at[ki[d]], rowk.at[d], kdev[d]) for d in DIRS]
+    t_gn = LineSum(lambda to: sgn.at[:, to], rgn.at[0], rgn.at[1], rgn.at[pl.ds(2, 2)], cgn)
+    t_ow = SquareSum(lambda to, at: preso.at[to, :, at], rowk, qow, cow)
+
+    t_out.collect()
+    ao[...] = t_out.total().astype(BF)
+    t_ao = [send(ao.at[ki[d]], oseg.at[i], kdev[d]) for d in DIRS]
+    oseg[i] = ao[i]
 
     arrived(t_hd)
     dsum[0] = nn(lanes(hseg[...]), c_all[...]).astype(BF)
@@ -629,10 +792,13 @@
         + sm1[3, 19:20].astype(F32)
     ) / D
     t_s1 = [send(sm2.at[0], sm2.at[d], kdev[d]) for d in DIRS]
+    t_gn.step(0)
     arrived(t_vz)
     zvg[0, j] = vz[0, j]
     t_vk = [send(zvg.at[0, ki[d]], kvg.at[0, i], kdev[d]) for d in DIRS]
     kvg[0, i] = zvg[0, i]
+    t_gn.step(1)
+    t_ow.step()
 
     arrived(t_qa)
     kqa[i] = qka[i]
@@ -646,9 +812,9 @@
     t_qs = send(qksum.at[0], qksum.at[1], partner)
     t_es = send(esum.at[0], esum.at[1], partner)
 
-    arrived(t_fw)
     for n in range(2):
-        fin_f[par, n] = total(pres[n, i], rfw.at[n]).astype(BF)
+        t_fw[n].collect()
+        fin_f[par, n] = t_fw[n].total().astype(BF)
     t_ff = send(fin_f.at[par], fin_f.at[par], partner)
     arrived(t_s1)
     sm3[0] = total(sm2[0], sm2).astype(BF)
@@ -662,28 +828,17 @@
     sm4[j] = (sm3[0].astype(F32) + sm3[1].astype(F32)).astype(BF)
     t_s3 = [send(sm4.at[j], sm4.at[j], vdev[d]) for d in DIRS]
 
-    arrived(t_ow)
-    mid_o[...] = total(preso[i], rowk).astype(BF).reshape(W, 64, half)
+    t_ow.collect()
+    mid_o[...] = t_ow.total().astype(BF).reshape(W, 64, half)
     t_oz = [send(mid_o.at[vj[d]], rowz.at[d], vdev[d]) for d in DIRS]
 
-    arrived(t_gn)
+    t_gn.collect()
+    summed = t_gn.total()
     for h in range(W):
-        got = sgn[h, j].astype(F32)
-        for d in DIRS:
-            got = got + rgn[d, h].astype(F32)
         at = pl.ds(pl.multiple_of((h * W + j) * 64, 64), 64)
-        ai[h] = (got - xr_v[at, :].astype(F32) * m1).astype(BF)
+        ai[h] = (summed[h] - xr_v[at, :].astype(F32) * m1).astype(BF)
     t_ai = [send(ai.at[ki[d]], iseg.at[i], kdev[d]) for d in DIRS]
     iseg[i] = ai[i]
-
-    arrived(t_out + t_out2)
-    for h in range(W):
-        got = so[h, j].astype(F32)
-        for d in DIRS:
-            got = got + ro[d, h].astype(F32)
-        ao[h] = got.astype(BF)
-    t_ao = [send(ao.at[ki[d]], oseg.at[i], kdev[d]) for d in DIRS]
-    oseg[i] = ao[i]
 
     outs = []
     t_ds.wait_recv()
@@ -733,9 +888,19 @@
     for cp in sent:
         cp.wait_send()
 
-
-N_REMOTE = 260
-N_LOCAL = 40
+    @pl.when(inner)
+    def _():
+        for cp in inner_sent:
+            cp.wait_send()
+
+    @pl.when(jnp.logical_not(inner))
+    def _():
+        for cp in outer_sent:
+            cp.wait_send()
+
+
+N_REMOTE = 172
+N_LOCAL = 27
 
 
 def layer(n_seq, args):
@@ -793,12 +958,15 @@
         vm((W, T, VC)),
         vm((W, T, VC)),
         vm((W, T, VC)),
+        vm((2, T, VC)),
         vm((8, T), F32),
         vm((W, 8, T), F32),
         vm((W, W, 64, T)),
         vm((W, W, 64, T)),
+        vm((2, W, 64, T)),
         vm((W, W, 64, T)),
         vm((W, W, 64, T)),
+        vm((2, W, 64, T)),
         vm((W, 64, T)),
         vm((W, 64, T)),
         vm((W, 64, T)),
@@ -808,13 +976,17 @@
         vm((2, W, FB, D)),
         vm((2, W, FB, half)),
         vm((2, W, FB, half)),
-        vm((2, W, FB, half)),
+        vm((2, 2, FB, half)),
+        vm((2, 2, FB, half // 2)),
+        vm((2, 2, FB, half // 2)),
         vm((2, 2, FB, half)),
         vm((2, FB, D)),
         vm((W, VC, D)),
         vm((W, VC, half)),
         vm((W, VC, half)),
-        vm((W, VC, half)),
+        vm((2, VC, half)),
+        vm((2, VC, half // 2)),
+        vm((2, VC, half // 2)),
         vm((W, 64, half)),
         vm((W, 64, half)),
         vm((2, 64, half)),
@@ -836,8 +1008,8 @@
         vm((T, W * FB), F32),
         vm((3, T, VC), F32),
         vm((T, D), F32),
-        pltpu.SemaphoreType.DMA((N_REMOTE,)),
-        pltpu.SemaphoreType.DMA((N_REMOTE,)),
+        pltpu.SemaphoreType.DMA((N_REMOTE + 2 * n_seq,)),
+        pltpu.SemaphoreType.DMA((N_REMOTE + 2 * n_seq,)),
         pltpu.SemaphoreType.DMA((N_LOCAL,)),
     ]
     return pl.pallas_call(

time: 120 us -> 102 us (0.85)
  Pallas kernels: 119 us -> 100 us
    pallas_call x1, Pallas kernels: 115 us -> 96.8 us  [layer(): pl.pallas_call(functools.partial(layer_kernel, n_seq), out_shape=outs, in...]
where the time goes in v3:
time: 102 us; the launch traced here: 101 us
  Pallas kernels  100 us (98%)
    pallas_call x1, Pallas kernels, layer(): pl.pallas_call(functools.partial(layer_kernel, n_seq), out_shape=outs, in...  96.8 us
    pallas_call x1, Pallas kernels, finish(): pl.pallas_call(finish_kernel, out_shape=outs, in_specs=[pl.BlockSpec(memo...  3.46 us

profile of v3, /device:TPU:0, one launch (start us, length us, event | category | flops | bytes accessed | tf_op | source)
XLA Modules:
  0.0 101.1 jit_solution(4192856545428064784)
XLA Ops:
  0.7 96.8 %layer.1 = (bf16[4,64,256]{2,1,0:T(8,128)(2,1)}, bf16[4,64,256]{2,1,0:T(8,128)(2,1)}, bf16[2,2,176,512]{3,2,1,0:T(8,128)(2,1)}, bf16[176,1024]{1,0:T(8,128)(2,1)...) custom-call(bf16[1024,1024]{1,0:T(8,128)(2,1)} %tok.1, ...), custom_call_target="tpu_custom_call" | custom-call | tf_op jit(solution)/shard_map/layer/pallas_call | solution.py:1015
  97.5 3.5 %finish.1 = (bf16[64,1024]{1,0:T(8,128)(2,1)}, bf16[64,1024]{1,0:T(8,128)(2,1)}, f32[1,64]{1,0:T(1,128)}, f32[32,1024]{1,0:T(8,128)}, f32[32,1024]{1,0:T(8,128)}...) custom-call(bf16[4,64,256]{2,1,0:T(8,128)(2,1)} %get-tuple-element.4, ...), custom_call_target="tpu_custom_call" | custom-call | tf_op jit(solution)/shard_map/finish/pallas_call | solution.py:1098

commit v4 on v3

--- a/solution.py
+++ b/solution.py
@@ -83,15 +83,22 @@
     fg,
     fu,
     fd,
-    o_out,
-    o_in,
-    o_f,
-    o_d,
-    o_vg,
-    o_qk,
-    o_ext,
-    o_ow,
-    o_small,
+    r_out,
+    r_in,
+    r_ng,
+    r_q,
+    r_k,
+    r_v,
+    r_g,
+    r_dd,
+    r_du,
+    r_db,
+    r_gg,
+    r_o,
+    r_fn,
+    r_fg,
+    r_fu,
+    r_fd,
     x_v,
     c_v,
     x_all,
@@ -152,6 +159,7 @@
     cow,
     mid_o,
     rowz,
+    coz,
     fin_ow,
     vz,
     zvg,
@@ -167,7 +175,7 @@
     sm3,
     sm4,
     pick,
-    small_v,
+    lall_v,
     gh_v,
     act_v,
     p_v,
@@ -226,9 +234,30 @@
         cp.start()
         return cp
 
-    def left(cp):
-        cp.wait_send()
-        sent[:] = [one for one in sent if one is not cp]
+    class Fan:
+        def __init__(self, copies, size):
+            n = slot()
+
+            def one(src, dst, dev):
+                return pltpu.make_async_remote_copy(
+                    src_ref=src,
+                    dst_ref=dst,
+                    send_sem=ss.at[n],
+                    recv_sem=rs.at[n],
+                    device_id=dev,
+                    device_id_type=MESH,
+                )
+
+            for src, dst, dev in copies:
+                one(src, dst, dev).start()
+            self.all = one(size, size, partner)
+            sent.append(self)
+
+        def wait_recv(self):
+            self.all.wait_recv()
+
+        def wait_send(self):
+            self.all.wait_send()
 
     def arrived(copies):
         for cp in copies:
@@ -297,7 +326,6 @@
                 for cp in self.first:
                     cp.start()
 
-            self.direct = send(part(vj[1]), near, vdev[1])
             self.second = [
                 remote(summed.at[0], far, vdev[2], b),
                 remote(summed.at[1], far, vdev[3], b),
@@ -312,6 +340,10 @@
                 device_id_type=MESH,
             )
 
+        def rest(self):
+            self.direct = send(self.part(vj[1]), self.near, vdev[1])
+            return self
+
         def step(self, n):
             @pl.when(inner)
             def _():
@@ -391,15 +423,15 @@
     )
     ext_v[i] = sq_v[...].T[:32].astype(BF)
     sq_v[...] = jnp.zeros_like(sq_v)
-    sq_v[0:8, 0:64] = jnp.broadcast_to(ggn_v[...].astype(F32), (8, 64))
-    gge_v[j] = sq_v[...].T[:64].astype(BF)
+    sq_v[0:16, 0:64] = jnp.broadcast_to(ggn_v[...].astype(F32), (16, 64))
+    gge_v[j] = sq_v[0:16].astype(BF)
 
     pl.semaphore_wait(barrier, 6 + len(seqdev))
 
     here(l_qk)
     t_qk = [None] + [send(qk_v.at[i, par], qk_v.at[i, par], kdev[d]) for d in DIRS]
     t_v = [None] + [send(wv.at[vj[d], :, mine], v_v.at[j, :, mine], vdev[d]) for d in DIRS]
-    t_ext = [send(ext_v.at[i], ext_v.at[i], kdev[d]) for d in DIRS]
+    t_ext = Fan([(ext_v.at[i], ext_v.at[i], kdev[d]) for d in DIRS], ext_v.at[pl.ds(0, 3)])
     low = pl.ds(0, 32)
     high = pl.ds(32, 32)
     t_oa = [None] + [
@@ -441,7 +473,7 @@
 
     t_fd = gather_weight(2)
     t_g = [None] + [send(wg.at[vj[d], :, mine], g_v.at[j, :, mine], vdev[d]) for d in DIRS]
-    t_gge = [send(gge_v.at[j], gge_v.at[j], vdev[d]) for d in DIRS]
+    t_gge = Fan([(gge_v.at[j], gge_v.at[j], vdev[d]) for d in DIRS], gge_v.at[pl.ds(0, 3)])
 
     here(l_x)
     x = x_v[...].astype(F32)
@@ -453,12 +485,12 @@
     lane = lax.broadcasted_iota(jnp.int32, (T, 128), 1)
     lrp = jnp.where(lane == 16, 1.0, nt(n_v[...], dd_v[...]))
 
-    f_qk = []
     for d in DIRS:
         t_qk[d].wait_recv()
-        f_qk.append(send(qk_v.at[ki[d], par], qk_v.at[ki[d], par], partner))
-    arrived(t_ext)
-    arrived(f_qk)
+    views = [qk_v.at[ki[d], par] for d in DIRS]
+    f_qk = Fan([(view, view, partner) for view in views], qk_v.at[pl.ds(0, 3), 0])
+    t_ext.wait_recv()
+    f_qk.wait_recv()
     normed = n_v[...]
     wq_all = qk_v[:, 0].reshape(W * 32, D)
     wk_all = qk_v[:, 1].reshape(W * 32, D)
@@ -493,11 +525,12 @@
         score.append(jnp.where(causal, nt(qd[c], kd[c]), 0.0).astype(BF))
 
     l_v.wait()
-    f_vv = []
     for d in DIRS:
         t_v[d].wait_recv()
-        f_vv.append(send(v_v.at[vj[d], :, mine], v_v.at[vj[d], :, mine], partner))
-    arrived(f_vv)
+    first_half = pl.ds(0, half)
+    views = [v_v.at[vj[d], :, mine] for d in DIRS]
+    f_vv = Fan([(view, view, partner) for view in views], v_v.at[pl.ds(0, 3), :, first_half])
+    f_vv.wait_recv()
     wv_all = v_v[...].reshape(W * 64, D)
     v = nt(normed, wv_all).astype(BF)
     up = [tn(v[blk[c]], ke[c]) for c in range(nblk)]
@@ -509,7 +542,7 @@
     VC = loc.shape[0]
     st_v[i, :VC] = loc.astype(BF)
     st_v[i, VC:] = jnp.broadcast_to(locd, (16, 128)).astype(BF)
-    t_st = [send(st_v.at[i], st_v.at[i], kdev[d]) for d in DIRS]
+    t_st = Fan([(st_v.at[i], st_v.at[i], kdev[d]) for d in DIRS], st_v.at[pl.ds(0, 3)])
     t_fg = gather_weight(0)
     t_fu = gather_weight(1)
     mixed = [nn(score[c], v[blk[c]]) for c in range(nblk)]
@@ -558,14 +591,14 @@
             far = jnp.where(use, far * one_d + one_s, far)
         return pre_s + pre_d * far
 
-    arrived(t_st)
+    t_st.wait_recv()
     states = gather_states(st_v, tt_v, False)
 
-    f_g = []
     l_g.wait()
     for d in DIRS:
         t_g[d].wait_recv()
-        f_g.append(send(g_v.at[vj[d], :, mine], g_v.at[vj[d], :, mine], partner))
+    views = [g_v.at[vj[d], :, mine] for d in DIRS]
+    f_g = Fan([(view, view, partner) for view in views], g_v.at[pl.ds(0, 3), :, first_half])
     start = [entering(tt_v, False, *states)]
     for c in range(nblk):
         start.append(start[c] * dec[c] + up[c])
@@ -575,11 +608,11 @@
     mix = jnp.concatenate(mixed, axis=0)
     r2 = lax.rsqrt(jnp.sum(mix * mix, axis=1, keepdims=True) / VC + EPS)
     normal = mix * r2
-    arrived(f_g)
-    arrived(t_gge)
+    f_g.wait_recv()
+    t_gge.wait_recv()
     wg_all = g_v[...].reshape(W * 64, D)
     gate = nt(normed, wg_all)
-    gg = gge_v[...].astype(F32).reshape(W * 64, 128).T[:1]
+    gg = jnp.concatenate([gge_v[h].astype(F32)[0:1, 0:64] for h in range(W)], axis=1)
     sig = 1.0 / (1.0 + jnp.exp(-gate))
     act = gate * sig
     act_v[0] = act
@@ -595,6 +628,10 @@
         ra = lax.rsqrt(jnp.sum(xa * xa, axis=1, keepdims=True) / D + EPS)
         n_all[at, :] = (xa * ra * g1).astype(BF)
     xr_v[...] = (x * (r1 * r1 * r1)).astype(BF).T
+    low_all = jnp.where(
+        lax.broadcasted_iota(jnp.int32, (rows, 128), 1) == 16, 1.0, nt(n_all[...], dd_v[...])
+    )
+    lall_v[...] = low_all.astype(BF)
     t_ob2.step(0)
     t_ob2.step(1)
     f_f += t_fg.step()
@@ -639,52 +676,71 @@
     part = nn(ggate, gT) + nn(gup, uT)
     p_v[...] = part
     sst[...] = as_row(jnp.sum(resid * g3 * part, axis=1, keepdims=True))
-    t_m3 = [send(sst, rst.at[d], vdev[d]) for d in DIRS]
+    t_m3 = Fan([(sst, rst.at[d], vdev[d]) for d in DIRS], rst.at[pl.ds(1, 3)])
     ggp = nt((part * g3).astype(BF), o_v[...].reshape(W * W * 64, D))
     for h in range(W):
         sgg[h] = ggp[:, h * VC : (h + 1) * VC].astype(BF)
-    t_gg = LineSum(lambda to: sgg.at[to], rgg.at[0], rgg.at[1], rgg.at[pl.ds(2, 2)], cgg)
+    halves = [pl.ds(n * T // 2, T // 2) for n in range(2)]
+    t_gg = [
+        LineSum(
+            lambda to, at=at: sgg.at[to, at],
+            rgg.at[0, at],
+            rgg.at[1, at],
+            rgg.at[pl.ds(2, 2), at],
+            cgg.at[:, at],
+        )
+        for at in halves
+    ]
+    for line in t_gg:
+        line.rest()
     hd[...] = hid.T.reshape(W, FB, T)
-    t_hd = [send(hd.at[ki[d]], hseg.at[i], kdev[d]) for d in DIRS]
+    t_hd = Fan([(hd.at[ki[d]], hseg.at[i], kdev[d]) for d in DIRS], hseg.at[pl.ds(0, 3)])
     hseg[i] = hd[i]
 
-    t_gg.step(0)
-
-    t_pre = []
-    for n, grad in enumerate((ggate, gup)):
+    def weight_part(n, grad):
         gw[n] = tn(grad, fin).astype(BF).reshape(W, FB, D)
-        t_pre.append(send(gw.at[n, :, :, other], pre.at[n], partner))
+        return send(gw.at[n, :, :, other], pre.at[n], partner)
+
+    def settle(n, move):
+        move.wait_recv()
+        pres[n] = (gw[n, :, :, mine].astype(F32) + pre[n].astype(F32)).astype(BF)
+
+    def square(n):
+        return SquareSum(
+            lambda to, at: pres.at[n, to, :, at], rfw.at[n], qfw.at[n], cfw.at[n]
+        )
+
+    t_pre0 = weight_part(0, ggate)
 
     feature = lax.broadcasted_iota(jnp.int32, (1, D), 1)
     own_slab = jnp.where(lax.rem(feature // 64, W) == j, 1.0, 0.0)
     own_run = jnp.where(feature // (D // W) == j, 1.0, 0.0)
-    so[...] = (nn(hid, dn) + own_slab * resid).astype(BF).T.reshape(W, W, 64, T)
-    t_gg.step(1)
-    t_out = LineSum(lambda to: so.at[:, to], ro.at[0], ro.at[1], ro.at[pl.ds(2, 2)], co)
-    ffn_gain = jnp.sum(part * resid * r3, axis=0, keepdims=True)
-
-    def settle(n):
-        t_pre[n].wait_recv()
-        pres[n] = (gw[n, :, :, mine].astype(F32) + pre[n].astype(F32)).astype(BF)
-        return SquareSum(
-            lambda to, at: pres.at[n, to, :, at], rfw.at[n], qfw.at[n], cfw.at[n]
-        )
-
-    t_fw = [settle(0)]
-
-    arrived(t_m3)
+    t_m3.wait_recv()
     m3 = as_column(sst[...] + rst[1] + rst[2] + rst[3]) / D
     base = c_v[...].astype(F32) - resid * (r3 * r3 * r3 * m3)
+    t_gg[0].step(0)
     direct = nt(base.astype(BF), o_v[j].reshape(W * 64, D))
     full = p_v[...] * (g3 * r3)
     mixed_in = (full + own_run * base).astype(BF)
     for h in range(W):
         gow[h] = tn(ga_v[h], mixed_in).astype(BF)
     t_po = send(gow.at[:, :, other], preo, partner)
-    t_out.step(0)
-    t_gg.collect()
-
-    ggs = t_gg.total()
+    t_gg[0].step(1)
+    settle(0, t_pre0)
+    t_fw0 = square(0)
+    so[...] = (nn(hid, dn) + own_slab * resid).astype(BF).T.reshape(W, W, 64, T)
+    t_gg[1].step(0)
+    t_out = LineSum(lambda to: so.at[:, to], ro.at[0], ro.at[1], ro.at[pl.ds(2, 2)], co).rest()
+    ffn_gain = jnp.sum(part * resid * r3, axis=0, keepdims=True)
+    t_gg[1].step(1)
+    t_pre1 = weight_part(1, gup)
+    t_po.wait_recv()
+    preso[...] = (gow[:, :, mine].astype(F32) + preo[...].astype(F32)).astype(BF)
+    t_fw0.step()
+    for line in t_gg:
+        line.collect()
+
+    ggs = jnp.concatenate([line.total() for line in t_gg], axis=0)
     ggrad = direct + r3 * ggs
     act = act_v[0]
     normal = act_v[2]
@@ -700,24 +756,21 @@
         bloc = bloc * dec[c] + qst[c]
     bst_v[i, :VC] = bloc.astype(BF)
     bst_v[i, VC:] = jnp.broadcast_to(locd, (16, 128)).astype(BF)
-    t_bst = [send(bst_v.at[i], bst_v.at[i], kdev[d]) for d in DIRS]
+    t_bst = Fan([(bst_v.at[i], bst_v.at[i], kdev[d]) for d in DIRS], bst_v.at[pl.ds(0, 3)])
+    t_ow = SquareSum(lambda to, at: preso.at[to, :, at], rowk, qow, cow)
     vz[1] = dgate.T.reshape(W, 64, T)
-    t_gz = [send(vz.at[1, vj[d]], zvg.at[1, j], vdev[d]) for d in DIRS]
-    t_fw.append(settle(1))
-    t_out.step(1)
-    t_fw[0].step()
-    dscore, dq_in, dk_in, dv_in = [], [], [], []
+    t_gz = Fan([(vz.at[1, vj[d]], zvg.at[1, j], vdev[d]) for d in DIRS], zvg.at[1, pl.ds(0, 3)])
+    dq_in, dk_in, dv_in = [], [], []
     for c in range(nblk):
         ds = jnp.where(causal, nt(gmix[blk[c]], v[blk[c]]), 0.0).astype(BF)
         dq_in.append(nn(ds, kd[c]) + em[c] * nn(gmix[blk[c]], start_low[c]))
         dk_in.append(tn(ds, qd[c]))
         dv_in.append(tn(score[c], gmix[blk[c]]))
-    t_po.wait_recv()
-    preso[...] = (gow[:, :, mine].astype(F32) + preo[...].astype(F32)).astype(BF)
-    arrived(t_bst)
+    settle(1, t_pre1)
+    t_bst.wait_recv()
     after = [None] * nblk
     states = gather_states(bst_v, btt_v, True)
-    t_fw[1].step()
+    t_out.step(0)
     after[nblk - 1] = entering(btt_v, True, *states)
     for c in range(nblk - 2, -1, -1):
         after[c] = after[c + 1] * dec[c + 1] + qst[c + 1]
@@ -741,11 +794,12 @@
     vl = jnp.concatenate(vl, axis=0)
     ga = jnp.concatenate(ga, axis=0).astype(BF)
     vz[0] = vl.T.reshape(W, 64, T)
-    t_vz = [send(vz.at[0, vj[d]], zvg.at[0, j], vdev[d]) for d in DIRS]
+    t_vz = Fan([(vz.at[0, vj[d]], zvg.at[0, j], vdev[d]) for d in DIRS], zvg.at[0, pl.ds(0, 3)])
     qka[:, 0] = ql.T.reshape(W, 32, T)
     qka[:, 1] = kl.T.reshape(W, 32, T)
     qka[:, 2] = ga.T.reshape(W, 32, T)
-    t_qa = [send(qka.at[ki[d]], kqa.at[i], kdev[d]) for d in DIRS]
+    t_qa = Fan([(qka.at[ki[d]], kqa.at[i], kdev[d]) for d in DIRS], kqa.at[pl.ds(0, 3)])
+    t_out.step(1)
     glr = nn(ga, ext_all).astype(BF)
     gn = nn(ql, wq_all) + nn(kl, wk_all) + nn(vl, wv_all) + nn(dgate, wg_all) + nn(glr, dd_v[...])
     x = x_v[...].astype(F32)
@@ -763,27 +817,40 @@
         if h == 0:
             rest = jnp.where(rid == 2, group, rest)
         sm0[h, 16:32] = rest.astype(BF)
-    t_s0 = [send(sm0.at[vj[d]], sm1.at[d], vdev[d]) for d in DIRS]
+    t_s0 = Fan([(sm0.at[vj[d]], sm1.at[d], vdev[d]) for d in DIRS], sm1.at[pl.ds(1, 3)])
     whole = gn * (r1 * g1) + full + own_slab * base
     sgn[...] = whole.astype(BF).T.reshape(W, W, 64, T)
-    t_gn = LineSum(lambda to: sgn.at[:, to], rgn.at[0], rgn.at[1], rgn.at[pl.ds(2, 2)], cgn)
-    t_ow = SquareSum(lambda to, at: preso.at[to, :, at], rowk, qow, cow)
+    pairs = [pl.ds(n * W // 2, W // 2) for n in range(2)]
+    t_gn = [
+        LineSum(
+            lambda to, at=at: sgn.at[at, to],
+            rgn.at[0, at],
+            rgn.at[1, at],
+            rgn.at[pl.ds(2, 2), at],
+            cgn.at[:, at],
+        )
+        for at in pairs
+    ]
+    for line in t_gn:
+        line.rest()
+    t_ow.step()
+    t_fw1 = square(1)
 
     t_out.collect()
     ao[...] = t_out.total().astype(BF)
-    t_ao = [send(ao.at[ki[d]], oseg.at[i], kdev[d]) for d in DIRS]
+    t_ao = Fan([(ao.at[ki[d]], oseg.at[i], kdev[d]) for d in DIRS], oseg.at[pl.ds(0, 3)])
     oseg[i] = ao[i]
 
-    arrived(t_hd)
+    t_gz.wait_recv()
+    zvg[1, j] = vz[1, j]
+    t_gk = Fan([(zvg.at[1, ki[d]], kvg.at[1, i], kdev[d]) for d in DIRS], kvg.at[1, pl.ds(0, 3)])
+    kvg[1, i] = zvg[1, i]
+
+    t_hd.wait_recv()
     dsum[0] = nn(lanes(hseg[...]), c_all[...]).astype(BF)
     t_ds = send(dsum.at[0], dsum.at[1], partner)
 
-    arrived(t_gz)
-    zvg[1, j] = vz[1, j]
-    t_gk = [send(zvg.at[1, ki[d]], kvg.at[1, i], kdev[d]) for d in DIRS]
-    kvg[1, i] = zvg[1, i]
-
-    arrived(t_s0)
+    t_s0.wait_recv()
     sm2[0] = total(sm0[j], sm1).astype(BF)
     m1 = (
         sm0[0, 19:20].astype(F32)
@@ -791,100 +858,108 @@
         + sm1[2, 19:20].astype(F32)
         + sm1[3, 19:20].astype(F32)
     ) / D
-    t_s1 = [send(sm2.at[0], sm2.at[d], kdev[d]) for d in DIRS]
-    t_gn.step(0)
-    arrived(t_vz)
+    t_s1 = Fan([(sm2.at[0], sm2.at[d], kdev[d]) for d in DIRS], sm2.at[pl.ds(1, 3)])
+    t_vz.wait_recv()
     zvg[0, j] = vz[0, j]
-    t_vk = [send(zvg.at[0, ki[d]], kvg.at[0, i], kdev[d]) for d in DIRS]
+    t_vk = Fan([(zvg.at[0, ki[d]], kvg.at[0, i], kdev[d]) for d in DIRS], kvg.at[0, pl.ds(0, 3)])
     kvg[0, i] = zvg[0, i]
-    t_gn.step(1)
-    t_ow.step()
-
-    arrived(t_qa)
+    t_gn[0].step(0)
+    t_gn[0].step(1)
+    t_fw1.step()
+    t_gn[1].step(0)
+    t_gn[1].step(1)
+
+    t_ow.collect()
+    mid_o[...] = t_ow.total().astype(BF).reshape(W, 64, half)
+    t_oz = LineSum(
+        lambda to: mid_o.at[to], rowz.at[0], rowz.at[1], rowz.at[pl.ds(2, 2)], coz
+    ).rest()
+
+    t_qa.wait_recv()
     kqa[i] = qka[i]
     nall = n_all[...]
     for n in range(2):
         qksum[0, n] = nn(lanes(kqa[:, n]), nall).astype(BF)
-    low_all = jnp.where(
-        lax.broadcasted_iota(jnp.int32, (rows, 128), 1) == 16, 1.0, nt(nall, dd_v[...])
-    )
-    esum[0] = nn(lanes(kqa[:, 2]), low_all.astype(BF))
+    esum[0] = nn(lanes(kqa[:, 2]), lall_v[...])
     t_qs = send(qksum.at[0], qksum.at[1], partner)
     t_es = send(esum.at[0], esum.at[1], partner)
 
-    for n in range(2):
-        t_fw[n].collect()
-        fin_f[par, n] = t_fw[n].total().astype(BF)
-    t_ff = send(fin_f.at[par], fin_f.at[par], partner)
-    arrived(t_s1)
+    t_s1.wait_recv()
     sm3[0] = total(sm2[0], sm2).astype(BF)
     t_s2 = send(sm3.at[0], sm3.at[1], partner)
 
-    arrived(t_gk + t_vk)
+    def finish_square(n, line):
+        line.collect()
+        fin_f[par, n] = line.total().astype(BF)
+        return send(fin_f.at[par, n], fin_f.at[par, n], partner)
+
+    t_ff = [finish_square(0, t_fw0)]
+
+    t_gk.wait_recv()
+    t_vk.wait_recv()
     for n in range(2):
         vgsum[0, n] = nn(lanes(kvg[n]), nall).astype(BF)
     t_vs = send(vgsum.at[0], vgsum.at[1], partner)
     t_s2.wait_recv()
     sm4[j] = (sm3[0].astype(F32) + sm3[1].astype(F32)).astype(BF)
-    t_s3 = [send(sm4.at[j], sm4.at[j], vdev[d]) for d in DIRS]
-
-    t_ow.collect()
-    mid_o[...] = t_ow.total().astype(BF).reshape(W, 64, half)
-    t_oz = [send(mid_o.at[vj[d]], rowz.at[d], vdev[d]) for d in DIRS]
-
-    t_gn.collect()
-    summed = t_gn.total()
+    t_s3 = Fan([(sm4.at[j], sm4.at[j], vdev[d]) for d in DIRS], sm4.at[pl.ds(0, 3)])
+
+    for line in t_gn:
+        line.collect()
+    summed = jnp.concatenate([line.total() for line in t_gn], axis=0)
     for h in range(W):
         at = pl.ds(pl.multiple_of((h * W + j) * 64, 64), 64)
         ai[h] = (summed[h] - xr_v[at, :].astype(F32) * m1).astype(BF)
-    t_ai = [send(ai.at[ki[d]], iseg.at[i], kdev[d]) for d in DIRS]
+    t_ai = Fan([(ai.at[ki[d]], iseg.at[i], kdev[d]) for d in DIRS], iseg.at[pl.ds(0, 3)])
     iseg[i] = ai[i]
-
-    outs = []
+    t_oz.step(0)
+    t_oz.step(1)
+    t_ff.append(finish_square(1, t_fw1))
+
     t_ds.wait_recv()
-    left(t_ds)
-    dsum[0] = (dsum[0].astype(F32) + dsum[1].astype(F32)).astype(BF)
-    outs.append(load(dsum.at[0], o_d))
+    r_fd[...] = dsum[0].astype(F32) + dsum[1].astype(F32)
+    t_ao.wait_recv()
+    r_out[...] = lanes(oseg[...])
     t_qs.wait_recv()
+    r_q[...] = qksum[0, 0].astype(F32) + qksum[1, 0].astype(F32)
+    r_k[...] = qksum[0, 1].astype(F32) + qksum[1, 1].astype(F32)
     t_es.wait_recv()
-    left(t_qs)
-    left(t_es)
-    qksum[0] = (qksum[0].astype(F32) + qksum[1].astype(F32)).astype(BF)
-    esum[0] = esum[0] + esum[1]
-    outs.append(load(qksum.at[0], o_qk))
-    outs.append(load(esum.at[0], o_ext))
-    t_ff.wait_recv()
-    outs.append(load(fin_f, o_f))
+    decay = (esum[0] + esum[1]).T
+    r_du[...] = decay[0:16, :].reshape(16, 1, 32)
+    r_db[...] = decay[16:17, :]
     t_vs.wait_recv()
-    left(t_vs)
-    vgsum[0] = (vgsum[0].astype(F32) + vgsum[1].astype(F32)).astype(BF)
-    outs.append(load(vgsum.at[0], o_vg))
-    arrived(t_s3)
+    r_v[...] = vgsum[0, 0].astype(F32) + vgsum[1, 0].astype(F32)
+    r_g[...] = vgsum[0, 1].astype(F32) + vgsum[1, 1].astype(F32)
+    t_ff[0].wait_recv()
+    for h in range(2):
+        r_fg[:, h * half : (h + 1) * half] = fin_f[h, 0].astype(F32)
+    t_oz.collect()
+    fin_ow[par] = t_oz.total().astype(BF)
+    t_fo = send(fin_ow.at[par], fin_ow.at[par], partner)
+    t_ff[1].wait_recv()
+    for h in range(2):
+        r_fu[:, h * half : (h + 1) * half] = fin_f[h, 1].astype(F32)
+    t_s3.wait_recv()
     for h in range(W):
         pick[:, h * T : (h + 1) * T] = sm4[h].astype(F32)
     pair = i * W + j
-    small_v[...] = jnp.zeros_like(small_v)
-    small_v[0:1, :] = pick[pl.ds(pair, 1), :]
+    r_dd[...] = pick[pl.ds(pair, 1), :]
     wide = pick[16:24, :]
     slab = D // (W * W)
     chosen = jnp.zeros((8, slab), F32)
     for n in range(W * W):
         chosen = jnp.where(pair == n, wide[:, n * slab : (n + 1) * slab], chosen)
+    r_ng[...] = chosen[0:1]
+    r_fn[...] = chosen[1:2]
+    chosen = jnp.zeros((8, 64), F32)
     for n in range(W):
-        group_slab = jnp.where(j == n, wide[2:3, n * 64 : (n + 1) * 64], 0.0)
-        small_v[3:4, 0:64] = small_v[3:4, 0:64] + group_slab
-    small_v[1:3, 0:slab] = chosen[0:2]
-    outs.append(load(small_v, o_small))
-    arrived(t_oz)
-    fin_ow[par] = total(mid_o[j], rowz).astype(BF)
-    t_fo = send(fin_ow.at[par], fin_ow.at[par], partner)
-    arrived(t_ai)
-    outs.append(load(iseg, o_in))
-    arrived(t_ao)
-    outs.append(load(oseg, o_out))
+        chosen = jnp.where(j == n, wide[:, n * 64 : (n + 1) * 64], chosen)
+    r_gg[...] = chosen[2:3]
+    t_ai.wait_recv()
+    r_in[...] = lanes(iseg[...])
     t_fo.wait_recv()
-    outs.append(load(fin_ow, o_ow))
-    here(outs)
+    for h in range(2):
+        r_o[:, h * half : (h + 1) * half] = fin_ow[h].astype(F32)
     for cp in sent:
         cp.wait_send()
 
@@ -899,8 +974,8 @@
             cp.wait_send()
 
 
-N_REMOTE = 172
-N_LOCAL = 27
+N_REMOTE = 150
+N_LOCAL = 18
 
 
 def layer(n_seq, args):
@@ -911,22 +986,30 @@
     VC = W * 64
     half = D // 2
 
-    def sds(shape, dtype=BF):
-        return jax.ShapeDtypeStruct(shape, dtype)
+    def sds(shape, dtype=F32):
+        return pltpu.VMEM(shape, dtype)
 
     def vm(shape, dtype=BF):
         return pltpu.VMEM(shape, dtype)
 
+    slab = D // (W * W)
     outs = [
-        sds((W, 64, T)),
-        sds((W, 64, T)),
-        sds((2, 2, FB, half)),
+        sds((64, rows), BF),
+        sds((64, rows), BF),
+        sds((1, slab)),
+        sds((32, D)),
+        sds((32, D)),
+        sds((64, D)),
+        sds((64, D)),
+        sds((1, D)),
+        sds((16, 1, 32)),
+        sds((1, 32)),
+        sds((1, 64)),
+        sds((64, D)),
+        sds((1, slab)),
         sds((FB, D)),
-        sds((2, 64, D)),
-        sds((2, 32, D)),
-        sds((32, 128), F32),
-        sds((2, 64, half)),
-        sds((8, D), F32),
+        sds((FB, D)),
+        sds((FB, D)),
     ]
     scratch = [
         vm((T, D)),
@@ -948,7 +1031,7 @@
         vm((W, 32, 128)),
         vm((W, 64, D)),
         vm((W, 64, D)),
-        vm((W, 64, 128)),
+        vm((W, 16, 128)),
         vm((W, W, 64, D)),
         vm((3, W, FB, D)),
         vm((W, VC + 16, 128)),
@@ -990,6 +1073,7 @@
         vm((W, 64, half)),
         vm((W, 64, half)),
         vm((2, 64, half)),
+        vm((2, 64, half)),
         vm((2, W, 64, T)),
         vm((2, W, 64, T)),
         vm((2, W, 64, T)),
@@ -1004,7 +1088,7 @@
         vm((2, 32, T)),
         vm((W, 32, T)),
         vm((32, D), F32),
-        vm((8, D), F32),
+        vm((rows, 128)),
         vm((T, W * FB), F32),
         vm((3, T, VC), F32),
         vm((T, D), F32),
@@ -1016,7 +1100,7 @@
         functools.partial(layer_kernel, n_seq),
         out_shape=outs,
         in_specs=[pl.BlockSpec(memory_space=pl.ANY)] * len(args),
-        out_specs=[pl.BlockSpec(memory_space=pl.ANY)] * len(outs),
+        out_specs=[pl.BlockSpec(memory_space=pltpu.VMEM)] * len(outs),
         scratch_shapes=scratch,
         compiler_params=pltpu.CompilerParams(
             collective_id=0, has_side_effects=True, vmem_limit_bytes=60 * 2**20
@@ -1026,83 +1110,23 @@
 
 
 def finish_kernel(*refs):
-    n_in = 9
-    parts, rest = refs[:n_in], refs[n_in:]
-    results, held, sem = rest[:16], rest[16:-1], rest[-1]
-    copies = [pltpu.make_async_copy(a, b, sem.at[n]) for n, (a, b) in enumerate(zip(parts, held))]
+    n = len(refs) // 2
+    sem = refs[-1]
+    copies = [pltpu.make_async_copy(refs[k], refs[n + k], sem.at[k]) for k in range(n)]
     for cp in copies:
         cp.start()
-    o_out, o_in, o_f, o_d, o_vg, o_qk, o_ext, o_ow, o_small = held
-    (r_out, r_in, r_ng, r_q, r_k, r_v, r_g, r_dd, r_du, r_db, r_gg, r_o, r_fn, r_fg, r_fu, r_fd) = results
-    T = o_out.shape[2]
-    half = o_f.shape[3]
-    copies[3].wait()
-    r_fd[...] = o_d[...].astype(F32)
-    copies[2].wait()
-    for h in range(2):
-        at = slice(h * half, (h + 1) * half)
-        r_fg[:, at] = o_f[h, 0].astype(F32)
-        r_fu[:, at] = o_f[h, 1].astype(F32)
-    copies[4].wait()
-    r_v[...] = o_vg[0].astype(F32)
-    r_g[...] = o_vg[1].astype(F32)
-    copies[5].wait()
-    r_q[...] = o_qk[0].astype(F32)
-    r_k[...] = o_qk[1].astype(F32)
-    copies[7].wait()
-    for h in range(2):
-        r_o[:, h * half : (h + 1) * half] = o_ow[h].astype(F32)
-    copies[0].wait()
-    copies[1].wait()
-    for n in range(WAYS):
-        r_out[:, n * T : (n + 1) * T] = o_out[n]
-        r_in[:, n * T : (n + 1) * T] = o_in[n]
-    copies[8].wait()
-    r_dd[...] = o_small[0:1, :]
-    r_ng[...] = o_small[1:2, 0 : r_ng.shape[1]]
-    r_fn[...] = o_small[2:3, 0 : r_fn.shape[1]]
-    r_gg[...] = o_small[3:4, 0:64]
-    copies[6].wait()
-    decay = o_ext[...].T
-    r_du[...] = decay[0:16, :].reshape(16, 1, 32)
-    r_db[...] = decay[16:17, :]
+    for cp in copies:
+        cp.wait()
 
 
 def finish(parts):
-    rows = parts[0].shape[0] * parts[0].shape[2]
-    D = parts[3].shape[1]
-    FB = parts[3].shape[0]
-    slab = D // (WAYS * WAYS)
-
-    def sds(shape, dtype=F32):
-        return jax.ShapeDtypeStruct(shape, dtype)
-
-    outs = [
-        sds((64, rows), BF),
-        sds((64, rows), BF),
-        sds((1, slab)),
-        sds((32, D)),
-        sds((32, D)),
-        sds((64, D)),
-        sds((64, D)),
-        sds((1, D)),
-        sds((16, 1, 32)),
-        sds((1, 32)),
-        sds((1, 64)),
-        sds((64, D)),
-        sds((1, slab)),
-        sds((FB, D)),
-        sds((FB, D)),
-        sds((FB, D)),
-    ]
     return pl.pallas_call(
         finish_kernel,
-        out_shape=outs,
-        in_specs=[pl.BlockSpec(memory_space=pl.ANY)] * len(parts),
-        out_specs=[pl.BlockSpec(memory_space=pltpu.VMEM)] * len(outs),
-        scratch_shapes=[pltpu.VMEM(p.shape, p.dtype) for p in parts]
-        + [pltpu.SemaphoreType.DMA((len(parts),))],
-        compiler_params=pltpu.CompilerParams(vmem_limit_bytes=60 * 2**20),
+        out_shape=[jax.ShapeDtypeStruct(p.shape, p.dtype) for p in parts],
+        in_specs=[pl.BlockSpec(memory_space=pltpu.VMEM)] * len(parts),
+        out_specs=[pl.BlockSpec(memory_space=pl.ANY)] * len(parts),
+        scratch_shapes=[pltpu.SemaphoreType.DMA((len(parts),))],
+        compiler_params=pltpu.CompilerParams(vmem_limit_bytes=16 * 2**20),
         name="finish",
     )(*parts)
 

time: 102 us -> 95.1 us (0.932)
  Pallas kernels: 100 us -> 94 us
    pallas_call x1, Pallas kernels: 96.8 us -> 92 us  [layer(): pl.pallas_call(functools.partial(layer_kernel, n_seq), out_shape=outs, in...]
    pallas_call x1, Pallas kernels: 3.46 us -> 1.95 us  [finish(): pl.pallas_call(finish_kernel, out_shape=[jax.ShapeDtypeStruct(p.shape, p....]
where the time goes in v4:
time: 95.1 us; the launch traced here: 94.8 us
  Pallas kernels  94 us (99%)
    pallas_call x1, Pallas kernels, layer(): pl.pallas_call(functools.partial(layer_kernel, n_seq), out_shape=outs, in...  92 us
    pallas_call x1, Pallas kernels, finish(): pl.pallas_call(finish_kernel, out_shape=[jax.ShapeDtypeStruct(p.shape, p....  1.95 us

profile of v4, /device:TPU:0, one launch (start us, length us, event | category | flops | bytes accessed | tf_op | source)
XLA Modules:
  0.0 94.8 jit_solution(2544352188360738760)
XLA Ops:
  0.7 92.0 %layer.1 = (bf16[64,1024]{1,0:T(8,128)(2,1)S(1)}, bf16[64,1024]{1,0:T(8,128)(2,1)S(1)}, f32[1,64]{1,0:T(1,128)S(1)}, f32[32,1024]{1,0:T(8,128)S(1)}, f32[32,1024...) custom-call(bf16[1024,1024]{1,0:T(8,128)(2,1)} %tok.1, ...), custom_call_target="tpu_custom_call" | custom-call | tf_op jit(solution)/shard_map/layer/pallas_call | solution.py:1099
  92.7 1.9 %finish.1 = (bf16[64,1024]{1,0:T(8,128)(2,1)}, bf16[64,1024]{1,0:T(8,128)(2,1)}, f32[1,64]{1,0:T(1,128)}, f32[32,1024]{1,0:T(8,128)}, f32[32,1024]{1,0:T(8,128)}...) custom-call(bf16[64,1024]{1,0:T(8,128)(2,1)S(1)} %get-tuple-element., ...), custom_call_target="tpu_custom_call" | custom-call | tf_op jit(solution)/shard_map/finish/pallas_call | solution.py:1123

commit v5 on v4

--- a/solution.py
+++ b/solution.py
@@ -173,8 +173,6 @@
     sm1,
     sm2,
     sm3,
-    sm4,
-    pick,
     lall_v,
     gh_v,
     act_v,
@@ -203,61 +201,50 @@
     vj = [None] + [xor(j, d) for d in DIRS]
     seqdev = [{"seq": lax.rem(s + e, n_seq)} for e in range(1, n_seq)]
 
-    count = [0, 0]
-    sent = []
-
-    def slot():
-        count[0] += 1
-        return count[0] - 1
-
-    def remote(src, dst, dev, to=None):
-        n = slot()
+    count = [0, 0, 0]
+    sent, inner_sent, outer_sent = [], [], []
+
+    def slot(kind):
+        count[kind] += 1
+        return count[kind] - 1
+
+    def out_slot():
+        return slot(0)
+
+    def in_slot():
+        return slot(1)
+
+    def copy(src, dst, dev, n, m):
         return pltpu.make_async_remote_copy(
             src_ref=src,
             dst_ref=dst,
             send_sem=ss.at[n],
-            recv_sem=rs.at[n if to is None else to],
+            recv_sem=rs.at[m],
             device_id=dev,
             device_id_type=MESH,
         )
 
     def send(src, dst, dev):
-        cp = remote(src, dst, dev)
+        cp = copy(src, dst, dev, out_slot(), in_slot())
         cp.start()
         sent.append(cp)
         return cp
 
     def load(src, dst):
-        n = count[1]
-        count[1] += 1
-        cp = pltpu.make_async_copy(src, dst, ls.at[n])
+        cp = pltpu.make_async_copy(src, dst, ls.at[slot(2)])
         cp.start()
         return cp
 
     class Fan:
         def __init__(self, copies, size):
-            n = slot()
-
-            def one(src, dst, dev):
-                return pltpu.make_async_remote_copy(
-                    src_ref=src,
-                    dst_ref=dst,
-                    send_sem=ss.at[n],
-                    recv_sem=rs.at[n],
-                    device_id=dev,
-                    device_id_type=MESH,
-                )
-
+            n, m = out_slot(), in_slot()
             for src, dst, dev in copies:
-                one(src, dst, dev).start()
-            self.all = one(size, size, partner)
-            sent.append(self)
+                copy(src, dst, dev, n, m).start()
+            self.all = copy(size, size, partner, n, m)
+            sent.append(self.all)
 
         def wait_recv(self):
             self.all.wait_recv()
-
-        def wait_send(self):
-            self.all.wait_send()
 
     def arrived(copies):
         for cp in copies:
@@ -268,33 +255,24 @@
             cp.wait()
 
     inner = lax.rem(j + 1, W) >= 2
-    inner_sent = []
-    outer_sent = []
 
     class LineGather:
-        def __init__(self, view):
-            a, b, c = slot(), slot(), slot()
-            self.near = remote(view(j), view(j), vdev[1], a)
-            self.near.start()
-            sent.append(self.near)
-            across = remote(view(j), view(j), vdev[3], c)
+        def __init__(self, view, four):
+            a, b, c = in_slot(), in_slot(), in_slot()
+            n, m = out_slot(), out_slot()
+            near = copy(view(j), view(j), vdev[1], n, a)
+            near.start()
+            sent.append(near)
+            across = copy(view(j), view(j), vdev[3], m, c)
             self.got = [
-                pltpu.make_async_remote_copy(
-                    src_ref=view(vj[d]),
-                    dst_ref=view(vj[d]),
-                    send_sem=ss.at[n],
-                    recv_sem=rs.at[n],
-                    device_id=vdev[1],
-                    device_id_type=MESH,
-                )
-                for d, n in zip(DIRS, (a, b, c))
+                copy(view(vj[d]), view(vj[d]), vdev[1], n, at) for d, at in zip(DIRS, (a, b, c))
             ]
             self.on = [
-                remote(view(vj[1]), view(vj[1]), vdev[3], b),
-                remote(view(vj[3]), view(vj[3]), vdev[1], b),
-                remote(view(vj[2]), view(vj[2]), vdev[1], c),
+                copy(view(vj[1]), view(vj[1]), vdev[3], m, b),
+                copy(view(vj[3]), view(vj[3]), vdev[1], m, b),
+                copy(view(vj[2]), view(vj[2]), vdev[1], m, c),
             ]
-            inner_sent.extend([across] + self.on)
+            inner_sent.append(copy(four, four, vdev[1], m, a))
 
             @pl.when(inner)
             def _():
@@ -312,36 +290,34 @@
                 arrived(self.got)
 
     class LineSum:
-        def __init__(self, part, near, far, relay, summed):
-            self.part, self.near, self.far, self.relay, self.summed = part, near, far, relay, summed
-            b = slot()
+        def __init__(self, part, both, relay, summed):
+            self.part, self.both, self.relay, self.summed = part, both, relay, summed
+            a, b, c = in_slot(), in_slot(), in_slot()
+            n, m, o = out_slot(), out_slot(), out_slot()
             self.first = [
-                remote(part(vj[3]), relay.at[0], vdev[1]),
-                remote(part(vj[2]), relay.at[1], vdev[1]),
+                copy(part(vj[3]), relay.at[0], vdev[1], n, a),
+                copy(part(vj[2]), relay.at[1], vdev[1], n, b),
             ]
-            outer_sent.extend(self.first)
-
-            @pl.when(jnp.logical_not(inner))
-            def _():
-                for cp in self.first:
-                    cp.start()
-
-            self.second = [
-                remote(summed.at[0], far, vdev[2], b),
-                remote(summed.at[1], far, vdev[3], b),
-            ]
-            inner_sent.extend(self.second)
-            self.last = pltpu.make_async_remote_copy(
-                src_ref=far,
-                dst_ref=far,
-                send_sem=ss.at[b],
-                recv_sem=rs.at[b],
-                device_id=vdev[1],
-                device_id_type=MESH,
-            )
+            self.direct = copy(part(vj[1]), both.at[0], vdev[1], m, c)
+            self.second = [copy(summed.at[k], both.at[1], vdev[2 + k], o, c) for k in range(2)]
+            self.all = copy(both, both, vdev[1], m, c)
+            outer_sent.append(copy(relay, relay, vdev[1], n, a))
+            sent.append(self.direct)
+            inner_sent.append(copy(summed, summed, vdev[1], o, a))
+
+        def go(self, n):
+            if n < 2:
+
+                @pl.when(jnp.logical_not(inner))
+                def _():
+                    self.first[n].start()
+
+            elif n == 2:
+                self.direct.start()
 
         def rest(self):
-            self.direct = send(self.part(vj[1]), self.near, vdev[1])
+            for n in range(3):
+                self.go(n)
             return self
 
         def step(self, n):
@@ -353,24 +329,25 @@
                 self.second[n].start()
 
         def collect(self):
-            self.direct.wait_recv()
-            self.last.wait_recv()
+            self.all.wait_recv()
 
         def total(self):
             out = self.part(j)[...].astype(F32)
-            return out + self.near[...].astype(F32) + self.far[...].astype(F32)
+            return out + self.both[0].astype(F32) + self.both[1].astype(F32)
 
     class SquareSum:
         def __init__(self, part, got, relay, summed):
             self.part, self.got, self.relay, self.summed = part, got, relay, summed
             q = got.shape[-1] // 2
             self.at = [pl.ds(0, q), pl.ds(q, q)]
-            self.first = [
-                send(self.half(ki[3], n), relay.at[n], kdev[1 + n]) for n in range(2)
-            ]
-            self.direct = [
-                send(self.half(ki[1 + n], n), self.into(n, n), kdev[1 + n]) for n in range(2)
-            ]
+            a, self.into_slot = in_slot(), in_slot()
+            n, self.out = out_slot(), out_slot()
+            for k in range(2):
+                copy(self.half(ki[3], k), relay.at[k], kdev[1 + k], n, a).start()
+            for k in range(2):
+                copy(self.half(ki[1 + k], k), self.into(k, k), kdev[1 + k], n, self.into_slot).start()
+            self.relayed = copy(relay, relay, kdev[1], n, a)
+            sent.append(copy(got, got, kdev[1], n, a))
 
         def half(self, target, n):
             return self.part(target, self.at[n])
@@ -379,21 +356,54 @@
             return self.got.at[n, :, self.at[h]]
 
         def step(self):
-            self.second = []
-            for n in range(2):
-                self.first[n].wait_recv()
-                own = self.half(ki[2 - n], n)[...].astype(F32)
-                self.summed[n] = (own + self.relay[n].astype(F32)).astype(BF)
-                self.second.append(
-                    send(self.summed.at[n], self.into(1 - n, n), kdev[2 - n])
-                )
+            self.relayed.wait_recv()
+            for k in range(2):
+                own = self.half(ki[2 - k], k)[...].astype(F32)
+                self.summed[k] = (own + self.relay[k].astype(F32)).astype(BF)
+                copy(
+                    self.summed.at[k], self.into(1 - k, k), kdev[2 - k], self.out, self.into_slot
+                ).start()
+            sent.append(copy(self.summed, self.summed, kdev[1], self.out, self.into_slot))
 
         def collect(self):
-            arrived(self.direct + self.second)
+            copy(self.got, self.got, kdev[1], self.out, self.into_slot).wait_recv()
 
         def total(self):
             out = self.part(i, pl.ds(0, self.got.shape[-1]))[...].astype(F32)
             return out + self.got[0].astype(F32) + self.got[1].astype(F32)
+
+    quarter = half // 2
+    mine_parts = [
+        pl.ds(pl.multiple_of(par * half + n * quarter, quarter), quarter) for n in range(2)
+    ]
+
+    class SquareGather:
+        def __init__(self, view, many, whole=mine, parts=mine_parts, own=None, pass_on=True):
+            self.view, self.many, self.whole, self.parts = view, many, whole, parts
+            self.pass_on = pass_on
+            own = view(i, whole) if own is None else own
+            into = view(i, whole)
+            self.near = Fan([(own, into, kdev[d]) for d in (1, 2)], many(2))
+
+        def forward(self, sources):
+            if not self.pass_on:
+                return []
+            views = [self.view(src, self.whole) for src in sources]
+            return [Fan([(one, one, partner) for one in views], self.many(len(views)))]
+
+        def step(self):
+            self.near.wait_recv()
+            views = [self.view(ki[1 + n], self.parts[n]) for n in range(2)]
+            self.far = Fan([(views[n], views[n], kdev[2 - n]) for n in range(2)], self.many(1))
+            return self.forward((ki[1], ki[2]))
+
+        def collect(self):
+            self.far.wait_recv()
+            return self.forward((ki[3],))
+
+    barrier = pltpu.get_barrier_semaphore()
+    for dev in kdev[1:] + vdev[1:] + seqdev:
+        pl.semaphore_signal(barrier, inc=1, device_id=dev, device_id_type=MESH)
 
     l_small = [load(dup, dup_v), load(dbi, dbi_v), load(ggn, ggn_v)]
     l_qk = [load(wq.at[j], qk_v.at[i, 0]), load(wk.at[j], qk_v.at[i, 1])]
@@ -408,10 +418,6 @@
     l_xa = load(tok, x_all)
     l_ca = load(cot, c_all)
 
-    barrier = pltpu.get_barrier_semaphore()
-    for dev in kdev[1:] + vdev[1:] + seqdev:
-        pl.semaphore_signal(barrier, inc=1, device_id=dev, device_id_type=MESH)
-
     dd_v[16:, :] = jnp.zeros((dd_v.shape[0] - 16, D), BF)
     here(l_small)
     head3 = lax.broadcasted_iota(jnp.int32, (16, W, 32), 1)
@@ -429,50 +435,41 @@
     pl.semaphore_wait(barrier, 6 + len(seqdev))
 
     here(l_qk)
-    t_qk = [None] + [send(qk_v.at[i, par], qk_v.at[i, par], kdev[d]) for d in DIRS]
-    t_v = [None] + [send(wv.at[vj[d], :, mine], v_v.at[j, :, mine], vdev[d]) for d in DIRS]
+    t_qk = Fan(
+        [(qk_v.at[i, par], qk_v.at[i, par], kdev[d]) for d in DIRS], qk_v.at[pl.ds(0, 3), 0]
+    )
+    left = pl.ds(0, half)
+    t_v = Fan(
+        [(wv.at[vj[d], :, mine], v_v.at[j, :, mine], vdev[d]) for d in DIRS],
+        v_v.at[pl.ds(0, 3), :, left],
+    )
     t_ext = Fan([(ext_v.at[i], ext_v.at[i], kdev[d]) for d in DIRS], ext_v.at[pl.ds(0, 3)])
     low = pl.ds(0, 32)
     high = pl.ds(32, 32)
-    t_oa = [None] + [
-        send(wo.at[low, mine], o_v.at[i, j, low, mine], vdev[d]) for d in DIRS
-    ]
-    t_ob = [None] + [
-        send(wo.at[high, mine], o_v.at[i, j, high, mine], kdev[d]) for d in DIRS
-    ]
-    quarter = half // 2
-    two = [
-        pl.ds(pl.multiple_of(par * half + n * quarter, quarter), quarter) for n in range(2)
-    ]
-
-    class SquareGather:
-        def __init__(self, view, own=None):
-            self.view = view
-            own = view(i, mine) if own is None else own
-            self.near = [send(own, view(i, mine), kdev[d]) for d in (1, 2)]
-
-        def step(self):
-            self.far, moves = [], []
-            for n in range(2):
-                self.near[n].wait_recv()
-                view = self.view(ki[1 + n], two[n])
-                self.far.append(send(view, view, kdev[2 - n]))
-                view = self.view(ki[1 + n], mine)
-                moves.append(send(view, view, partner))
-            return moves
-
-        def collect(self):
-            arrived(self.far)
-            view = self.view(ki[3], mine)
-            return [send(view, view, partner)]
-
+    t_ob = Fan(
+        [(wo.at[high, mine], o_v.at[i, j, high, mine], kdev[d]) for d in DIRS],
+        o_v.at[pl.ds(0, 3), 0, high, mine],
+    )
     weights = (fg, fu, fd)
 
-    def gather_weight(n):
-        return SquareGather(lambda src, at: f_v.at[n, src, :, at], weights[n].at[:, mine])
-
-    t_fd = gather_weight(2)
-    t_g = [None] + [send(wg.at[vj[d], :, mine], g_v.at[j, :, mine], vdev[d]) for d in DIRS]
+    def gather_weight(n, rows_at):
+        return SquareGather(
+            lambda src, at: f_v.at[n, src, rows_at, at],
+            lambda count: f_v.at[n, pl.ds(0, count), rows_at, mine],
+            own=weights[n].at[rows_at, mine],
+        )
+
+    cut = FB // 32 * 16
+    top = pl.ds(0, cut)
+    bottom = pl.ds(cut, FB - cut)
+    every = pl.ds(0, FB)
+    t_fd = gather_weight(2, every)
+    l_o.wait()
+    t_oa = LineGather(lambda src: o_v.at[i, src, low, mine], o_v.at[0, :, low, mine])
+    t_g = Fan(
+        [(wg.at[vj[d], :, mine], g_v.at[j, :, mine], vdev[d]) for d in DIRS],
+        g_v.at[pl.ds(0, 3), :, left],
+    )
     t_gge = Fan([(gge_v.at[j], gge_v.at[j], vdev[d]) for d in DIRS], gge_v.at[pl.ds(0, 3)])
 
     here(l_x)
@@ -485,12 +482,12 @@
     lane = lax.broadcasted_iota(jnp.int32, (T, 128), 1)
     lrp = jnp.where(lane == 16, 1.0, nt(n_v[...], dd_v[...]))
 
-    for d in DIRS:
-        t_qk[d].wait_recv()
+    t_qk.wait_recv()
     views = [qk_v.at[ki[d], par] for d in DIRS]
-    f_qk = Fan([(view, view, partner) for view in views], qk_v.at[pl.ds(0, 3), 0])
+    f_qk = Fan([(one, one, partner) for one in views], qk_v.at[pl.ds(0, 3), 0])
+    t_fg = [gather_weight(0, top)]
+    f_qk.wait_recv()
     t_ext.wait_recv()
-    f_qk.wait_recv()
     normed = n_v[...]
     wq_all = qk_v[:, 0].reshape(W * 32, D)
     wk_all = qk_v[:, 1].reshape(W * 32, D)
@@ -525,11 +522,9 @@
         score.append(jnp.where(causal, nt(qd[c], kd[c]), 0.0).astype(BF))
 
     l_v.wait()
-    for d in DIRS:
-        t_v[d].wait_recv()
-    first_half = pl.ds(0, half)
+    t_v.wait_recv()
     views = [v_v.at[vj[d], :, mine] for d in DIRS]
-    f_vv = Fan([(view, view, partner) for view in views], v_v.at[pl.ds(0, 3), :, first_half])
+    f_vv = Fan([(one, one, partner) for one in views], v_v.at[pl.ds(0, 3), :, left])
     f_vv.wait_recv()
     wv_all = v_v[...].reshape(W * 64, D)
     v = nt(normed, wv_all).astype(BF)
@@ -543,24 +538,19 @@
     st_v[i, :VC] = loc.astype(BF)
     st_v[i, VC:] = jnp.broadcast_to(locd, (16, 128)).astype(BF)
     t_st = Fan([(st_v.at[i], st_v.at[i], kdev[d]) for d in DIRS], st_v.at[pl.ds(0, 3)])
-    t_fg = gather_weight(0)
-    t_fu = gather_weight(1)
+    t_fg.append(gather_weight(0, bottom))
+    t_fu = gather_weight(1, every)
+    t_oa.step(0)
+    t_oa.step(1)
     mixed = [nn(score[c], v[blk[c]]) for c in range(nblk)]
 
-    f_o = []
-    l_o.wait()
-    for d in DIRS:
-        t_oa[d].wait_recv()
-        view = o_v.at[i, vj[d], low, mine]
-        f_o.append(send(view, view, partner))
-    t_oa2 = SquareGather(lambda src, at: o_v.at[src, :, low, at])
-    for d in DIRS:
-        t_ob[d].wait_recv()
-        view = o_v.at[ki[d], j, high, mine]
-        f_o.append(send(view, view, partner))
-    t_ob2 = LineGather(lambda src: o_v.at[:, src, high, mine])
+    t_ob.wait_recv()
+    views = [o_v.at[ki[d], j, high, mine] for d in DIRS]
+    f_o = [Fan([(one, one, partner) for one in views], o_v.at[pl.ds(0, 3), 0, high, mine])]
+    t_ob2 = LineGather(lambda src: o_v.at[:, src, high, mine], o_v.at[:, :, high, mine])
     here(l_f)
     f_f = t_fd.step()
+    t_oa.step(2)
 
     def gather_states(slots, totals, back):
         order = range(W - 1, -1, -1) if back else range(W)
@@ -595,10 +585,11 @@
     states = gather_states(st_v, tt_v, False)
 
     l_g.wait()
-    for d in DIRS:
-        t_g[d].wait_recv()
+    t_g.wait_recv()
     views = [g_v.at[vj[d], :, mine] for d in DIRS]
-    f_g = Fan([(view, view, partner) for view in views], g_v.at[pl.ds(0, 3), :, first_half])
+    f_g = Fan([(one, one, partner) for one in views], g_v.at[pl.ds(0, 3), :, left])
+    t_ob2.step(0)
+    t_ob2.step(1)
     start = [entering(tt_v, False, *states)]
     for c in range(nblk):
         start.append(start[c] * dec[c] + up[c])
@@ -619,7 +610,15 @@
     act_v[1] = sig + act * (1.0 - sig)
     ga_v[j] = (normal * gg * act).astype(BF)
     act_v[2] = normal
-    t_ga = LineGather(lambda src: ga_v.at[src])
+    halves = [pl.ds(n * T // 2, T // 2) for n in range(2)]
+    t_ga = [LineGather(lambda src, at=at: ga_v.at[src, at], ga_v.at[:, at]) for at in halves]
+
+    t_oa.collect()
+    views = [o_v.at[i, vj[d], low, mine] for d in DIRS]
+    f_o.append(Fan([(one, one, partner) for one in views], o_v.at[0, pl.ds(0, 3), low, mine]))
+    t_oa2 = SquareGather(
+        lambda src, at: o_v.at[src, :, low, at], lambda count: o_v.at[pl.ds(0, count), :, low, mine]
+    )
 
     here([l_xa, l_ca])
     for part in range(rows // T):
@@ -632,39 +631,41 @@
         lax.broadcasted_iota(jnp.int32, (rows, 128), 1) == 16, 1.0, nt(n_all[...], dd_v[...])
     )
     lall_v[...] = low_all.astype(BF)
-    t_ob2.step(0)
-    t_ob2.step(1)
-    f_f += t_fg.step()
+    for line in t_fg:
+        f_f += line.step()
     t_ob2.step(2)
-    t_ga.step(0)
-    t_ga.step(1)
+    t_ga[0].step(0)
+    t_ga[0].step(1)
+    t_ga[1].step(0)
+    t_ga[1].step(1)
+    f_f += t_fu.step()
+    t_ga[0].step(2)
+    t_ga[1].step(2)
+    f_o += t_oa2.step()
     f_f += t_fd.collect()
-    f_f += t_fu.step()
-    f_o += t_oa2.step()
-    t_ga.step(2)
     l_c.wait()
     arrived(f_f)
     dn = f_v[2].reshape(W * FB, D)
     gh_v[...] = nt(c_v[...], dn)
-    f_f = t_fg.collect()
+    f_f = t_fg[0].collect() + t_fg[1].collect()
     f_f += t_fu.collect()
     f_o += t_oa2.collect()
     t_ob2.collect()
-    for d in DIRS:
-        view = o_v.at[:, vj[d], high, mine]
-        f_o.append(send(view, view, partner))
-    t_ga.collect()
+    views = [o_v.at[:, vj[d], high, mine] for d in DIRS]
+    f_o.append(Fan([(one, one, partner) for one in views], o_v.at[:, pl.ds(0, 3), high, mine]))
+    for line in t_ga:
+        line.collect()
     arrived(f_o)
+    arrived(f_f)
+
+    gT = f_v[0].reshape(W * FB, D)
+    uT = f_v[1].reshape(W * FB, D)
     att = nn(ga_v[0], o_v[0].reshape(W * 64, D))
     for h in range(1, W):
         att = att + nn(ga_v[h], o_v[h].reshape(W * 64, D))
     resid = x_v[...].astype(F32) + att
     r3 = lax.rsqrt(jnp.sum(resid * resid, axis=1, keepdims=True) / D + EPS)
     fin = (resid * r3 * g3).astype(BF)
-    arrived(f_f)
-
-    gT = f_v[0].reshape(W * FB, D)
-    uT = f_v[1].reshape(W * FB, D)
     gval = nt(fin, gT)
     uval = nt(fin, uT)
     fsig = 1.0 / (1.0 + jnp.exp(-gval))
@@ -673,29 +674,29 @@
     gh = gh_v[...]
     gup = (gh * fact).astype(BF)
     ggate = (gh * uval * (fsig + fact * (1.0 - fsig))).astype(BF)
+    hd[...] = hid.T.reshape(W, FB, T)
+    t_hd = Fan([(hd.at[ki[d]], hseg.at[i], kdev[d]) for d in DIRS], hseg.at[pl.ds(0, 3)])
+    hseg[i] = hd[i]
     part = nn(ggate, gT) + nn(gup, uT)
     p_v[...] = part
     sst[...] = as_row(jnp.sum(resid * g3 * part, axis=1, keepdims=True))
     t_m3 = Fan([(sst, rst.at[d], vdev[d]) for d in DIRS], rst.at[pl.ds(1, 3)])
-    ggp = nt((part * g3).astype(BF), o_v[...].reshape(W * W * 64, D))
-    for h in range(W):
-        sgg[h] = ggp[:, h * VC : (h + 1) * VC].astype(BF)
-    halves = [pl.ds(n * T // 2, T // 2) for n in range(2)]
+    part_low = (part * g3).astype(BF)
     t_gg = [
         LineSum(
             lambda to, at=at: sgg.at[to, at],
-            rgg.at[0, at],
-            rgg.at[1, at],
+            rgg.at[pl.ds(0, 2), at],
             rgg.at[pl.ds(2, 2), at],
             cgg.at[:, at],
         )
         for at in halves
     ]
-    for line in t_gg:
-        line.rest()
-    hd[...] = hid.T.reshape(W, FB, T)
-    t_hd = Fan([(hd.at[ki[d]], hseg.at[i], kdev[d]) for d in DIRS], hseg.at[pl.ds(0, 3)])
-    hseg[i] = hd[i]
+    ggp = nt(part_low, o_v[...].reshape(W * W * 64, D))
+    for h in range(W):
+        sgg[h] = ggp[:, h * VC : (h + 1) * VC].astype(BF)
+    for n in range(3):
+        for line in t_gg:
+            line.go(n)
 
     def weight_part(n, grad):
         gw[n] = tn(grad, fin).astype(BF).reshape(W, FB, D)
@@ -719,6 +720,8 @@
     m3 = as_column(sst[...] + rst[1] + rst[2] + rst[3]) / D
     base = c_v[...].astype(F32) - resid * (r3 * r3 * r3 * m3)
     t_gg[0].step(0)
+    settle(0, t_pre0)
+    t_fw0 = square(0)
     direct = nt(base.astype(BF), o_v[j].reshape(W * 64, D))
     full = p_v[...] * (g3 * r3)
     mixed_in = (full + own_run * base).astype(BF)
@@ -726,17 +729,17 @@
         gow[h] = tn(ga_v[h], mixed_in).astype(BF)
     t_po = send(gow.at[:, :, other], preo, partner)
     t_gg[0].step(1)
-    settle(0, t_pre0)
-    t_fw0 = square(0)
     so[...] = (nn(hid, dn) + own_slab * resid).astype(BF).T.reshape(W, W, 64, T)
     t_gg[1].step(0)
-    t_out = LineSum(lambda to: so.at[:, to], ro.at[0], ro.at[1], ro.at[pl.ds(2, 2)], co).rest()
+    t_out = LineSum(lambda to: so.at[:, to], ro.at[pl.ds(0, 2)], ro.at[pl.ds(2, 2)], co).rest()
     ffn_gain = jnp.sum(part * resid * r3, axis=0, keepdims=True)
     t_gg[1].step(1)
     t_pre1 = weight_part(1, gup)
     t_po.wait_recv()
     preso[...] = (gow[:, :, mine].astype(F32) + preo[...].astype(F32)).astype(BF)
     t_fw0.step()
+    settle(1, t_pre1)
+    t_fw1 = square(1)
     for line in t_gg:
         line.collect()
 
@@ -747,6 +750,12 @@
     dgate = (ggrad * normal * gg * act_v[1]).astype(BF)
     gs = ggrad * act
     group = jnp.sum(gs * normal, axis=0, keepdims=True)
+    group_rows = [
+        jnp.concatenate(
+            [group[:, h * 64 : (h + 1) * 64], jnp.zeros((1, T - 64), F32)], axis=1
+        )
+        for h in range(W)
+    ]
     gnm = gs * gg
     gmix = (r2 * (gnm - normal * (jnp.sum(normal * gnm, axis=1, keepdims=True) / VC))).astype(BF)
 
@@ -766,14 +775,18 @@
         dq_in.append(nn(ds, kd[c]) + em[c] * nn(gmix[blk[c]], start_low[c]))
         dk_in.append(tn(ds, qd[c]))
         dv_in.append(tn(score[c], gmix[blk[c]]))
-    settle(1, t_pre1)
+    t_out.step(0)
+    t_hd.wait_recv()
+    dsum[0] = nn(lanes(hseg[...]), c_all[...]).astype(BF)
+    t_ds = send(dsum.at[0], dsum.at[1], partner)
     t_bst.wait_recv()
     after = [None] * nblk
     states = gather_states(bst_v, btt_v, True)
-    t_out.step(0)
     after[nblk - 1] = entering(btt_v, True, *states)
     for c in range(nblk - 2, -1, -1):
         after[c] = after[c + 1] * dec[c + 1] + qst[c + 1]
+    t_out.step(1)
+    t_fw1.step()
 
     ql, kl, vl, ga = [], [], [], []
     for c in range(nblk):
@@ -794,28 +807,37 @@
     vl = jnp.concatenate(vl, axis=0)
     ga = jnp.concatenate(ga, axis=0).astype(BF)
     vz[0] = vl.T.reshape(W, 64, T)
-    t_vz = Fan([(vz.at[0, vj[d]], zvg.at[0, j], vdev[d]) for d in DIRS], zvg.at[0, pl.ds(0, 3)])
     qka[:, 0] = ql.T.reshape(W, 32, T)
     qka[:, 1] = kl.T.reshape(W, 32, T)
     qka[:, 2] = ga.T.reshape(W, 32, T)
     t_qa = Fan([(qka.at[ki[d]], kqa.at[i], kdev[d]) for d in DIRS], kqa.at[pl.ds(0, 3)])
-    t_out.step(1)
     glr = nn(ga, ext_all).astype(BF)
     gn = nn(ql, wq_all) + nn(kl, wk_all) + nn(vl, wv_all) + nn(dgate, wg_all) + nn(glr, dd_v[...])
     x = x_v[...].astype(F32)
     gnx = gn * x
     norm_gain = jnp.sum(gnx * r1, axis=0, keepdims=True)
     m1p = as_row(jnp.sum(gnx * g1, axis=1, keepdims=True))[:1]
-    small = tn(glr, normed)[:16]
+    rank_row = lax.broadcasted_iota(jnp.int32, (16, 128), 0)
+    rank_col = lax.broadcasted_iota(jnp.int32, (16, 128), 1)
+    by_owner = jnp.where(rank_col == lax.rem(rank_row, W) * W + rank_row // W, 1.0, 0.0)
+    small = nn(by_owner.astype(BF), tn(glr, normed).astype(BF))
+    slab = D // (W * W)
     rid = lax.broadcasted_iota(jnp.int32, (16, T), 0)
     for h in range(W):
-        at = slice(h * T, (h + 1) * T)
-        sm0[h, 0:16] = small[:, at].astype(BF)
-        rest = jnp.where(rid == 0, norm_gain[:, at], 0.0)
-        rest = jnp.where(rid == 1, ffn_gain[:, at], rest)
+        ranks = small[h * W : (h + 1) * W]
+        sm0[h, 0:16] = jnp.concatenate(
+            [ranks[:, n * T : (n + 1) * T] for n in range(W)], axis=0
+        ).astype(BF)
+
+        def slabs(row):
+            return jnp.concatenate(
+                [row[:, (W * n + h) * slab : (W * n + h + 1) * slab] for n in range(W)], axis=1
+            )
+
+        rest = jnp.where(rid == 0, slabs(norm_gain), 0.0)
+        rest = jnp.where(rid == 1, slabs(ffn_gain), rest)
+        rest = jnp.where(rid == 2, group_rows[h], rest)
         rest = jnp.where(rid == 3, m1p, rest)
-        if h == 0:
-            rest = jnp.where(rid == 2, group, rest)
         sm0[h, 16:32] = rest.astype(BF)
     t_s0 = Fan([(sm0.at[vj[d]], sm1.at[d], vdev[d]) for d in DIRS], sm1.at[pl.ds(1, 3)])
     whole = gn * (r1 * g1) + full + own_slab * base
@@ -824,31 +846,30 @@
     t_gn = [
         LineSum(
             lambda to, at=at: sgn.at[at, to],
-            rgn.at[0, at],
-            rgn.at[1, at],
+            rgn.at[pl.ds(0, 2), at],
             rgn.at[pl.ds(2, 2), at],
             cgn.at[:, at],
         )
         for at in pairs
     ]
-    for line in t_gn:
-        line.rest()
+    for n in range(3):
+        for line in t_gn:
+            line.go(n)
+    t_vz = Fan([(vz.at[0, vj[d]], zvg.at[0, j], vdev[d]) for d in DIRS], zvg.at[0, pl.ds(0, 3)])
+
     t_ow.step()
-    t_fw1 = square(1)
-
-    t_out.collect()
-    ao[...] = t_out.total().astype(BF)
-    t_ao = Fan([(ao.at[ki[d]], oseg.at[i], kdev[d]) for d in DIRS], oseg.at[pl.ds(0, 3)])
-    oseg[i] = ao[i]
 
     t_gz.wait_recv()
     zvg[1, j] = vz[1, j]
     t_gk = Fan([(zvg.at[1, ki[d]], kvg.at[1, i], kdev[d]) for d in DIRS], kvg.at[1, pl.ds(0, 3)])
     kvg[1, i] = zvg[1, i]
 
-    t_hd.wait_recv()
-    dsum[0] = nn(lanes(hseg[...]), c_all[...]).astype(BF)
-    t_ds = send(dsum.at[0], dsum.at[1], partner)
+    def finish_square(n, line):
+        line.collect()
+        fin_f[par, n] = line.total().astype(BF)
+        return send(fin_f.at[par, n], fin_f.at[par, n], partner)
+
+    t_ff = [finish_square(0, t_fw0)]
 
     t_s0.wait_recv()
     sm2[0] = total(sm0[j], sm1).astype(BF)
@@ -859,20 +880,22 @@
         + sm1[3, 19:20].astype(F32)
     ) / D
     t_s1 = Fan([(sm2.at[0], sm2.at[d], kdev[d]) for d in DIRS], sm2.at[pl.ds(1, 3)])
-    t_vz.wait_recv()
-    zvg[0, j] = vz[0, j]
-    t_vk = Fan([(zvg.at[0, ki[d]], kvg.at[0, i], kdev[d]) for d in DIRS], kvg.at[0, pl.ds(0, 3)])
-    kvg[0, i] = zvg[0, i]
+
+    t_out.collect()
+    ao[...] = t_out.total().astype(BF)
+    t_ao = Fan([(ao.at[ki[d]], oseg.at[i], kdev[d]) for d in DIRS], oseg.at[pl.ds(0, 3)])
+    oseg[i] = ao[i]
+
     t_gn[0].step(0)
+    t_gn[1].step(0)
     t_gn[0].step(1)
-    t_fw1.step()
-    t_gn[1].step(0)
     t_gn[1].step(1)
+    t_ff.append(finish_square(1, t_fw1))
 
     t_ow.collect()
     mid_o[...] = t_ow.total().astype(BF).reshape(W, 64, half)
     t_oz = LineSum(
-        lambda to: mid_o.at[to], rowz.at[0], rowz.at[1], rowz.at[pl.ds(2, 2)], coz
+        lambda to: mid_o.at[to], rowz.at[pl.ds(0, 2)], rowz.at[pl.ds(2, 2)], coz
     ).rest()
 
     t_qa.wait_recv()
@@ -884,25 +907,9 @@
     t_qs = send(qksum.at[0], qksum.at[1], partner)
     t_es = send(esum.at[0], esum.at[1], partner)
 
-    t_s1.wait_recv()
-    sm3[0] = total(sm2[0], sm2).astype(BF)
-    t_s2 = send(sm3.at[0], sm3.at[1], partner)
-
-    def finish_square(n, line):
-        line.collect()
-        fin_f[par, n] = line.total().astype(BF)
-        return send(fin_f.at[par, n], fin_f.at[par, n], partner)
-
-    t_ff = [finish_square(0, t_fw0)]
-
     t_gk.wait_recv()
-    t_vk.wait_recv()
-    for n in range(2):
-        vgsum[0, n] = nn(lanes(kvg[n]), nall).astype(BF)
-    t_vs = send(vgsum.at[0], vgsum.at[1], partner)
-    t_s2.wait_recv()
-    sm4[j] = (sm3[0].astype(F32) + sm3[1].astype(F32)).astype(BF)
-    t_s3 = Fan([(sm4.at[j], sm4.at[j], vdev[d]) for d in DIRS], sm4.at[pl.ds(0, 3)])
+    vgsum[0, 1] = nn(lanes(kvg[1]), nall).astype(BF)
+    t_vs = [send(vgsum.at[0, 1], vgsum.at[1, 1], partner)]
 
     for line in t_gn:
         line.collect()
@@ -912,9 +919,20 @@
         ai[h] = (summed[h] - xr_v[at, :].astype(F32) * m1).astype(BF)
     t_ai = Fan([(ai.at[ki[d]], iseg.at[i], kdev[d]) for d in DIRS], iseg.at[pl.ds(0, 3)])
     iseg[i] = ai[i]
+
+    t_vz.wait_recv()
+    zvg[0, j] = vz[0, j]
+    t_vk = Fan([(zvg.at[0, ki[d]], kvg.at[0, i], kdev[d]) for d in DIRS], kvg.at[0, pl.ds(0, 3)])
+    kvg[0, i] = zvg[0, i]
+
+    t_s1.wait_recv()
+    sm3[0] = total(sm2[0], sm2).astype(BF)
+    t_s2 = send(sm3.at[0], sm3.at[1], partner)
     t_oz.step(0)
     t_oz.step(1)
-    t_ff.append(finish_square(1, t_fw1))
+    t_vk.wait_recv()
+    vgsum[0, 0] = nn(lanes(kvg[0]), nall).astype(BF)
+    t_vs.append(send(vgsum.at[0, 0], vgsum.at[1, 0], partner))
 
     t_ds.wait_recv()
     r_fd[...] = dsum[0].astype(F32) + dsum[1].astype(F32)
@@ -927,9 +945,6 @@
     decay = (esum[0] + esum[1]).T
     r_du[...] = decay[0:16, :].reshape(16, 1, 32)
     r_db[...] = decay[16:17, :]
-    t_vs.wait_recv()
-    r_v[...] = vgsum[0, 0].astype(F32) + vgsum[1, 0].astype(F32)
-    r_g[...] = vgsum[0, 1].astype(F32) + vgsum[1, 1].astype(F32)
     t_ff[0].wait_recv()
     for h in range(2):
         r_fg[:, h * half : (h + 1) * half] = fin_f[h, 0].astype(F32)
@@ -939,22 +954,22 @@
     t_ff[1].wait_recv()
     for h in range(2):
         r_fu[:, h * half : (h + 1) * half] = fin_f[h, 1].astype(F32)
-    t_s3.wait_recv()
-    for h in range(W):
-        pick[:, h * T : (h + 1) * T] = sm4[h].astype(F32)
-    pair = i * W + j
-    r_dd[...] = pick[pl.ds(pair, 1), :]
-    wide = pick[16:24, :]
-    slab = D // (W * W)
-    chosen = jnp.zeros((8, slab), F32)
-    for n in range(W * W):
-        chosen = jnp.where(pair == n, wide[:, n * slab : (n + 1) * slab], chosen)
-    r_ng[...] = chosen[0:1]
-    r_fn[...] = chosen[1:2]
-    chosen = jnp.zeros((8, 64), F32)
+    arrived(t_vs)
+    r_v[...] = vgsum[0, 0].astype(F32) + vgsum[1, 0].astype(F32)
+    r_g[...] = vgsum[0, 1].astype(F32) + vgsum[1, 1].astype(F32)
+    t_s2.wait_recv()
+    tot = sm3[0].astype(F32) + sm3[1].astype(F32)
+    own_ranks, own_slabs = [], jnp.zeros((2, slab), F32)
     for n in range(W):
-        chosen = jnp.where(j == n, wide[:, n * 64 : (n + 1) * 64], chosen)
-    r_gg[...] = chosen[2:3]
+        own_ranks.append(jnp.zeros((1, T), F32))
+        for h in range(W):
+            row = tot[n * W + h : n * W + h + 1]
+            own_ranks[n] = jnp.where(i == h, row, own_ranks[n])
+        own_slabs = jnp.where(i == n, tot[16:18, n * slab : (n + 1) * slab], own_slabs)
+    r_dd[...] = jnp.concatenate(own_ranks, axis=1)
+    r_ng[...] = own_slabs[0:1]
+    r_fn[...] = own_slabs[1:2]
+    r_gg[...] = tot[18:19, 0:64]
     t_ai.wait_recv()
     r_in[...] = lanes(iseg[...])
     t_fo.wait_recv()
@@ -974,7 +989,8 @@
             cp.wait_send()
 
 
-N_REMOTE = 150
+N_OUT = 88
+N_IN = 92
 N_LOCAL = 18
 
 
@@ -1086,14 +1102,12 @@
         vm((W, 32, T)),
         vm((W, 32, T)),
         vm((2, 32, T)),
-        vm((W, 32, T)),
-        vm((32, D), F32),
         vm((rows, 128)),
         vm((T, W * FB), F32),
         vm((3, T, VC), F32),
         vm((T, D), F32),
-        pltpu.SemaphoreType.DMA((N_REMOTE + 2 * n_seq,)),
-        pltpu.SemaphoreType.DMA((N_REMOTE + 2 * n_seq,)),
+        pltpu.SemaphoreType.DMA((N_OUT + 2 * n_seq,)),
+        pltpu.SemaphoreType.DMA((N_IN + 2 * n_seq,)),
         pltpu.SemaphoreType.DMA((N_LOCAL,)),
     ]
     return pl.pallas_call(

time: 95.1 us -> 89 us (0.936)
  Pallas kernels: 94 us -> 87.8 us
    pallas_call x1, Pallas kernels: 92 us -> 85.9 us  [layer(): pl.pallas_call(functools.partial(layer_kernel, n_seq), out_shape=outs, in...]
where the time goes in v5:
time: 89 us; the launch traced here: 88.6 us
  Pallas kernels  87.8 us (99%)
    pallas_call x1, Pallas kernels, layer(): pl.pallas_call(functools.partial(layer_kernel, n_seq), out_shape=outs, in...  85.9 us
    pallas_call x1, Pallas kernels, finish(): pl.pallas_call(finish_kernel, out_shape=[jax.ShapeDtypeStruct(p.shape, p....  1.95 us

profile of v5, /device:TPU:0, one launch (start us, length us, event | category | flops | bytes accessed | tf_op | source)
XLA Modules:
  0.0 88.6 jit_solution(15880226862624877526)
XLA Ops:
  0.7 85.9 %layer.1 = (bf16[64,1024]{1,0:T(8,128)(2,1)S(1)}, bf16[64,1024]{1,0:T(8,128)(2,1)S(1)}, f32[1,64]{1,0:T(1,128)S(1)}, f32[32,1024]{1,0:T(8,128)S(1)}, f32[32,1024...) custom-call(bf16[1024,1024]{1,0:T(8,128)(2,1)} %tok.1, ...), custom_call_target="tpu_custom_call" | custom-call | tf_op jit(solution)/shard_map/layer/pallas_call | solution.py:1113
  86.5 1.9 %finish.1 = (bf16[64,1024]{1,0:T(8,128)(2,1)}, bf16[64,1024]{1,0:T(8,128)(2,1)}, f32[1,64]{1,0:T(1,128)}, f32[32,1024]{1,0:T(8,128)}, f32[32,1024]{1,0:T(8,128)}...) custom-call(bf16[64,1024]{1,0:T(8,128)(2,1)S(1)} %get-tuple-element., ...), custom_call_target="tpu_custom_call" | custom-call | tf_op jit(solution)/shard_map/finish/pallas_call | solution.py:1137

commit v6 on v5

--- a/solution.py
+++ b/solution.py
@@ -224,10 +224,20 @@
             device_id_type=MESH,
         )
 
+    ring = []
+
+    def ring_slot():
+        if len(ring) < 28:
+            return out_slot()
+        n, cp = ring.pop(0)
+        cp.wait_send()
+        return n
+
     def send(src, dst, dev):
-        cp = copy(src, dst, dev, out_slot(), in_slot())
+        n = ring_slot()
+        cp = copy(src, dst, dev, n, in_slot())
         cp.start()
-        sent.append(cp)
+        ring.append((n, cp))
         return cp
 
     def load(src, dst):
@@ -237,11 +247,11 @@
 
     class Fan:
         def __init__(self, copies, size):
-            n, m = out_slot(), in_slot()
+            n, m = ring_slot(), in_slot()
             for src, dst, dev in copies:
                 copy(src, dst, dev, n, m).start()
             self.all = copy(size, size, partner, n, m)
-            sent.append(self.all)
+            ring.append((n, self.all))
 
         def wait_recv(self):
             self.all.wait_recv()
@@ -642,6 +652,9 @@
     t_ga[0].step(2)
     t_ga[1].step(2)
     f_o += t_oa2.step()
+    t_ob2.collect()
+    views = [o_v.at[:, vj[d], high, mine] for d in DIRS]
+    f_o.append(Fan([(one, one, partner) for one in views], o_v.at[:, pl.ds(0, 3), high, mine]))
     f_f += t_fd.collect()
     l_c.wait()
     arrived(f_f)
@@ -649,20 +662,22 @@
     gh_v[...] = nt(c_v[...], dn)
     f_f = t_fg[0].collect() + t_fg[1].collect()
     f_f += t_fu.collect()
-    f_o += t_oa2.collect()
-    t_ob2.collect()
-    views = [o_v.at[:, vj[d], high, mine] for d in DIRS]
-    f_o.append(Fan([(one, one, partner) for one in views], o_v.at[:, pl.ds(0, 3), high, mine]))
+    f_far = t_oa2.collect()
     for line in t_ga:
         line.collect()
     arrived(f_o)
+
+
+    def attention(head):
+        return nn(ga_v[head], o_v[head].reshape(W * 64, D))
+
+    att = attention(i) + attention(ki[1]) + attention(ki[2])
+    p_v[...] = att
+    arrived(f_far)
     arrived(f_f)
-
     gT = f_v[0].reshape(W * FB, D)
     uT = f_v[1].reshape(W * FB, D)
-    att = nn(ga_v[0], o_v[0].reshape(W * 64, D))
-    for h in range(1, W):
-        att = att + nn(ga_v[h], o_v[h].reshape(W * 64, D))
+    att = p_v[...] + attention(ki[3])
     resid = x_v[...].astype(F32) + att
     r3 = lax.rsqrt(jnp.sum(resid * resid, axis=1, keepdims=True) / D + EPS)
     fin = (resid * r3 * g3).astype(BF)
@@ -706,22 +721,29 @@
         move.wait_recv()
         pres[n] = (gw[n, :, :, mine].astype(F32) + pre[n].astype(F32)).astype(BF)
 
-    def square(n):
+    def square(n, rows_at):
         return SquareSum(
-            lambda to, at: pres.at[n, to, :, at], rfw.at[n], qfw.at[n], cfw.at[n]
+            lambda to, at: pres.at[n, to, rows_at, at],
+            rfw.at[n, :, rows_at],
+            qfw.at[n, :, rows_at],
+            cfw.at[n, :, rows_at],
         )
 
     t_pre0 = weight_part(0, ggate)
+    t_pre1 = weight_part(1, gup)
 
     feature = lax.broadcasted_iota(jnp.int32, (1, D), 1)
     own_slab = jnp.where(lax.rem(feature // 64, W) == j, 1.0, 0.0)
     own_run = jnp.where(feature // (D // W) == j, 1.0, 0.0)
+    so[...] = (nn(hid, dn) + own_slab * resid).astype(BF).T.reshape(W, W, 64, T)
+    t_out = LineSum(lambda to: so.at[:, to], ro.at[pl.ds(0, 2)], ro.at[pl.ds(2, 2)], co).rest()
+    ffn_gain = jnp.sum(part * resid * r3, axis=0, keepdims=True)
+    t_gg[0].step(0)
     t_m3.wait_recv()
     m3 = as_column(sst[...] + rst[1] + rst[2] + rst[3]) / D
     base = c_v[...].astype(F32) - resid * (r3 * r3 * r3 * m3)
-    t_gg[0].step(0)
     settle(0, t_pre0)
-    t_fw0 = square(0)
+    t_fw0 = square(0, every)
     direct = nt(base.astype(BF), o_v[j].reshape(W * 64, D))
     full = p_v[...] * (g3 * r3)
     mixed_in = (full + own_run * base).astype(BF)
@@ -729,17 +751,13 @@
         gow[h] = tn(ga_v[h], mixed_in).astype(BF)
     t_po = send(gow.at[:, :, other], preo, partner)
     t_gg[0].step(1)
-    so[...] = (nn(hid, dn) + own_slab * resid).astype(BF).T.reshape(W, W, 64, T)
     t_gg[1].step(0)
-    t_out = LineSum(lambda to: so.at[:, to], ro.at[pl.ds(0, 2)], ro.at[pl.ds(2, 2)], co).rest()
-    ffn_gain = jnp.sum(part * resid * r3, axis=0, keepdims=True)
     t_gg[1].step(1)
-    t_pre1 = weight_part(1, gup)
     t_po.wait_recv()
     preso[...] = (gow[:, :, mine].astype(F32) + preo[...].astype(F32)).astype(BF)
     t_fw0.step()
     settle(1, t_pre1)
-    t_fw1 = square(1)
+    t_fw1 = [square(1, top)]
     for line in t_gg:
         line.collect()
 
@@ -767,6 +785,7 @@
     bst_v[i, VC:] = jnp.broadcast_to(locd, (16, 128)).astype(BF)
     t_bst = Fan([(bst_v.at[i], bst_v.at[i], kdev[d]) for d in DIRS], bst_v.at[pl.ds(0, 3)])
     t_ow = SquareSum(lambda to, at: preso.at[to, :, at], rowk, qow, cow)
+    t_fw1.append(square(1, bottom))
     vz[1] = dgate.T.reshape(W, 64, T)
     t_gz = Fan([(vz.at[1, vj[d]], zvg.at[1, j], vdev[d]) for d in DIRS], zvg.at[1, pl.ds(0, 3)])
     dq_in, dk_in, dv_in = [], [], []
@@ -786,7 +805,7 @@
     for c in range(nblk - 2, -1, -1):
         after[c] = after[c + 1] * dec[c + 1] + qst[c + 1]
     t_out.step(1)
-    t_fw1.step()
+    t_fw1[0].step()
 
     ql, kl, vl, ga = [], [], [], []
     for c in range(nblk):
@@ -857,19 +876,21 @@
             line.go(n)
     t_vz = Fan([(vz.at[0, vj[d]], zvg.at[0, j], vdev[d]) for d in DIRS], zvg.at[0, pl.ds(0, 3)])
 
-    t_ow.step()
 
     t_gz.wait_recv()
     zvg[1, j] = vz[1, j]
     t_gk = Fan([(zvg.at[1, ki[d]], kvg.at[1, i], kdev[d]) for d in DIRS], kvg.at[1, pl.ds(0, 3)])
     kvg[1, i] = zvg[1, i]
 
-    def finish_square(n, line):
-        line.collect()
-        fin_f[par, n] = line.total().astype(BF)
+    def finish_square(n, lines):
+        for line, rows_at in lines:
+            line.collect()
+            fin_f[par, n, rows_at] = line.total().astype(BF)
         return send(fin_f.at[par, n], fin_f.at[par, n], partner)
 
-    t_ff = [finish_square(0, t_fw0)]
+    t_ff = [finish_square(0, [(t_fw0, every)])]
+    t_ow.step()
+    t_fw1[1].step()
 
     t_s0.wait_recv()
     sm2[0] = total(sm0[j], sm1).astype(BF)
@@ -890,7 +911,6 @@
     t_gn[1].step(0)
     t_gn[0].step(1)
     t_gn[1].step(1)
-    t_ff.append(finish_square(1, t_fw1))
 
     t_ow.collect()
     mid_o[...] = t_ow.total().astype(BF).reshape(W, 64, half)
@@ -906,6 +926,7 @@
     esum[0] = nn(lanes(kqa[:, 2]), lall_v[...])
     t_qs = send(qksum.at[0], qksum.at[1], partner)
     t_es = send(esum.at[0], esum.at[1], partner)
+    t_ff.append(finish_square(1, list(zip(t_fw1, (top, bottom)))))
 
     t_gk.wait_recv()
     vgsum[0, 1] = nn(lanes(kvg[1]), nall).astype(BF)
@@ -975,7 +996,7 @@
     t_fo.wait_recv()
     for h in range(2):
         r_o[:, h * half : (h + 1) * half] = fin_ow[h].astype(F32)
-    for cp in sent:
+    for cp in sent + [cp for _, cp in ring]:
         cp.wait_send()
 
     @pl.when(inner)
@@ -989,8 +1010,8 @@
             cp.wait_send()
 
 
-N_OUT = 88
-N_IN = 92
+N_OUT = 62
+N_IN = 93
 N_LOCAL = 18
 
 
@@ -1106,7 +1127,7 @@
         vm((T, W * FB), F32),
         vm((3, T, VC), F32),
         vm((T, D), F32),
-        pltpu.SemaphoreType.DMA((N_OUT + 2 * n_seq,)),
+        pltpu.SemaphoreType.DMA((N_OUT,)),
         pltpu.SemaphoreType.DMA((N_IN + 2 * n_seq,)),
         pltpu.SemaphoreType.DMA((N_LOCAL,)),
     ]

time: 89 us -> 87.8 us (0.987)
  Pallas kernels: 87.8 us -> 86.7 us
    pallas_call x1, Pallas kernels: 85.9 us -> 84.8 us  [layer(): pl.pallas_call(functools.partial(layer_kernel, n_seq), out_shape=outs, in...]
where the time goes in v6:
time: 87.8 us; the launch traced here: 87.6 us
  Pallas kernels  86.7 us (99%)
    pallas_call x1, Pallas kernels, layer(): pl.pallas_call(functools.partial(layer_kernel, n_seq), out_shape=outs, in...  84.8 us
    pallas_call x1, Pallas kernels, finish(): pl.pallas_call(finish_kernel, out_shape=[jax.ShapeDtypeStruct(p.shape, p....  1.95 us

profile of v6, /device:TPU:0, one launch (start us, length us, event | category | flops | bytes accessed | tf_op | source)
XLA Modules:
  0.0 87.6 jit_solution(16321274867899368054)
XLA Ops:
  0.7 84.8 %layer.1 = (bf16[64,1024]{1,0:T(8,128)(2,1)S(1)}, bf16[64,1024]{1,0:T(8,128)(2,1)S(1)}, f32[1,64]{1,0:T(1,128)S(1)}, f32[32,1024]{1,0:T(8,128)S(1)}, f32[32,1024...) custom-call(bf16[1024,1024]{1,0:T(8,128)(2,1)} %tok.1, ...), custom_call_target="tpu_custom_call" | custom-call | tf_op jit(solution)/shard_map/layer/pallas_call | solution.py:1134
  85.4 1.9 %finish.1 = (bf16[64,1024]{1,0:T(8,128)(2,1)}, bf16[64,1024]{1,0:T(8,128)(2,1)}, f32[1,64]{1,0:T(1,128)}, f32[32,1024]{1,0:T(8,128)}, f32[32,1024]{1,0:T(8,128)}...) custom-call(bf16[64,1024]{1,0:T(8,128)(2,1)S(1)} %get-tuple-element., ...), custom_call_target="tpu_custom_call" | custom-call | tf_op jit(solution)/shard_map/finish/pallas_call | solution.py:1158

commit v7 on v6

--- a/solution.py
+++ b/solution.py
@@ -202,7 +202,7 @@
     seqdev = [{"seq": lax.rem(s + e, n_seq)} for e in range(1, n_seq)]
 
     count = [0, 0, 0]
-    sent, inner_sent, outer_sent = [], [], []
+    inner_sent, outer_sent = [], []
 
     def slot(kind):
         count[kind] += 1
@@ -269,10 +269,10 @@
     class LineGather:
         def __init__(self, view, four):
             a, b, c = in_slot(), in_slot(), in_slot()
-            n, m = out_slot(), out_slot()
+            n, m = ring_slot(), out_slot()
             near = copy(view(j), view(j), vdev[1], n, a)
             near.start()
-            sent.append(near)
+            ring.append((n, near))
             across = copy(view(j), view(j), vdev[3], m, c)
             self.got = [
                 copy(view(vj[d]), view(vj[d]), vdev[1], n, at) for d, at in zip(DIRS, (a, b, c))
@@ -303,16 +303,15 @@
         def __init__(self, part, both, relay, summed):
             self.part, self.both, self.relay, self.summed = part, both, relay, summed
             a, b, c = in_slot(), in_slot(), in_slot()
-            n, m, o = out_slot(), out_slot(), out_slot()
+            n, o = out_slot(), out_slot()
+            self.into_slot = c
             self.first = [
                 copy(part(vj[3]), relay.at[0], vdev[1], n, a),
                 copy(part(vj[2]), relay.at[1], vdev[1], n, b),
             ]
-            self.direct = copy(part(vj[1]), both.at[0], vdev[1], m, c)
             self.second = [copy(summed.at[k], both.at[1], vdev[2 + k], o, c) for k in range(2)]
-            self.all = copy(both, both, vdev[1], m, c)
+            self.all = copy(both, both, vdev[1], o, c)
             outer_sent.append(copy(relay, relay, vdev[1], n, a))
-            sent.append(self.direct)
             inner_sent.append(copy(summed, summed, vdev[1], o, a))
 
         def go(self, n):
@@ -323,7 +322,10 @@
                     self.first[n].start()
 
             elif n == 2:
-                self.direct.start()
+                m = ring_slot()
+                direct = copy(self.part(vj[1]), self.both.at[0], vdev[1], m, self.into_slot)
+                direct.start()
+                ring.append((m, direct))
 
         def rest(self):
             for n in range(3):
@@ -351,13 +353,13 @@
             q = got.shape[-1] // 2
             self.at = [pl.ds(0, q), pl.ds(q, q)]
             a, self.into_slot = in_slot(), in_slot()
-            n, self.out = out_slot(), out_slot()
+            n = ring_slot()
             for k in range(2):
                 copy(self.half(ki[3], k), relay.at[k], kdev[1 + k], n, a).start()
             for k in range(2):
                 copy(self.half(ki[1 + k], k), self.into(k, k), kdev[1 + k], n, self.into_slot).start()
             self.relayed = copy(relay, relay, kdev[1], n, a)
-            sent.append(copy(got, got, kdev[1], n, a))
+            ring.append((n, copy(got, got, kdev[1], n, a)))
 
         def half(self, target, n):
             return self.part(target, self.at[n])
@@ -367,16 +369,17 @@
 
         def step(self):
             self.relayed.wait_recv()
+            n = ring_slot()
             for k in range(2):
                 own = self.half(ki[2 - k], k)[...].astype(F32)
                 self.summed[k] = (own + self.relay[k].astype(F32)).astype(BF)
                 copy(
-                    self.summed.at[k], self.into(1 - k, k), kdev[2 - k], self.out, self.into_slot
+                    self.summed.at[k], self.into(1 - k, k), kdev[2 - k], n, self.into_slot
                 ).start()
-            sent.append(copy(self.summed, self.summed, kdev[1], self.out, self.into_slot))
+            ring.append((n, copy(self.summed, self.summed, kdev[1], n, self.into_slot)))
 
         def collect(self):
-            copy(self.got, self.got, kdev[1], self.out, self.into_slot).wait_recv()
+            copy(self.got, self.got, kdev[1], 0, self.into_slot).wait_recv()
 
         def total(self):
             out = self.part(i, pl.ds(0, self.got.shape[-1]))[...].astype(F32)
@@ -428,6 +431,17 @@
     l_xa = load(tok, x_all)
     l_ca = load(cot, c_all)
 
+    pl.semaphore_wait(barrier, 6 + len(seqdev))
+
+    here(l_qk)
+    t_qk = Fan(
+        [(qk_v.at[i, par], qk_v.at[i, par], kdev[d]) for d in DIRS], qk_v.at[pl.ds(0, 3), 0]
+    )
+    left = pl.ds(0, half)
+    t_v = Fan(
+        [(wv.at[vj[d], :, mine], v_v.at[j, :, mine], vdev[d]) for d in DIRS],
+        v_v.at[pl.ds(0, 3), :, left],
+    )
     dd_v[16:, :] = jnp.zeros((dd_v.shape[0] - 16, D), BF)
     here(l_small)
     head3 = lax.broadcasted_iota(jnp.int32, (16, W, 32), 1)
@@ -442,17 +456,6 @@
     sq_v[0:16, 0:64] = jnp.broadcast_to(ggn_v[...].astype(F32), (16, 64))
     gge_v[j] = sq_v[0:16].astype(BF)
 
-    pl.semaphore_wait(barrier, 6 + len(seqdev))
-
-    here(l_qk)
-    t_qk = Fan(
-        [(qk_v.at[i, par], qk_v.at[i, par], kdev[d]) for d in DIRS], qk_v.at[pl.ds(0, 3), 0]
-    )
-    left = pl.ds(0, half)
-    t_v = Fan(
-        [(wv.at[vj[d], :, mine], v_v.at[j, :, mine], vdev[d]) for d in DIRS],
-        v_v.at[pl.ds(0, 3), :, left],
-    )
     t_ext = Fan([(ext_v.at[i], ext_v.at[i], kdev[d]) for d in DIRS], ext_v.at[pl.ds(0, 3)])
     low = pl.ds(0, 32)
     high = pl.ds(32, 32)
@@ -738,26 +741,26 @@
     so[...] = (nn(hid, dn) + own_slab * resid).astype(BF).T.reshape(W, W, 64, T)
     t_out = LineSum(lambda to: so.at[:, to], ro.at[pl.ds(0, 2)], ro.at[pl.ds(2, 2)], co).rest()
     ffn_gain = jnp.sum(part * resid * r3, axis=0, keepdims=True)
+    settle(0, t_pre0)
+    t_fw0 = square(0, every)
     t_gg[0].step(0)
     t_m3.wait_recv()
     m3 = as_column(sst[...] + rst[1] + rst[2] + rst[3]) / D
     base = c_v[...].astype(F32) - resid * (r3 * r3 * r3 * m3)
-    settle(0, t_pre0)
-    t_fw0 = square(0, every)
+    t_gg[0].step(1)
     direct = nt(base.astype(BF), o_v[j].reshape(W * 64, D))
     full = p_v[...] * (g3 * r3)
     mixed_in = (full + own_run * base).astype(BF)
     for h in range(W):
         gow[h] = tn(ga_v[h], mixed_in).astype(BF)
     t_po = send(gow.at[:, :, other], preo, partner)
-    t_gg[0].step(1)
     t_gg[1].step(0)
+    t_fw0.step()
+    settle(1, t_pre1)
+    t_fw1 = [square(1, top)]
     t_gg[1].step(1)
     t_po.wait_recv()
     preso[...] = (gow[:, :, mine].astype(F32) + preo[...].astype(F32)).astype(BF)
-    t_fw0.step()
-    settle(1, t_pre1)
-    t_fw1 = [square(1, top)]
     for line in t_gg:
         line.collect()
 
@@ -788,78 +791,46 @@
     t_fw1.append(square(1, bottom))
     vz[1] = dgate.T.reshape(W, 64, T)
     t_gz = Fan([(vz.at[1, vj[d]], zvg.at[1, j], vdev[d]) for d in DIRS], zvg.at[1, pl.ds(0, 3)])
-    dq_in, dk_in, dv_in = [], [], []
+    dq_all, dk_in, dv_in = [], [], []
     for c in range(nblk):
         ds = jnp.where(causal, nt(gmix[blk[c]], v[blk[c]]), 0.0).astype(BF)
-        dq_in.append(nn(ds, kd[c]) + em[c] * nn(gmix[blk[c]], start_low[c]))
+        dq_all.append(e1[c] * (nn(ds, kd[c]) + em[c] * nn(gmix[blk[c]], start_low[c])))
         dk_in.append(tn(ds, qd[c]))
         dv_in.append(tn(score[c], gmix[blk[c]]))
+    ql = jnp.concatenate([(dq * scale).astype(BF) for dq in dq_all], axis=0)
+    known = nn(dgate, wg_all) + nn(ql, wq_all)
+    rest_in = full + own_slab * base
     t_out.step(0)
     t_hd.wait_recv()
     dsum[0] = nn(lanes(hseg[...]), c_all[...]).astype(BF)
     t_ds = send(dsum.at[0], dsum.at[1], partner)
+    t_fw1[0].step()
     t_bst.wait_recv()
     after = [None] * nblk
     states = gather_states(bst_v, btt_v, True)
+    t_out.step(1)
     after[nblk - 1] = entering(btt_v, True, *states)
     for c in range(nblk - 2, -1, -1):
         after[c] = after[c + 1] * dec[c + 1] + qst[c + 1]
-    t_out.step(1)
-    t_fw1[0].step()
-
-    ql, kl, vl, ga = [], [], [], []
+
+    kl, vl, ga = [], [], []
     for c in range(nblk):
         low_after = after[c].astype(BF)
-        dq = e1[c] * dq_in[c]
         dk = e2[c] * (dk_in[c] + el[c] * nn(v[blk[c]], low_after))
         dv = dv_in[c] + nt(ke[c], low_after)
-        gc = q[blk[c]] * dq - k[blk[c]] * dk
+        gc = q[blk[c]] * dq_all[c] - k[blk[c]] * dk
         extra = jnp.sum(after[c] * start[c + 1], axis=0, keepdims=True)
         gc = jnp.where(row_id == CB - 1, gc + extra, gc)
         gr = tn(tri, gc, HIGH)
         ga.append(gr / (1.0 + jnp.exp(arg[blk[c]])) / 16.0)
-        ql.append((dq * scale).astype(BF))
         kl.append(dk.astype(BF))
         vl.append(dv.astype(BF))
-    ql = jnp.concatenate(ql, axis=0)
     kl = jnp.concatenate(kl, axis=0)
     vl = jnp.concatenate(vl, axis=0)
     ga = jnp.concatenate(ga, axis=0).astype(BF)
-    vz[0] = vl.T.reshape(W, 64, T)
-    qka[:, 0] = ql.T.reshape(W, 32, T)
-    qka[:, 1] = kl.T.reshape(W, 32, T)
-    qka[:, 2] = ga.T.reshape(W, 32, T)
-    t_qa = Fan([(qka.at[ki[d]], kqa.at[i], kdev[d]) for d in DIRS], kqa.at[pl.ds(0, 3)])
     glr = nn(ga, ext_all).astype(BF)
-    gn = nn(ql, wq_all) + nn(kl, wk_all) + nn(vl, wv_all) + nn(dgate, wg_all) + nn(glr, dd_v[...])
-    x = x_v[...].astype(F32)
-    gnx = gn * x
-    norm_gain = jnp.sum(gnx * r1, axis=0, keepdims=True)
-    m1p = as_row(jnp.sum(gnx * g1, axis=1, keepdims=True))[:1]
-    rank_row = lax.broadcasted_iota(jnp.int32, (16, 128), 0)
-    rank_col = lax.broadcasted_iota(jnp.int32, (16, 128), 1)
-    by_owner = jnp.where(rank_col == lax.rem(rank_row, W) * W + rank_row // W, 1.0, 0.0)
-    small = nn(by_owner.astype(BF), tn(glr, normed).astype(BF))
-    slab = D // (W * W)
-    rid = lax.broadcasted_iota(jnp.int32, (16, T), 0)
-    for h in range(W):
-        ranks = small[h * W : (h + 1) * W]
-        sm0[h, 0:16] = jnp.concatenate(
-            [ranks[:, n * T : (n + 1) * T] for n in range(W)], axis=0
-        ).astype(BF)
-
-        def slabs(row):
-            return jnp.concatenate(
-                [row[:, (W * n + h) * slab : (W * n + h + 1) * slab] for n in range(W)], axis=1
-            )
-
-        rest = jnp.where(rid == 0, slabs(norm_gain), 0.0)
-        rest = jnp.where(rid == 1, slabs(ffn_gain), rest)
-        rest = jnp.where(rid == 2, group_rows[h], rest)
-        rest = jnp.where(rid == 3, m1p, rest)
-        sm0[h, 16:32] = rest.astype(BF)
-    t_s0 = Fan([(sm0.at[vj[d]], sm1.at[d], vdev[d]) for d in DIRS], sm1.at[pl.ds(1, 3)])
-    whole = gn * (r1 * g1) + full + own_slab * base
+    gn = known + nn(kl, wk_all) + nn(vl, wv_all) + nn(glr, dd_v[...])
+    whole = gn * (r1 * g1) + rest_in
     sgn[...] = whole.astype(BF).T.reshape(W, W, 64, T)
     pairs = [pl.ds(n * W // 2, W // 2) for n in range(2)]
     t_gn = [
@@ -874,13 +845,36 @@
     for n in range(3):
         for line in t_gn:
             line.go(n)
+    vz[0] = vl.T.reshape(W, 64, T)
     t_vz = Fan([(vz.at[0, vj[d]], zvg.at[0, j], vdev[d]) for d in DIRS], zvg.at[0, pl.ds(0, 3)])
 
-
-    t_gz.wait_recv()
-    zvg[1, j] = vz[1, j]
-    t_gk = Fan([(zvg.at[1, ki[d]], kvg.at[1, i], kdev[d]) for d in DIRS], kvg.at[1, pl.ds(0, 3)])
-    kvg[1, i] = zvg[1, i]
+    gnx = gn * x_v[...].astype(F32)
+    norm_gain = jnp.sum(gnx * r1, axis=0, keepdims=True)
+    m1p = as_row(jnp.sum(gnx * g1, axis=1, keepdims=True))[:1]
+    rank_row = lax.broadcasted_iota(jnp.int32, (16, 128), 0)
+    rank_col = lax.broadcasted_iota(jnp.int32, (16, 128), 1)
+    by_owner = jnp.where(rank_col == lax.rem(rank_row, W) * W + rank_row // W, 1.0, 0.0)
+    small = nn(by_owner.astype(BF), tn(glr, normed).astype(BF))
+    slab = D // (W * W)
+    rid = lax.broadcasted_iota(jnp.int32, (16, T), 0)
+    for h in range(W):
+        ranks = small[h * W : (h + 1) * W]
+        sm0[h, 0:16] = jnp.concatenate(
+            [ranks[:, n * T : (n + 1) * T] for n in range(W)], axis=0
+        ).astype(BF)
+
+        def slabs(row):
+            return jnp.concatenate(
+                [row[:, (W * n + h) * slab : (W * n + h + 1) * slab] for n in range(W)], axis=1
+            )
+
+        rest = jnp.where(rid == 0, slabs(norm_gain), 0.0)
+        rest = jnp.where(rid == 1, slabs(ffn_gain), rest)
+        rest = jnp.where(rid == 2, group_rows[h], rest)
+        rest = jnp.where(rid == 3, m1p, rest)
+        sm0[h, 16:32] = rest.astype(BF)
+    t_s0 = Fan([(sm0.at[vj[d]], sm1.at[d], vdev[d]) for d in DIRS], sm1.at[pl.ds(1, 3)])
+
 
     def finish_square(n, lines):
         for line, rows_at in lines:
@@ -891,7 +885,45 @@
     t_ff = [finish_square(0, [(t_fw0, every)])]
     t_ow.step()
     t_fw1[1].step()
-
+    qka[:, 0] = ql.T.reshape(W, 32, T)
+    qka[:, 1] = kl.T.reshape(W, 32, T)
+    qka[:, 2] = ga.T.reshape(W, 32, T)
+    t_qa = Fan([(qka.at[ki[d]], kqa.at[i], kdev[d]) for d in DIRS], kqa.at[pl.ds(0, 3)])
+    t_gz.wait_recv()
+    zvg[1, j] = vz[1, j]
+    t_gk = Fan([(zvg.at[1, ki[d]], kvg.at[1, i], kdev[d]) for d in DIRS], kvg.at[1, pl.ds(0, 3)])
+    kvg[1, i] = zvg[1, i]
+
+    t_out.collect()
+    ao[...] = t_out.total().astype(BF)
+    t_ao = Fan([(ao.at[ki[d]], oseg.at[i], kdev[d]) for d in DIRS], oseg.at[pl.ds(0, 3)])
+    oseg[i] = ao[i]
+
+    t_gn[0].step(0)
+    t_gn[1].step(0)
+    t_gn[0].step(1)
+    t_gn[1].step(1)
+
+    t_ow.collect()
+    mid_o[...] = t_ow.total().astype(BF).reshape(W, 64, half)
+    t_oz = LineSum(
+        lambda to: mid_o.at[to], rowz.at[pl.ds(0, 2)], rowz.at[pl.ds(2, 2)], coz
+    ).rest()
+
+    t_qa.wait_recv()
+    kqa[i] = qka[i]
+    nall = n_all[...]
+    for n in range(2):
+        qksum[0, n] = nn(lanes(kqa[:, n]), nall).astype(BF)
+    esum[0] = nn(lanes(kqa[:, 2]), lall_v[...])
+    t_qs = send(qksum.at[0], qksum.at[1], partner)
+    t_es = send(esum.at[0], esum.at[1], partner)
+    for line in t_gn:
+        line.collect()
+    t_vz.wait_recv()
+    zvg[0, j] = vz[0, j]
+    t_vk = Fan([(zvg.at[0, ki[d]], kvg.at[0, i], kdev[d]) for d in DIRS], kvg.at[0, pl.ds(0, 3)])
+    kvg[0, i] = zvg[0, i]
     t_s0.wait_recv()
     sm2[0] = total(sm0[j], sm1).astype(BF)
     m1 = (
@@ -900,40 +932,7 @@
         + sm1[2, 19:20].astype(F32)
         + sm1[3, 19:20].astype(F32)
     ) / D
-    t_s1 = Fan([(sm2.at[0], sm2.at[d], kdev[d]) for d in DIRS], sm2.at[pl.ds(1, 3)])
-
-    t_out.collect()
-    ao[...] = t_out.total().astype(BF)
-    t_ao = Fan([(ao.at[ki[d]], oseg.at[i], kdev[d]) for d in DIRS], oseg.at[pl.ds(0, 3)])
-    oseg[i] = ao[i]
-
-    t_gn[0].step(0)
-    t_gn[1].step(0)
-    t_gn[0].step(1)
-    t_gn[1].step(1)
-
-    t_ow.collect()
-    mid_o[...] = t_ow.total().astype(BF).reshape(W, 64, half)
-    t_oz = LineSum(
-        lambda to: mid_o.at[to], rowz.at[pl.ds(0, 2)], rowz.at[pl.ds(2, 2)], coz
-    ).rest()
-
-    t_qa.wait_recv()
-    kqa[i] = qka[i]
-    nall = n_all[...]
-    for n in range(2):
-        qksum[0, n] = nn(lanes(kqa[:, n]), nall).astype(BF)
-    esum[0] = nn(lanes(kqa[:, 2]), lall_v[...])
-    t_qs = send(qksum.at[0], qksum.at[1], partner)
-    t_es = send(esum.at[0], esum.at[1], partner)
-    t_ff.append(finish_square(1, list(zip(t_fw1, (top, bottom)))))
-
-    t_gk.wait_recv()
-    vgsum[0, 1] = nn(lanes(kvg[1]), nall).astype(BF)
-    t_vs = [send(vgsum.at[0, 1], vgsum.at[1, 1], partner)]
-
-    for line in t_gn:
-        line.collect()
+
     summed = jnp.concatenate([line.total() for line in t_gn], axis=0)
     for h in range(W):
         at = pl.ds(pl.multiple_of((h * W + j) * 64, 64), 64)
@@ -941,19 +940,22 @@
     t_ai = Fan([(ai.at[ki[d]], iseg.at[i], kdev[d]) for d in DIRS], iseg.at[pl.ds(0, 3)])
     iseg[i] = ai[i]
 
-    t_vz.wait_recv()
-    zvg[0, j] = vz[0, j]
-    t_vk = Fan([(zvg.at[0, ki[d]], kvg.at[0, i], kdev[d]) for d in DIRS], kvg.at[0, pl.ds(0, 3)])
-    kvg[0, i] = zvg[0, i]
-
+    t_s1 = Fan([(sm2.at[0], sm2.at[d], kdev[d]) for d in DIRS], sm2.at[pl.ds(1, 3)])
+    t_ff.append(finish_square(1, list(zip(t_fw1, (top, bottom)))))
+
+    t_gk.wait_recv()
+    vgsum[0, 1] = nn(lanes(kvg[1]), nall).astype(BF)
+    t_vs = [send(vgsum.at[0, 1], vgsum.at[1, 1], partner)]
+
+    t_oz.step(0)
+    t_oz.step(1)
+
+    t_vk.wait_recv()
+    vgsum[0, 0] = nn(lanes(kvg[0]), nall).astype(BF)
+    t_vs.append(send(vgsum.at[0, 0], vgsum.at[1, 0], partner))
     t_s1.wait_recv()
     sm3[0] = total(sm2[0], sm2).astype(BF)
     t_s2 = send(sm3.at[0], sm3.at[1], partner)
-    t_oz.step(0)
-    t_oz.step(1)
-    t_vk.wait_recv()
-    vgsum[0, 0] = nn(lanes(kvg[0]), nall).astype(BF)
-    t_vs.append(send(vgsum.at[0, 0], vgsum.at[1, 0], partner))
 
     t_ds.wait_recv()
     r_fd[...] = dsum[0].astype(F32) + dsum[1].astype(F32)
@@ -996,7 +998,7 @@
     t_fo.wait_recv()
     for h in range(2):
         r_o[:, h * half : (h + 1) * half] = fin_ow[h].astype(F32)
-    for cp in sent + [cp for _, cp in ring]:
+    for _, cp in ring:
         cp.wait_send()
 
     @pl.when(inner)
@@ -1010,7 +1012,7 @@
             cp.wait_send()
 
 
-N_OUT = 62
+N_OUT = 44
 N_IN = 93
 N_LOCAL = 18
 

time: 87.8 us -> 86.8 us (0.989)
  no operation moved by 1% of the time
where the time goes in v7:
time: 86.8 us; the launch traced here: 86.7 us
  Pallas kernels  85.9 us (99%)
    pallas_call x1, Pallas kernels, layer(): pl.pallas_call(functools.partial(layer_kernel, n_seq), out_shape=outs, in...  83.9 us
    pallas_call x1, Pallas kernels, finish(): pl.pallas_call(finish_kernel, out_shape=[jax.ShapeDtypeStruct(p.shape, p....  1.95 us

profile of v7, /device:TPU:0, one launch (start us, length us, event | category | flops | bytes accessed | tf_op | source)
XLA Modules:
  0.0 86.7 jit_solution(789478994125179254)
XLA Ops:
  0.7 83.9 %layer.1 = (bf16[64,1024]{1,0:T(8,128)(2,1)S(1)}, bf16[64,1024]{1,0:T(8,128)(2,1)S(1)}, f32[1,64]{1,0:T(1,128)S(1)}, f32[32,1024]{1,0:T(8,128)S(1)}, f32[32,1024...) custom-call(bf16[1024,1024]{1,0:T(8,128)(2,1)} %tok.1, ...), custom_call_target="tpu_custom_call" | custom-call | tf_op jit(solution)/shard_map/layer/pallas_call | solution.py:1136
  84.6 1.9 %finish.1 = (bf16[64,1024]{1,0:T(8,128)(2,1)}, bf16[64,1024]{1,0:T(8,128)(2,1)}, f32[1,64]{1,0:T(1,128)}, f32[32,1024]{1,0:T(8,128)}, f32[32,1024]{1,0:T(8,128)}...) custom-call(bf16[64,1024]{1,0:T(8,128)(2,1)S(1)} %get-tuple-element., ...), custom_call_target="tpu_custom_call" | custom-call | tf_op jit(solution)/shard_map/finish/pallas_call | solution.py:1160

commit v8 on v7

--- a/solution.py
+++ b/solution.py
@@ -567,21 +567,21 @@
 
     def gather_states(slots, totals, back):
         order = range(W - 1, -1, -1) if back else range(W)
-        pre_s = jnp.zeros((VC, 128), F32)
-        pre_d = jnp.ones((1, 128), F32)
-        tot_s = jnp.zeros((VC, 128), F32)
-        tot_d = jnp.ones((1, 128), F32)
+        tot_s, tot_d = jnp.zeros((VC, 128), F32), jnp.ones((1, 128), F32)
         for other_i in order:
-            one_s = slots[other_i, :VC].astype(F32)
             one_d = slots[other_i, VC : VC + 1].astype(F32)
-            use = (other_i > i) if back else (other_i < i)
-            pre_s = jnp.where(use, pre_s * one_d + one_s, pre_s)
-            pre_d = jnp.where(use, pre_d * one_d, pre_d)
-            tot_s = tot_s * one_d + one_s
+            tot_s = tot_s * one_d + slots[other_i, :VC].astype(F32)
             tot_d = tot_d * one_d
         totals[s, :VC] = tot_s.astype(BF)
         totals[s, VC:] = jnp.broadcast_to(tot_d, (16, 128)).astype(BF)
-        return pre_s, pre_d, [send(totals.at[s], totals.at[s], dev) for dev in seqdev]
+        moves = [send(totals.at[s], totals.at[s], dev) for dev in seqdev]
+        pre_s, pre_d = jnp.zeros((VC, 128), F32), jnp.ones((1, 128), F32)
+        for other_i in order[:-1]:
+            one_d = slots[other_i, VC : VC + 1].astype(F32)
+            use = (other_i > i) if back else (other_i < i)
+            pre_s = jnp.where(use, pre_s * one_d + slots[other_i, :VC].astype(F32), pre_s)
+            pre_d = jnp.where(use, pre_d * one_d, pre_d)
+        return pre_s, pre_d, moves
 
     def entering(totals, back, pre_s, pre_d, moves):
         arrived(moves)

time: 86.8 us -> 87 us (level)
  no operation moved by 1% of the time
where the time goes in v8:
time: 87 us; the launch traced here: 86.8 us
  Pallas kernels  86 us (99%)
    pallas_call x1, Pallas kernels, layer(): pl.pallas_call(functools.partial(layer_kernel, n_seq), out_shape=outs, in...  84 us
    pallas_call x1, Pallas kernels, finish(): pl.pallas_call(finish_kernel, out_shape=[jax.ShapeDtypeStruct(p.shape, p....  1.95 us

profile of v8, /device:TPU:0, one launch (start us, length us, event | category | flops | bytes accessed | tf_op | source)
XLA Modules:
  0.0 86.8 jit_solution(118121729975167572)
XLA Ops:
  0.7 84.0 %layer.1 = (bf16[64,1024]{1,0:T(8,128)(2,1)S(1)}, bf16[64,1024]{1,0:T(8,128)(2,1)S(1)}, f32[1,64]{1,0:T(1,128)S(1)}, f32[32,1024]{1,0:T(8,128)S(1)}, f32[32,1024...) custom-call(bf16[1024,1024]{1,0:T(8,128)(2,1)} %tok.1, ...), custom_call_target="tpu_custom_call" | custom-call | tf_op jit(solution)/shard_map/layer/pallas_call | solution.py:1136
  84.7 1.9 %finish.1 = (bf16[64,1024]{1,0:T(8,128)(2,1)}, bf16[64,1024]{1,0:T(8,128)(2,1)}, f32[1,64]{1,0:T(1,128)}, f32[32,1024]{1,0:T(8,128)}, f32[32,1024]{1,0:T(8,128)}...) custom-call(bf16[64,1024]{1,0:T(8,128)(2,1)S(1)} %get-tuple-element., ...), custom_call_target="tpu_custom_call" | custom-call | tf_op jit(solution)/shard_map/finish/pallas_call | solution.py:1160

commit v9 on v7

--- a/solution.py
+++ b/solution.py
@@ -932,6 +932,7 @@
         + sm1[2, 19:20].astype(F32)
         + sm1[3, 19:20].astype(F32)
     ) / D
+    t_s1 = Fan([(sm2.at[0], sm2.at[d], kdev[d]) for d in DIRS], sm2.at[pl.ds(1, 3)])
 
     summed = jnp.concatenate([line.total() for line in t_gn], axis=0)
     for h in range(W):
@@ -940,7 +941,6 @@
     t_ai = Fan([(ai.at[ki[d]], iseg.at[i], kdev[d]) for d in DIRS], iseg.at[pl.ds(0, 3)])
     iseg[i] = ai[i]
 
-    t_s1 = Fan([(sm2.at[0], sm2.at[d], kdev[d]) for d in DIRS], sm2.at[pl.ds(1, 3)])
     t_ff.append(finish_square(1, list(zip(t_fw1, (top, bottom)))))
 
     t_gk.wait_recv()

time: 86.8 us -> 86.5 us (level)
  no operation moved by 1% of the time
where the time goes in v9:
time: 86.5 us; the launch traced here: 86.3 us
  Pallas kernels  85.5 us (99%)
    pallas_call x1, Pallas kernels, layer(): pl.pallas_call(functools.partial(layer_kernel, n_seq), out_shape=outs, in...  83.5 us
    pallas_call x1, Pallas kernels, finish(): pl.pallas_call(finish_kernel, out_shape=[jax.ShapeDtypeStruct(p.shape, p....  1.95 us

profile of v9, /device:TPU:0, one launch (start us, length us, event | category | flops | bytes accessed | tf_op | source)
XLA Modules:
  0.0 86.3 jit_solution(12502910893833516828)
XLA Ops:
  0.7 83.5 %layer.1 = (bf16[64,1024]{1,0:T(8,128)(2,1)S(1)}, bf16[64,1024]{1,0:T(8,128)(2,1)S(1)}, f32[1,64]{1,0:T(1,128)S(1)}, f32[32,1024]{1,0:T(8,128)S(1)}, f32[32,1024...) custom-call(bf16[1024,1024]{1,0:T(8,128)(2,1)} %tok.1, ...), custom_call_target="tpu_custom_call" | custom-call | tf_op jit(solution)/shard_map/layer/pallas_call | solution.py:1136
  84.2 1.9 %finish.1 = (bf16[64,1024]{1,0:T(8,128)(2,1)}, bf16[64,1024]{1,0:T(8,128)(2,1)}, f32[1,64]{1,0:T(1,128)}, f32[32,1024]{1,0:T(8,128)}, f32[32,1024]{1,0:T(8,128)}...) custom-call(bf16[64,1024]{1,0:T(8,128)(2,1)S(1)} %get-tuple-element., ...), custom_call_target="tpu_custom_call" | custom-call | tf_op jit(solution)/shard_map/finish/pallas_call | solution.py:1160
